TPU v7x, 1024 devices: a whole 8x8x8 slice. The times are simulated.
1024 devices in a mesh: tm: 8 (over z), gy: 16 (over x_hi, y), gz: 8 (over x_lo, core).
Axes of the slice: x: 8 (x_hi: 2, x_lo: 4; x = x_hi * 4 + x_lo), y: 8, z: 8, core: 2. Of those that a mesh axis runs over, the one named last changes fastest.
Arguments:
- iterate: float32 [8, 2, 4, 1024, 1024], P('tm', None, None, 'gy', 'gz'), may hold values from 0 to 1, as said below
- rates: float32 [2, 4, 1024, 1024], P(None, None, 'gy', 'gz'), may hold values from 0.02 to 0.3
Outputs:
- end_states: float32 [8, 2, 4, 1024, 1024], P('tm', None, None, 'gy', 'gz')
Inputs may be any that keep to these rules, and one draw needn't show every extreme that they name: `iterate`: species 0 lies within 0.4 to 1 and species 1 within 0 to 0.5.
All inputs are finite; a program needn't handle non-finite values.
Results may differ from a plain program's by a relative error of at most 0.00002.
Values sent between devices are 32-bit elements; how exact they have to be, the bound alone decides.
No kernel may reach another device: no remote copies, remote signals or barrier semaphores. Data moves between devices by JAX's collectives and lax.ppermute only.
A program may use at most 32 MiB of HBM per device.

v0:
```python
import jax
import jax.numpy as jnp
from jax import lax
from jax.sharding import PartitionSpec as P

ITERS = 2
FINE = 4


spread_fast = 0.2
spread_slow = 0.1
fine_step = 0.125
coarse_step = 0.5


def padded_2(block, sides, width):
    for axis, dim in sides:
        count = lax.axis_size(axis)
        forward = [(i, i + 1) for i in range(count - 1)]
        forward.append((count - 1, 0))
        backward = [(target, source) for source, target in forward]
        low = lax.ppermute(
            lax.slice_in_dim(block, block.shape[dim] - width, None, axis=dim), axis, forward
        )
        high = lax.ppermute(lax.slice_in_dim(block, 0, width, axis=dim), axis, backward)
        block = jnp.concatenate([low, block, high], axis=dim)
    return block


def from_behind(block, axis, distance):
    devices = range(lax.axis_size(axis))
    route = [(i - distance, i) for i in devices if i - distance in devices]
    return lax.ppermute(block, axis, route)


def react(state, spread, rates, length):
    substrate = state[0]
    catalyst = state[1]
    feed = rates[0]
    kill = rates[1]
    product = substrate * catalyst * catalyst
    change_a = spread_fast * spread[0] - product + feed * (1.0 - substrate)
    change_b = spread_slow * spread[1] + product - (feed + kill) * catalyst
    return jnp.stack([substrate + length * change_a, catalyst + length * change_b])


def step_on(extended, rates_here, length):
    centre = extended[:, :, 1:-1, 1:-1]
    walled = jnp.pad(centre, ((0, 0), (1, 1), (0, 0), (0, 0)), mode="edge")
    along_x = walled[:, :-2] + walled[:, 2:]
    along_y = extended[:, :, :-2, 1:-1] + extended[:, :, 2:, 1:-1]
    along_z = extended[:, :, 1:-1, :-2] + extended[:, :, 1:-1, 2:]
    spread = along_x + along_y + along_z - 6.0 * centre
    return react(centre, spread, rates_here, length)


def per_device(iterate, rates):
    own_start = iterate[0]
    position = lax.axis_index("tm")
    leading = position == 0
    slices = lax.axis_size("tm")
    end_state = own_start
    for iteration in range(ITERS):
        state = own_start
        coarse_old = own_start
        for substep in range(FINE):
            padded = padded_2(state, (("gy", 2), ("gz", 3)), 1)
            if substep == 0:
                coarse_old = step_on(padded, rates, coarse_step)
            state = step_on(padded, rates, fine_step)
        difference = state - coarse_old
        end_state = coarse_old + difference

        def turn(turn_index, carried):
            start, previous = carried
            received = from_behind(previous, "tm", 1)
            start = jnp.where(leading, own_start, received)
            extended = padded_2(start, (("gy", 2), ("gz", 3)), 1)
            updated = step_on(extended, rates, coarse_step) + difference
            return (start, updated)

        start, end_state = lax.fori_loop(0, slices - 1, turn, (own_start, end_state))
        own_start = start
    return end_state[None]


def solution(mesh):
    return jax.shard_map(
        per_device,
        mesh=mesh,
        in_specs=(P("tm", None, None, "gy", "gz"), P(None, None, "gy", "gz")),
        out_specs=P("tm", None, None, "gy", "gz"),
        check_vma=False,
    )
```

profile of v0, /device:TPU:14, one launch (start us, length us, event | category | flops | bytes accessed | tf_op | source)
XLA Modules:
  0.0 712.6 jit_solution(15951657151254930963)
XLA Ops:
  0.8 8.7 %collective-permute-start.11 = (f32[2,4,1,128]{3,2,1,0:T(1,128)S(1)}, f32[2,4,1,128]{3,2,1,0:T(1,128)S(1)}, u32[]{:S(2)}, u32[]{:S(2)}) collective-permute-start(f32[2,4,1,128]{3,2,1,0:T(1,128)S(1)} %get-tuple-element.261), channel_id=1, source_target_pairs={{8,0},{16,8},{24,16},{32,24},{40,32},{48,40},{56,48},{64,56},{72,6... | collective-permute-start | bytes 12296 | tf_op jit(solution)/shard_map/ppermute | solution.py:25
  11.5 9.6 %collective-permute-done.10 = f32[2,4,1,128]{3,2,1,0:T(1,128)S(1)} collective-permute-done((f32[2,4,1,128]{3,2,1,0:T(1,128)S(1)}, f32[2,4,1,128]{3,2,1,0:T(1,128)S(1)}, u32[]{:S(2)}, u32[]{:S(2)}) %collective-permute-start.10) | collective-permute-done | bytes 4128 | tf_op jit(solution)/shard_map/ppermute | solution.py:22
  40.7 7.6 %collective-permute-done.14 = f32[2,4,1,128]{3,2,1,0:T(1,128)S(1)} collective-permute-done((f32[2,4,1,128]{3,2,1,0:T(1,128)S(1)}, f32[2,4,1,128]{3,2,1,0:T(1,128)S(1)}, u32[]{:S(2)}, u32[]{:S(2)}) %collective-permute-start.14) | collective-permute-done | bytes 4128 | tf_op jit(solution)/shard_map/ppermute | solution.py:22
  67.2 6.9 collective-permute-done.18
  80.4 5.6 collective-permute-done.20
  92.4 7.5 %collective-permute-done.22 = f32[2,4,1,128]{3,2,1,0:T(1,128)S(1)} collective-permute-done((f32[2,4,1,128]{3,2,1,0:T(1,128)S(1)}, f32[2,4,1,128]{3,2,1,0:T(1,128)S(1)}, u32[]{:S(2)}, u32[]{:S(2)}) %collective-permute-start.22) | collective-permute-done | bytes 4128 | tf_op jit(solution)/shard_map/ppermute | solution.py:22
  106.2 5.6 collective-permute-done.24
  112.3 247.2 %while.24 = (s32[]{:T(128)}, f32[2,4,64,128]{3,2,1,0:T(8,128)}, f32[2,4,64,128]{3,2,1,0:T(8,128)S(1)}, pred[]{:T(512)}, f32[2,4,64,128]{3,2,1,0:T(8,128)S(1)}, /...) while((s32[]{:T(128)}, f32[2,4,64,128]{3,2,1,0:T(8,128)}, ...), condition=%wide.region_1.2_spmd, body=%wide.region_0.1_spmd.sunk | while | flops 1937410 | bytes 6264002 | solution.py:82
  127.3 7.6 %collective-permute-done.2 = f32[2,4,1,128]{3,2,1,0:T(1,128)S(1)} collective-permute-done((f32[2,4,1,128]{3,2,1,0:T(1,128)S(1)}, f32[2,4,1,128]{3,2,1,0:T(1,128)S(1)}, u32[]{:S(2)}, u32[]{:S(2)}) %collective-permute-start.2) | collective-permute-done | bytes 4128 | tf_op jit(solution)/shard_map/while/body/eval_jaxpr/ppermute | solution.py:22
  141.2 5.6 collective-permute-done.4
  162.2 7.6 %collective-permute-done.2 = f32[2,4,1,128]{3,2,1,0:T(1,128)S(1)} collective-permute-done((f32[2,4,1,128]{3,2,1,0:T(1,128)S(1)}, f32[2,4,1,128]{3,2,1,0:T(1,128)S(1)}, u32[]{:S(2)}, u32[]{:S(2)}) %collective-permute-start.2) | collective-permute-done | bytes 4128 | tf_op jit(solution)/shard_map/while/body/eval_jaxpr/ppermute | solution.py:22
  176.2 5.6 collective-permute-done.4
  197.2 7.6 %collective-permute-done.2 = f32[2,4,1,128]{3,2,1,0:T(1,128)S(1)} collective-permute-done((f32[2,4,1,128]{3,2,1,0:T(1,128)S(1)}, f32[2,4,1,128]{3,2,1,0:T(1,128)S(1)}, u32[]{:S(2)}, u32[]{:S(2)}) %collective-permute-start.2) | collective-permute-done | bytes 4128 | tf_op jit(solution)/shard_map/while/body/eval_jaxpr/ppermute | solution.py:22
  211.1 5.6 collective-permute-done.4
  217.2 6.4 collective-permute-start
  233.4 7.6 %collective-permute-done.2 = f32[2,4,1,128]{3,2,1,0:T(1,128)S(1)} collective-permute-done((f32[2,4,1,128]{3,2,1,0:T(1,128)S(1)}, f32[2,4,1,128]{3,2,1,0:T(1,128)S(1)}, u32[]{:S(2)}, u32[]{:S(2)}) %collective-permute-start.2) | collective-permute-done | bytes 4128 | tf_op jit(solution)/shard_map/while/body/eval_jaxpr/ppermute | solution.py:22
  247.3 5.6 collective-permute-done.4
  268.8 7.6 %collective-permute-done.2 = f32[2,4,1,128]{3,2,1,0:T(1,128)S(1)} collective-permute-done((f32[2,4,1,128]{3,2,1,0:T(1,128)S(1)}, f32[2,4,1,128]{3,2,1,0:T(1,128)S(1)}, u32[]{:S(2)}, u32[]{:S(2)}) %collective-permute-start.2) | collective-permute-done | bytes 4128 | tf_op jit(solution)/shard_map/while/body/eval_jaxpr/ppermute | solution.py:22
  282.7 5.6 collective-permute-done.4
  304.2 7.6 %collective-permute-done.2 = f32[2,4,1,128]{3,2,1,0:T(1,128)S(1)} collective-permute-done((f32[2,4,1,128]{3,2,1,0:T(1,128)S(1)}, f32[2,4,1,128]{3,2,1,0:T(1,128)S(1)}, u32[]{:S(2)}, u32[]{:S(2)}) %collective-permute-start.2) | collective-permute-done | bytes 4128 | tf_op jit(solution)/shard_map/while/body/eval_jaxpr/ppermute | solution.py:22
  318.1 5.6 collective-permute-done.4
  339.5 7.6 %collective-permute-done.2 = f32[2,4,1,128]{3,2,1,0:T(1,128)S(1)} collective-permute-done((f32[2,4,1,128]{3,2,1,0:T(1,128)S(1)}, f32[2,4,1,128]{3,2,1,0:T(1,128)S(1)}, u32[]{:S(2)}, u32[]{:S(2)}) %collective-permute-start.2) | collective-permute-done | bytes 4128 | tf_op jit(solution)/shard_map/while/body/eval_jaxpr/ppermute | solution.py:22
  353.4 5.6 collective-permute-done.4
  366.1 7.6 %collective-permute-done.26 = f32[2,4,1,128]{3,2,1,0:T(1,128)S(1)} collective-permute-done((f32[2,4,1,128]{3,2,1,0:T(1,128)S(1)}, f32[2,4,1,128]{3,2,1,0:T(1,128)S(1)}, u32[]{:S(2)}, u32[]{:S(2)}) %collective-permute-start.26) | collective-permute-done | bytes 4128 | tf_op jit(solution)/shard_map/ppermute | solution.py:22
  381.0 5.6 collective-permute-done.28
  392.9 7.6 %collective-permute-done.30 = f32[2,4,1,128]{3,2,1,0:T(1,128)S(1)} collective-permute-done((f32[2,4,1,128]{3,2,1,0:T(1,128)S(1)}, f32[2,4,1,128]{3,2,1,0:T(1,128)S(1)}, u32[]{:S(2)}, u32[]{:S(2)}) %collective-permute-start.30) | collective-permute-done | bytes 4128 | tf_op jit(solution)/shard_map/ppermute | solution.py:22
  406.8 5.6 collective-permute-done.32
  418.7 7.6 %collective-permute-done.34 = f32[2,4,1,128]{3,2,1,0:T(1,128)S(1)} collective-permute-done((f32[2,4,1,128]{3,2,1,0:T(1,128)S(1)}, f32[2,4,1,128]{3,2,1,0:T(1,128)S(1)}, u32[]{:S(2)}, u32[]{:S(2)}) %collective-permute-start.34) | collective-permute-done | bytes 4128 | tf_op jit(solution)/shard_map/ppermute | solution.py:22
  432.6 5.6 collective-permute-done.36
  444.5 7.6 %collective-permute-done.38 = f32[2,4,1,128]{3,2,1,0:T(1,128)S(1)} collective-permute-done((f32[2,4,1,128]{3,2,1,0:T(1,128)S(1)}, f32[2,4,1,128]{3,2,1,0:T(1,128)S(1)}, u32[]{:S(2)}, u32[]{:S(2)}) %collective-permute-start.38) | collective-permute-done | bytes 4128 | tf_op jit(solution)/shard_map/ppermute | solution.py:22
  458.4 5.6 collective-permute-done.40
  464.4 247.5 %while.25 = (s32[]{:T(128)}, f32[2,4,64,128]{3,2,1,0:T(8,128)S(1)}, pred[]{:T(512)}, f32[2,4,64,128]{3,2,1,0:T(8,128)S(1)}, f32[2,4,64,128]{3,2,1,0:T(8,128)S(1)...) while((s32[]{:T(128)}, f32[2,4,64,128]{3,2,1,0:T(8,128)S(1)}, pred[]{:T(512)}, ...), condition=%wide.region_3.4_spmd, body=%wide.region_2.3_spmd.sunk | while | flops 1937410 | bytes 5215390 | solution.py:82
  479.8 7.6 %collective-permute-done.7 = f32[2,4,1,128]{3,2,1,0:T(1,128)S(1)} collective-permute-done((f32[2,4,1,128]{3,2,1,0:T(1,128)S(1)}, f32[2,4,1,128]{3,2,1,0:T(1,128)S(1)}, u32[]{:S(2)}, u32[]{:S(2)}) %collective-permute-start.7) | collective-permute-done | bytes 4128 | tf_op jit(solution)/shard_map/while/body/eval_jaxpr/ppermute | solution.py:22
  493.7 5.6 collective-permute-done.9
  499.8 5.6 collective-permute-start.5
  515.2 7.6 %collective-permute-done.7 = f32[2,4,1,128]{3,2,1,0:T(1,128)S(1)} collective-permute-done((f32[2,4,1,128]{3,2,1,0:T(1,128)S(1)}, f32[2,4,1,128]{3,2,1,0:T(1,128)S(1)}, u32[]{:S(2)}, u32[]{:S(2)}) %collective-permute-start.7) | collective-permute-done | bytes 4128 | tf_op jit(solution)/shard_map/while/body/eval_jaxpr/ppermute | solution.py:22
  529.1 5.6 collective-permute-done.9
  550.6 7.6 %collective-permute-done.7 = f32[2,4,1,128]{3,2,1,0:T(1,128)S(1)} collective-permute-done((f32[2,4,1,128]{3,2,1,0:T(1,128)S(1)}, f32[2,4,1,128]{3,2,1,0:T(1,128)S(1)}, u32[]{:S(2)}, u32[]{:S(2)}) %collective-permute-start.7) | collective-permute-done | bytes 4128 | tf_op jit(solution)/shard_map/while/body/eval_jaxpr/ppermute | solution.py:22
  564.5 5.6 collective-permute-done.9
  585.9 7.6 %collective-permute-done.7 = f32[2,4,1,128]{3,2,1,0:T(1,128)S(1)} collective-permute-done((f32[2,4,1,128]{3,2,1,0:T(1,128)S(1)}, f32[2,4,1,128]{3,2,1,0:T(1,128)S(1)}, u32[]{:S(2)}, u32[]{:S(2)}) %collective-permute-start.7) | collective-permute-done | bytes 4128 | tf_op jit(solution)/shard_map/while/body/eval_jaxpr/ppermute | solution.py:22
  599.8 5.6 collective-permute-done.9
  621.3 7.6 %collective-permute-done.7 = f32[2,4,1,128]{3,2,1,0:T(1,128)S(1)} collective-permute-done((f32[2,4,1,128]{3,2,1,0:T(1,128)S(1)}, f32[2,4,1,128]{3,2,1,0:T(1,128)S(1)}, u32[]{:S(2)}, u32[]{:S(2)}) %collective-permute-start.7) | collective-permute-done | bytes 4128 | tf_op jit(solution)/shard_map/while/body/eval_jaxpr/ppermute | solution.py:22
  635.2 5.6 collective-permute-done.9
  641.2 5.6 collective-permute-start.5
  656.6 7.6 %collective-permute-done.7 = f32[2,4,1,128]{3,2,1,0:T(1,128)S(1)} collective-permute-done((f32[2,4,1,128]{3,2,1,0:T(1,128)S(1)}, f32[2,4,1,128]{3,2,1,0:T(1,128)S(1)}, u32[]{:S(2)}, u32[]{:S(2)}) %collective-permute-start.7) | collective-permute-done | bytes 4128 | tf_op jit(solution)/shard_map/while/body/eval_jaxpr/ppermute | solution.py:22
  670.5 5.6 collective-permute-done.9
  692.0 7.6 %collective-permute-done.7 = f32[2,4,1,128]{3,2,1,0:T(1,128)S(1)} collective-permute-done((f32[2,4,1,128]{3,2,1,0:T(1,128)S(1)}, f32[2,4,1,128]{3,2,1,0:T(1,128)S(1)}, u32[]{:S(2)}, u32[]{:S(2)}) %collective-permute-start.7) | collective-permute-done | bytes 4128 | tf_op jit(solution)/shard_map/while/body/eval_jaxpr/ppermute | solution.py:22
  705.9 5.6 collective-permute-done.9
  (345 shorter events, 403.7 us)
Async XLA Ops:
  0.8 10.7 %collective-permute-start.11 = (f32[2,4,1,128]{3,2,1,0:T(1,128)S(1)}, f32[2,4,1,128]{3,2,1,0:T(1,128)S(1)}, u32[]{:S(2)}, u32[]{:S(2)}) collective-permute-start(f32[2,4,1,128]{3,2,1,0:T(1,128)S(1)} %get-tuple-element.261), channel_id=1, source_target_pairs={{8,0},{16,8},{24,16},{32,24},{40,32},{48,40},{56,48},{64,56},{72,6... | collective-permute-start | bytes 12296 | tf_op jit(solution)/shard_map/ppermute | solution.py:25
  9.5 11.5 %collective-permute-start.10 = (f32[2,4,1,128]{3,2,1,0:T(1,128)S(1)}, f32[2,4,1,128]{3,2,1,0:T(1,128)S(1)}, u32[]{:S(2)}, u32[]{:S(2)}) collective-permute-start(f32[2,4,1,128]{3,2,1,0:T(1,128)S(1)} %get-tuple-element.260), channel_id=1, source_target_pairs={{0,8},{8,16},{16,24},{24,32},{32,40},{40,48},{48,56},{56,64},{64,7... | collective-permute-start | bytes 12296 | tf_op jit(solution)/shard_map/ppermute | solution.py:22
  24.1 9.7 %collective-permute-start.12 = (f32[2,4,66,1]{3,2,1,0:T(8,128)S(1)}, f32[2,4,66,1]{3,2,1,0:T(8,128)S(1)}, u32[]{:S(2)}, u32[]{:S(2)}) collective-permute-start(f32[2,4,66,1]{3,2,1,0:T(8,128)S(1)} %get-tuple-element.226), channel_id=1, source_target_pairs={{0,1},{1,2},{2,3},{3,4},{4,5},{5,6},{6,7},{7,0},{8,9},{9,10},{10,1... | collective-permute-start | bytes 6344 | tf_op jit(solution)/shard_map/ppermute | solution.py:22
  36.8 11.5 %collective-permute-start.14 = (f32[2,4,1,128]{3,2,1,0:T(1,128)S(1)}, f32[2,4,1,128]{3,2,1,0:T(1,128)S(1)}, u32[]{:S(2)}, u32[]{:S(2)}) collective-permute-start(f32[2,4,1,128]{3,2,1,0:T(1,128)S(1)} %get-tuple-element.254), channel_id=1, source_target_pairs={{0,8},{8,16},{16,24},{24,32},{32,40},{40,48},{48,56},{56,64},{64,7... | collective-permute-start | bytes 12296 | tf_op jit(solution)/shard_map/ppermute | solution.py:22
  50.4 9.8 %collective-permute-start.16 = (f32[2,4,66,1]{3,2,1,0:T(8,128)S(1)}, f32[2,4,66,1]{3,2,1,0:T(8,128)S(1)}, u32[]{:S(2)}, u32[]{:S(2)}) collective-permute-start(f32[2,4,66,1]{3,2,1,0:T(8,128)S(1)} %get-tuple-element.224), channel_id=1, source_target_pairs={{0,1},{1,2},{2,3},{3,4},{4,5},{5,6},{6,7},{7,0},{8,9},{9,10},{10,1... | collective-permute-start | bytes 6344 | tf_op jit(solution)/shard_map/ppermute | solution.py:22
  62.6 11.5 %collective-permute-start.18 = (f32[2,4,1,128]{3,2,1,0:T(1,128)S(1)}, f32[2,4,1,128]{3,2,1,0:T(1,128)S(1)}, u32[]{:S(2)}, u32[]{:S(2)}) collective-permute-start(f32[2,4,1,128]{3,2,1,0:T(1,128)S(1)} %get-tuple-element.250), channel_id=1, source_target_pairs={{0,8},{8,16},{16,24},{24,32},{32,40},{40,48},{48,56},{56,64},{64,7... | collective-permute-start | bytes 12296 | tf_op jit(solution)/shard_map/ppermute | solution.py:22
  76.2 9.8 %collective-permute-start.20 = (f32[2,4,66,1]{3,2,1,0:T(8,128)S(1)}, f32[2,4,66,1]{3,2,1,0:T(8,128)S(1)}, u32[]{:S(2)}, u32[]{:S(2)}) collective-permute-start(f32[2,4,66,1]{3,2,1,0:T(8,128)S(1)} %get-tuple-element.222), channel_id=1, source_target_pairs={{0,1},{1,2},{2,3},{3,4},{4,5},{5,6},{6,7},{7,0},{8,9},{9,10},{10,1... | collective-permute-start | bytes 6344 | tf_op jit(solution)/shard_map/ppermute | solution.py:22
  88.4 11.5 %collective-permute-start.22 = (f32[2,4,1,128]{3,2,1,0:T(1,128)S(1)}, f32[2,4,1,128]{3,2,1,0:T(1,128)S(1)}, u32[]{:S(2)}, u32[]{:S(2)}) collective-permute-start(f32[2,4,1,128]{3,2,1,0:T(1,128)S(1)} %get-tuple-element.246), channel_id=1, source_target_pairs={{0,8},{8,16},{16,24},{24,32},{32,40},{40,48},{48,56},{56,64},{64,7... | collective-permute-start | bytes 12296 | tf_op jit(solution)/shard_map/ppermute | solution.py:22
  102.0 9.8 %collective-permute-start.24 = (f32[2,4,66,1]{3,2,1,0:T(8,128)S(1)}, f32[2,4,66,1]{3,2,1,0:T(8,128)S(1)}, u32[]{:S(2)}, u32[]{:S(2)}) collective-permute-start(f32[2,4,66,1]{3,2,1,0:T(8,128)S(1)} %get-tuple-element.220), channel_id=1, source_target_pairs={{0,1},{1,2},{2,3},{3,4},{4,5},{5,6},{6,7},{7,0},{8,9},{9,10},{10,1... | collective-permute-start | bytes 6344 | tf_op jit(solution)/shard_map/ppermute | solution.py:22
  123.3 11.5 %collective-permute-start.2 = (f32[2,4,1,128]{3,2,1,0:T(1,128)S(1)}, f32[2,4,1,128]{3,2,1,0:T(1,128)S(1)}, u32[]{:S(2)}, u32[]{:S(2)}) collective-permute-start(f32[2,4,1,128]{3,2,1,0:T(1,128)S(1)} %get-tuple-element.362), channel_id=1, source_target_pairs={{0,8},{8,16},{16,24},{24,32},{32,40},{40,48},{48,56},{56,64},{64,7... | collective-permute-start | bytes 12296 | tf_op jit(solution)/shard_map/while/body/eval_jaxpr/ppermute | solution.py:22
  137.0 9.8 %collective-permute-start.4 = (f32[2,4,66,1]{3,2,1,0:T(8,128)S(1)}, f32[2,4,66,1]{3,2,1,0:T(8,128)S(1)}, u32[]{:S(2)}, u32[]{:S(2)}) collective-permute-start(f32[2,4,66,1]{3,2,1,0:T(8,128)S(1)} %get-tuple-element.364), channel_id=1, source_target_pairs={{0,1},{1,2},{2,3},{3,4},{4,5},{5,6},{6,7},{7,0},{8,9},{9,10},{10,1... | collective-permute-start | bytes 6344 | tf_op jit(solution)/shard_map/while/body/eval_jaxpr/ppermute | solution.py:22
  158.3 11.5 %collective-permute-start.2 = (f32[2,4,1,128]{3,2,1,0:T(1,128)S(1)}, f32[2,4,1,128]{3,2,1,0:T(1,128)S(1)}, u32[]{:S(2)}, u32[]{:S(2)}) collective-permute-start(f32[2,4,1,128]{3,2,1,0:T(1,128)S(1)} %get-tuple-element.362), channel_id=1, source_target_pairs={{0,8},{8,16},{16,24},{24,32},{32,40},{40,48},{48,56},{56,64},{64,7... | collective-permute-start | bytes 12296 | tf_op jit(solution)/shard_map/while/body/eval_jaxpr/ppermute | solution.py:22
  171.9 9.8 %collective-permute-start.4 = (f32[2,4,66,1]{3,2,1,0:T(8,128)S(1)}, f32[2,4,66,1]{3,2,1,0:T(8,128)S(1)}, u32[]{:S(2)}, u32[]{:S(2)}) collective-permute-start(f32[2,4,66,1]{3,2,1,0:T(8,128)S(1)} %get-tuple-element.364), channel_id=1, source_target_pairs={{0,1},{1,2},{2,3},{3,4},{4,5},{5,6},{6,7},{7,0},{8,9},{9,10},{10,1... | collective-permute-start | bytes 6344 | tf_op jit(solution)/shard_map/while/body/eval_jaxpr/ppermute | solution.py:22
  193.3 11.5 %collective-permute-start.2 = (f32[2,4,1,128]{3,2,1,0:T(1,128)S(1)}, f32[2,4,1,128]{3,2,1,0:T(1,128)S(1)}, u32[]{:S(2)}, u32[]{:S(2)}) collective-permute-start(f32[2,4,1,128]{3,2,1,0:T(1,128)S(1)} %get-tuple-element.362), channel_id=1, source_target_pairs={{0,8},{8,16},{16,24},{24,32},{32,40},{40,48},{48,56},{56,64},{64,7... | collective-permute-start | bytes 12296 | tf_op jit(solution)/shard_map/while/body/eval_jaxpr/ppermute | solution.py:22
  206.9 9.8 %collective-permute-start.4 = (f32[2,4,66,1]{3,2,1,0:T(8,128)S(1)}, f32[2,4,66,1]{3,2,1,0:T(8,128)S(1)}, u32[]{:S(2)}, u32[]{:S(2)}) collective-permute-start(f32[2,4,66,1]{3,2,1,0:T(8,128)S(1)} %get-tuple-element.364), channel_id=1, source_target_pairs={{0,1},{1,2},{2,3},{3,4},{4,5},{5,6},{6,7},{7,0},{8,9},{9,10},{10,1... | collective-permute-start | bytes 6344 | tf_op jit(solution)/shard_map/while/body/eval_jaxpr/ppermute | solution.py:22
  217.2 10.3 %collective-permute-start = (f32[2,4,64,128]{3,2,1,0:T(8,128)S(1)}, f32[2,4,64,128]{3,2,1,0:T(8,128)S(1)}, u32[]{:S(2)}, u32[]{:S(2)}) collective-permute-start(f32[2,4,64,128]{3,2,1,0:T(8,128)S(1)} %get-tuple-element.395), channel_id=1, source_target_pairs={{0,128},{128,256},{256,384},{384,512},{512,640},{640,768},{768,896... | collective-permute-start | bytes 786440 | tf_op jit(solution)/shard_map/while/body/eval_jaxpr/ppermute | solution.py:33
  229.5 11.5 %collective-permute-start.2 = (f32[2,4,1,128]{3,2,1,0:T(1,128)S(1)}, f32[2,4,1,128]{3,2,1,0:T(1,128)S(1)}, u32[]{:S(2)}, u32[]{:S(2)}) collective-permute-start(f32[2,4,1,128]{3,2,1,0:T(1,128)S(1)} %get-tuple-element.362), channel_id=1, source_target_pairs={{0,8},{8,16},{16,24},{24,32},{32,40},{40,48},{48,56},{56,64},{64,7... | collective-permute-start | bytes 12296 | tf_op jit(solution)/shard_map/while/body/eval_jaxpr/ppermute | solution.py:22
  243.1 9.8 %collective-permute-start.4 = (f32[2,4,66,1]{3,2,1,0:T(8,128)S(1)}, f32[2,4,66,1]{3,2,1,0:T(8,128)S(1)}, u32[]{:S(2)}, u32[]{:S(2)}) collective-permute-start(f32[2,4,66,1]{3,2,1,0:T(8,128)S(1)} %get-tuple-element.364), channel_id=1, source_target_pairs={{0,1},{1,2},{2,3},{3,4},{4,5},{5,6},{6,7},{7,0},{8,9},{9,10},{10,1... | collective-permute-start | bytes 6344 | tf_op jit(solution)/shard_map/while/body/eval_jaxpr/ppermute | solution.py:22
  253.4 9.5 %collective-permute-start = (f32[2,4,64,128]{3,2,1,0:T(8,128)S(1)}, f32[2,4,64,128]{3,2,1,0:T(8,128)S(1)}, u32[]{:S(2)}, u32[]{:S(2)}) collective-permute-start(f32[2,4,64,128]{3,2,1,0:T(8,128)S(1)} %get-tuple-element.395), channel_id=1, source_target_pairs={{0,128},{128,256},{256,384},{384,512},{512,640},{640,768},{768,896... | collective-permute-start | bytes 786440 | tf_op jit(solution)/shard_map/while/body/eval_jaxpr/ppermute | solution.py:33
  264.8 11.5 %collective-permute-start.2 = (f32[2,4,1,128]{3,2,1,0:T(1,128)S(1)}, f32[2,4,1,128]{3,2,1,0:T(1,128)S(1)}, u32[]{:S(2)}, u32[]{:S(2)}) collective-permute-start(f32[2,4,1,128]{3,2,1,0:T(1,128)S(1)} %get-tuple-element.362), channel_id=1, source_target_pairs={{0,8},{8,16},{16,24},{24,32},{32,40},{40,48},{48,56},{56,64},{64,7... | collective-permute-start | bytes 12296 | tf_op jit(solution)/shard_map/while/body/eval_jaxpr/ppermute | solution.py:22
  278.5 9.8 %collective-permute-start.4 = (f32[2,4,66,1]{3,2,1,0:T(8,128)S(1)}, f32[2,4,66,1]{3,2,1,0:T(8,128)S(1)}, u32[]{:S(2)}, u32[]{:S(2)}) collective-permute-start(f32[2,4,66,1]{3,2,1,0:T(8,128)S(1)} %get-tuple-element.364), channel_id=1, source_target_pairs={{0,1},{1,2},{2,3},{3,4},{4,5},{5,6},{6,7},{7,0},{8,9},{9,10},{10,1... | collective-permute-start | bytes 6344 | tf_op jit(solution)/shard_map/while/body/eval_jaxpr/ppermute | solution.py:22
  300.2 11.5 %collective-permute-start.2 = (f32[2,4,1,128]{3,2,1,0:T(1,128)S(1)}, f32[2,4,1,128]{3,2,1,0:T(1,128)S(1)}, u32[]{:S(2)}, u32[]{:S(2)}) collective-permute-start(f32[2,4,1,128]{3,2,1,0:T(1,128)S(1)} %get-tuple-element.362), channel_id=1, source_target_pairs={{0,8},{8,16},{16,24},{24,32},{32,40},{40,48},{48,56},{56,64},{64,7... | collective-permute-start | bytes 12296 | tf_op jit(solution)/shard_map/while/body/eval_jaxpr/ppermute | solution.py:22
  313.8 9.8 %collective-permute-start.4 = (f32[2,4,66,1]{3,2,1,0:T(8,128)S(1)}, f32[2,4,66,1]{3,2,1,0:T(8,128)S(1)}, u32[]{:S(2)}, u32[]{:S(2)}) collective-permute-start(f32[2,4,66,1]{3,2,1,0:T(8,128)S(1)} %get-tuple-element.364), channel_id=1, source_target_pairs={{0,1},{1,2},{2,3},{3,4},{4,5},{5,6},{6,7},{7,0},{8,9},{9,10},{10,1... | collective-permute-start | bytes 6344 | tf_op jit(solution)/shard_map/while/body/eval_jaxpr/ppermute | solution.py:22
  335.6 11.5 %collective-permute-start.2 = (f32[2,4,1,128]{3,2,1,0:T(1,128)S(1)}, f32[2,4,1,128]{3,2,1,0:T(1,128)S(1)}, u32[]{:S(2)}, u32[]{:S(2)}) collective-permute-start(f32[2,4,1,128]{3,2,1,0:T(1,128)S(1)} %get-tuple-element.362), channel_id=1, source_target_pairs={{0,8},{8,16},{16,24},{24,32},{32,40},{40,48},{48,56},{56,64},{64,7... | collective-permute-start | bytes 12296 | tf_op jit(solution)/shard_map/while/body/eval_jaxpr/ppermute | solution.py:22
  349.2 9.8 %collective-permute-start.4 = (f32[2,4,66,1]{3,2,1,0:T(8,128)S(1)}, f32[2,4,66,1]{3,2,1,0:T(8,128)S(1)}, u32[]{:S(2)}, u32[]{:S(2)}) collective-permute-start(f32[2,4,66,1]{3,2,1,0:T(8,128)S(1)} %get-tuple-element.364), channel_id=1, source_target_pairs={{0,1},{1,2},{2,3},{3,4},{4,5},{5,6},{6,7},{7,0},{8,9},{9,10},{10,1... | collective-permute-start | bytes 6344 | tf_op jit(solution)/shard_map/while/body/eval_jaxpr/ppermute | solution.py:22
  362.2 11.5 %collective-permute-start.26 = (f32[2,4,1,128]{3,2,1,0:T(1,128)S(1)}, f32[2,4,1,128]{3,2,1,0:T(1,128)S(1)}, u32[]{:S(2)}, u32[]{:S(2)}) collective-permute-start(f32[2,4,1,128]{3,2,1,0:T(1,128)S(1)} %get-tuple-element.242), channel_id=1, source_target_pairs={{0,8},{8,16},{16,24},{24,32},{32,40},{40,48},{48,56},{56,64},{64,7... | collective-permute-start | bytes 12296 | tf_op jit(solution)/shard_map/ppermute | solution.py:22
  376.8 9.8 %collective-permute-start.28 = (f32[2,4,66,1]{3,2,1,0:T(8,128)S(1)}, f32[2,4,66,1]{3,2,1,0:T(8,128)S(1)}, u32[]{:S(2)}, u32[]{:S(2)}) collective-permute-start(f32[2,4,66,1]{3,2,1,0:T(8,128)S(1)} %get-tuple-element.218), channel_id=1, source_target_pairs={{0,1},{1,2},{2,3},{3,4},{4,5},{5,6},{6,7},{7,0},{8,9},{9,10},{10,1... | collective-permute-start | bytes 6344 | tf_op jit(solution)/shard_map/ppermute | solution.py:22
  389.0 11.5 %collective-permute-start.30 = (f32[2,4,1,128]{3,2,1,0:T(1,128)S(1)}, f32[2,4,1,128]{3,2,1,0:T(1,128)S(1)}, u32[]{:S(2)}, u32[]{:S(2)}) collective-permute-start(f32[2,4,1,128]{3,2,1,0:T(1,128)S(1)} %get-tuple-element.238), channel_id=1, source_target_pairs={{0,8},{8,16},{16,24},{24,32},{32,40},{40,48},{48,56},{56,64},{64,7... | collective-permute-start | bytes 12296 | tf_op jit(solution)/shard_map/ppermute | solution.py:22
  402.6 9.8 %collective-permute-start.32 = (f32[2,4,66,1]{3,2,1,0:T(8,128)S(1)}, f32[2,4,66,1]{3,2,1,0:T(8,128)S(1)}, u32[]{:S(2)}, u32[]{:S(2)}) collective-permute-start(f32[2,4,66,1]{3,2,1,0:T(8,128)S(1)} %get-tuple-element.216), channel_id=1, source_target_pairs={{0,1},{1,2},{2,3},{3,4},{4,5},{5,6},{6,7},{7,0},{8,9},{9,10},{10,1... | collective-permute-start | bytes 6344 | tf_op jit(solution)/shard_map/ppermute | solution.py:22
  414.7 11.5 %collective-permute-start.34 = (f32[2,4,1,128]{3,2,1,0:T(1,128)S(1)}, f32[2,4,1,128]{3,2,1,0:T(1,128)S(1)}, u32[]{:S(2)}, u32[]{:S(2)}) collective-permute-start(f32[2,4,1,128]{3,2,1,0:T(1,128)S(1)} %get-tuple-element.234), channel_id=1, source_target_pairs={{0,8},{8,16},{16,24},{24,32},{32,40},{40,48},{48,56},{56,64},{64,7... | collective-permute-start | bytes 12296 | tf_op jit(solution)/shard_map/ppermute | solution.py:22
  428.4 9.8 %collective-permute-start.36 = (f32[2,4,66,1]{3,2,1,0:T(8,128)S(1)}, f32[2,4,66,1]{3,2,1,0:T(8,128)S(1)}, u32[]{:S(2)}, u32[]{:S(2)}) collective-permute-start(f32[2,4,66,1]{3,2,1,0:T(8,128)S(1)} %get-tuple-element.214), channel_id=1, source_target_pairs={{0,1},{1,2},{2,3},{3,4},{4,5},{5,6},{6,7},{7,0},{8,9},{9,10},{10,1... | collective-permute-start | bytes 6344 | tf_op jit(solution)/shard_map/ppermute | solution.py:22
  440.5 11.5 %collective-permute-start.38 = (f32[2,4,1,128]{3,2,1,0:T(1,128)S(1)}, f32[2,4,1,128]{3,2,1,0:T(1,128)S(1)}, u32[]{:S(2)}, u32[]{:S(2)}) collective-permute-start(f32[2,4,1,128]{3,2,1,0:T(1,128)S(1)} %get-tuple-element.230), channel_id=1, source_target_pairs={{0,8},{8,16},{16,24},{24,32},{32,40},{40,48},{48,56},{56,64},{64,7... | collective-permute-start | bytes 12296 | tf_op jit(solution)/shard_map/ppermute | solution.py:22
  454.2 9.8 %collective-permute-start.40 = (f32[2,4,66,1]{3,2,1,0:T(8,128)S(1)}, f32[2,4,66,1]{3,2,1,0:T(8,128)S(1)}, u32[]{:S(2)}, u32[]{:S(2)}) collective-permute-start(f32[2,4,66,1]{3,2,1,0:T(8,128)S(1)} %get-tuple-element.212), channel_id=1, source_target_pairs={{0,1},{1,2},{2,3},{3,4},{4,5},{5,6},{6,7},{7,0},{8,9},{9,10},{10,1... | collective-permute-start | bytes 6344 | tf_op jit(solution)/shard_map/ppermute | solution.py:22
  475.9 11.5 %collective-permute-start.7 = (f32[2,4,1,128]{3,2,1,0:T(1,128)S(1)}, f32[2,4,1,128]{3,2,1,0:T(1,128)S(1)}, u32[]{:S(2)}, u32[]{:S(2)}) collective-permute-start(f32[2,4,1,128]{3,2,1,0:T(1,128)S(1)} %get-tuple-element.377), channel_id=1, source_target_pairs={{0,8},{8,16},{16,24},{24,32},{32,40},{40,48},{48,56},{56,64},{64,7... | collective-permute-start | bytes 12296 | tf_op jit(solution)/shard_map/while/body/eval_jaxpr/ppermute | solution.py:22
  489.5 9.8 %collective-permute-start.9 = (f32[2,4,66,1]{3,2,1,0:T(8,128)S(1)}, f32[2,4,66,1]{3,2,1,0:T(8,128)S(1)}, u32[]{:S(2)}, u32[]{:S(2)}) collective-permute-start(f32[2,4,66,1]{3,2,1,0:T(8,128)S(1)} %get-tuple-element.379), channel_id=1, source_target_pairs={{0,1},{1,2},{2,3},{3,4},{4,5},{5,6},{6,7},{7,0},{8,9},{9,10},{10,1... | collective-permute-start | bytes 6344 | tf_op jit(solution)/shard_map/while/body/eval_jaxpr/ppermute | solution.py:22
  499.8 9.5 %collective-permute-start.5 = (f32[2,4,64,128]{3,2,1,0:T(8,128)S(1)}, f32[2,4,64,128]{3,2,1,0:T(8,128)S(1)}, u32[]{:S(2)}, u32[]{:S(2)}) collective-permute-start(f32[2,4,64,128]{3,2,1,0:T(8,128)S(1)} %get-tuple-element.420), channel_id=1, source_target_pairs={{0,128},{128,256},{256,384},{384,512},{512,640},{640,768},{768,896... | collective-permute-start | bytes 786440 | tf_op jit(solution)/shard_map/while/body/eval_jaxpr/ppermute | solution.py:33
  511.3 11.5 %collective-permute-start.7 = (f32[2,4,1,128]{3,2,1,0:T(1,128)S(1)}, f32[2,4,1,128]{3,2,1,0:T(1,128)S(1)}, u32[]{:S(2)}, u32[]{:S(2)}) collective-permute-start(f32[2,4,1,128]{3,2,1,0:T(1,128)S(1)} %get-tuple-element.377), channel_id=1, source_target_pairs={{0,8},{8,16},{16,24},{24,32},{32,40},{40,48},{48,56},{56,64},{64,7... | collective-permute-start | bytes 12296 | tf_op jit(solution)/shard_map/while/body/eval_jaxpr/ppermute | solution.py:22
  524.9 9.8 %collective-permute-start.9 = (f32[2,4,66,1]{3,2,1,0:T(8,128)S(1)}, f32[2,4,66,1]{3,2,1,0:T(8,128)S(1)}, u32[]{:S(2)}, u32[]{:S(2)}) collective-permute-start(f32[2,4,66,1]{3,2,1,0:T(8,128)S(1)} %get-tuple-element.379), channel_id=1, source_target_pairs={{0,1},{1,2},{2,3},{3,4},{4,5},{5,6},{6,7},{7,0},{8,9},{9,10},{10,1... | collective-permute-start | bytes 6344 | tf_op jit(solution)/shard_map/while/body/eval_jaxpr/ppermute | solution.py:22
  546.6 11.5 %collective-permute-start.7 = (f32[2,4,1,128]{3,2,1,0:T(1,128)S(1)}, f32[2,4,1,128]{3,2,1,0:T(1,128)S(1)}, u32[]{:S(2)}, u32[]{:S(2)}) collective-permute-start(f32[2,4,1,128]{3,2,1,0:T(1,128)S(1)} %get-tuple-element.377), channel_id=1, source_target_pairs={{0,8},{8,16},{16,24},{24,32},{32,40},{40,48},{48,56},{56,64},{64,7... | collective-permute-start | bytes 12296 | tf_op jit(solution)/shard_map/while/body/eval_jaxpr/ppermute | solution.py:22
  560.2 9.8 %collective-permute-start.9 = (f32[2,4,66,1]{3,2,1,0:T(8,128)S(1)}, f32[2,4,66,1]{3,2,1,0:T(8,128)S(1)}, u32[]{:S(2)}, u32[]{:S(2)}) collective-permute-start(f32[2,4,66,1]{3,2,1,0:T(8,128)S(1)} %get-tuple-element.379), channel_id=1, source_target_pairs={{0,1},{1,2},{2,3},{3,4},{4,5},{5,6},{6,7},{7,0},{8,9},{9,10},{10,1... | collective-permute-start | bytes 6344 | tf_op jit(solution)/shard_map/while/body/eval_jaxpr/ppermute | solution.py:22
  582.0 11.5 %collective-permute-start.7 = (f32[2,4,1,128]{3,2,1,0:T(1,128)S(1)}, f32[2,4,1,128]{3,2,1,0:T(1,128)S(1)}, u32[]{:S(2)}, u32[]{:S(2)}) collective-permute-start(f32[2,4,1,128]{3,2,1,0:T(1,128)S(1)} %get-tuple-element.377), channel_id=1, source_target_pairs={{0,8},{8,16},{16,24},{24,32},{32,40},{40,48},{48,56},{56,64},{64,7... | collective-permute-start | bytes 12296 | tf_op jit(solution)/shard_map/while/body/eval_jaxpr/ppermute | solution.py:22
  595.6 9.8 %collective-permute-start.9 = (f32[2,4,66,1]{3,2,1,0:T(8,128)S(1)}, f32[2,4,66,1]{3,2,1,0:T(8,128)S(1)}, u32[]{:S(2)}, u32[]{:S(2)}) collective-permute-start(f32[2,4,66,1]{3,2,1,0:T(8,128)S(1)} %get-tuple-element.379), channel_id=1, source_target_pairs={{0,1},{1,2},{2,3},{3,4},{4,5},{5,6},{6,7},{7,0},{8,9},{9,10},{10,1... | collective-permute-start | bytes 6344 | tf_op jit(solution)/shard_map/while/body/eval_jaxpr/ppermute | solution.py:22
  617.3 11.5 %collective-permute-start.7 = (f32[2,4,1,128]{3,2,1,0:T(1,128)S(1)}, f32[2,4,1,128]{3,2,1,0:T(1,128)S(1)}, u32[]{:S(2)}, u32[]{:S(2)}) collective-permute-start(f32[2,4,1,128]{3,2,1,0:T(1,128)S(1)} %get-tuple-element.377), channel_id=1, source_target_pairs={{0,8},{8,16},{16,24},{24,32},{32,40},{40,48},{48,56},{56,64},{64,7... | collective-permute-start | bytes 12296 | tf_op jit(solution)/shard_map/while/body/eval_jaxpr/ppermute | solution.py:22
  631.0 9.8 %collective-permute-start.9 = (f32[2,4,66,1]{3,2,1,0:T(8,128)S(1)}, f32[2,4,66,1]{3,2,1,0:T(8,128)S(1)}, u32[]{:S(2)}, u32[]{:S(2)}) collective-permute-start(f32[2,4,66,1]{3,2,1,0:T(8,128)S(1)} %get-tuple-element.379), channel_id=1, source_target_pairs={{0,1},{1,2},{2,3},{3,4},{4,5},{5,6},{6,7},{7,0},{8,9},{9,10},{10,1... | collective-permute-start | bytes 6344 | tf_op jit(solution)/shard_map/while/body/eval_jaxpr/ppermute | solution.py:22
  652.7 11.5 %collective-permute-start.7 = (f32[2,4,1,128]{3,2,1,0:T(1,128)S(1)}, f32[2,4,1,128]{3,2,1,0:T(1,128)S(1)}, u32[]{:S(2)}, u32[]{:S(2)}) collective-permute-start(f32[2,4,1,128]{3,2,1,0:T(1,128)S(1)} %get-tuple-element.377), channel_id=1, source_target_pairs={{0,8},{8,16},{16,24},{24,32},{32,40},{40,48},{48,56},{56,64},{64,7... | collective-permute-start | bytes 12296 | tf_op jit(solution)/shard_map/while/body/eval_jaxpr/ppermute | solution.py:22
  666.3 9.8 %collective-permute-start.9 = (f32[2,4,66,1]{3,2,1,0:T(8,128)S(1)}, f32[2,4,66,1]{3,2,1,0:T(8,128)S(1)}, u32[]{:S(2)}, u32[]{:S(2)}) collective-permute-start(f32[2,4,66,1]{3,2,1,0:T(8,128)S(1)} %get-tuple-element.379), channel_id=1, source_target_pairs={{0,1},{1,2},{2,3},{3,4},{4,5},{5,6},{6,7},{7,0},{8,9},{9,10},{10,1... | collective-permute-start | bytes 6344 | tf_op jit(solution)/shard_map/while/body/eval_jaxpr/ppermute | solution.py:22
  688.0 11.5 %collective-permute-start.7 = (f32[2,4,1,128]{3,2,1,0:T(1,128)S(1)}, f32[2,4,1,128]{3,2,1,0:T(1,128)S(1)}, u32[]{:S(2)}, u32[]{:S(2)}) collective-permute-start(f32[2,4,1,128]{3,2,1,0:T(1,128)S(1)} %get-tuple-element.377), channel_id=1, source_target_pairs={{0,8},{8,16},{16,24},{24,32},{32,40},{40,48},{48,56},{56,64},{64,7... | collective-permute-start | bytes 12296 | tf_op jit(solution)/shard_map/while/body/eval_jaxpr/ppermute | solution.py:22
  701.7 9.8 %collective-permute-start.9 = (f32[2,4,66,1]{3,2,1,0:T(8,128)S(1)}, f32[2,4,66,1]{3,2,1,0:T(8,128)S(1)}, u32[]{:S(2)}, u32[]{:S(2)}) collective-permute-start(f32[2,4,66,1]{3,2,1,0:T(8,128)S(1)} %get-tuple-element.379), channel_id=1, source_target_pairs={{0,1},{1,2},{2,3},{3,4},{4,5},{5,6},{6,7},{7,0},{8,9},{9,10},{10,1... | collective-permute-start | bytes 6344 | tf_op jit(solution)/shard_map/while/body/eval_jaxpr/ppermute | solution.py:22
  (65 other events, 552.8 us)
where the time goes:
time: 719 us; the launch traced here: 713 us
  waiting for transfers between devices  385 us (54%)
  starting transfers between devices  307 us (43%)
  other arithmetic  12 us (2%)
    ppermute x44, waiting for transfers between devices, padded_2(): lax.ppermute(lax.slice_in_dim(block, block.shape[dim] - width, None, axis...  291 us
    ppermute x44, starting transfers between devices, padded_2(): lax.ppermute(lax.slice_in_dim(block, block.shape[dim] - width, None, axis...  137 us
    ppermute x44, starting transfers between devices, padded_2(): lax.ppermute(lax.slice_in_dim(block, 0, width, axis=dim), axis, backward)  91.4 us
    ppermute x14, starting transfers between devices, from_behind(): return lax.ppermute(block, axis, route)  78.1 us
    ppermute x14, waiting for transfers between devices, from_behind(): return lax.ppermute(block, axis, route)  54 us
    ppermute x44, waiting for transfers between devices, padded_2(): lax.ppermute(lax.slice_in_dim(block, 0, width, axis=dim), axis, backward)  39.3 us
  transfers between devices with their start and end apart: 102, of which 80 were waited for; matrix products, arithmetic and copies ran while one was open for 0% of the time, Pallas kernels for 0%

commit v1 on v0

v1 whole, which is shorter than its diff:
```python
import jax
import jax.numpy as jnp
from jax import lax
from jax.experimental import pallas as pl
from jax.experimental.pallas import tpu as pltpu
from jax.sharding import PartitionSpec as P

FINE = 4
SLICES = 8
HALO = 16
SUB = 32
WIN = SUB + 2 * HALO
ROWS = 64
LANES = 128
EXT = ROWS + 2 * HALO
TILES = EXT // 8

spread_fast = 0.2
spread_slow = 0.1
fine_step = 0.125
coarse_step = 0.5

PAIRS = ((0, 3), (1, 2))


def lane_index():
    return lax.broadcasted_iota(jnp.int32, (8, LANES), 1)


def roll(block, shift, axis):
    shift = shift % block.shape[axis]
    return block if shift == 0 else pltpu.roll(block, shift, axis)


def ext_tile(low, own, high, index):
    if index < 2:
        return low[8 * index : 8 * index + 8, :]
    if index < 10:
        return own[8 * (index - 2) : 8 * (index - 2) + 8, :]
    return high[8 * (index - 10) : 8 * (index - 10) + 8, :]


def strips_kernel(state, rates, low, high, to_low, to_high):
    lane = lane_index()
    for which, source in enumerate((state, rates)):
        for tile in range(TILES):
            first = jnp.zeros((8, LANES), jnp.float32)
            last = jnp.zeros((8, LANES), jnp.float32)
            for k in range(8):
                c, x = k // 4, k % 4
                rows = ext_tile(low.at[which, c, x], source.at[c, x], high.at[which, c, x], tile)
                here = (lane >= 16 * k) & (lane < 16 * k + 16)
                first = jnp.where(here, roll(rows, 16 * k, 1), first)
                last = jnp.where(here, roll(rows, 16 * k + 16, 1), last)
            to_low[which, 8 * tile : 8 * tile + 8, :] = first
            to_high[which, 8 * tile : 8 * tile + 8, :] = last


def windows_of(low, own, high, left, right, tile, c, pair, tz, lane):
    parts = []
    for half, x in enumerate(PAIRS[pair]):
        rows = ext_tile(low.at[c, x], own.at[c, x], high.at[c, x], tile)
        parts.append(roll(rows, 64 * half - (SUB * tz - HALO), 1))
    block = jnp.where(lane < 64, parts[0], parts[1])
    if tz in (0, 3):
        edge = left if tz == 0 else right
        at = 0 if tz == 0 else 48
        strip = edge[8 * tile : 8 * tile + 8, :]
        for half, x in enumerate(PAIRS[pair]):
            k = 4 * c + x
            begin = 64 * half + at
            here = (lane >= begin) & (lane < begin + 16)
            block = jnp.where(here, roll(strip, begin - 16 * k, 1), block)
    return block


def windows_kernel(me, state, rates, low, high, left, right, windows, rates_here):
    lane = lane_index()
    my_y = me[0] // 4
    my_z = me[0] % 4
    for tz in range(4):
        for c in range(2):
            for pair in range(2):
                for tile in range(TILES):
                    block = windows_of(
                        low.at[0], state, high.at[0], left.at[0], right.at[0], tile, c, pair, tz, lane
                    )
                    for ty in range(2):
                        at = tile - 4 * ty
                        if 0 <= at < 8:
                            windows[4 * ty + tz, c, pair, 8 * at : 8 * at + 8, :] = block

    for mine in range(4):

        @pl.when(my_z == mine)
        def _():
            for c in range(2):
                for pair in range(2):
                    blocks = [
                        windows_of(
                            low.at[1], rates, high.at[1], left.at[1], right.at[1], tile, c, pair, mine, lane
                        )
                        for tile in range(TILES)
                    ]
                    for at in range(8):
                        block = jnp.where(my_y == 0, blocks[at], blocks[at + 4])
                        rates_here[c, pair, 8 * at : 8 * at + 8, :] = block


def load_state(ref):
    return [[[ref[c, p, j] for j in range(8)] for p in range(2)] for c in range(2)]


def save_state(ref, state):
    for c in range(2):
        for p in range(2):
            for j in range(8):
                ref[c, p, j] = state[c][p][j]


def neighbours(s, p, j, other):
    here = s[j]
    if p == 0:
        along_x = here + other[j]
    else:
        along_x = other[j] + roll(here, 64, 1)
    before = s[j - 1] if j > 0 else roll(s[7], 1, 0)
    after = s[j + 1] if j < 7 else roll(s[0], -1, 0)
    along_z = roll(here, 1, 1) + roll(here, -1, 1)
    return (along_x + (before + after)) + along_z


def step(state, coefs, which, length):
    a, b = state
    new_a = [[None] * 8, [None] * 8]
    new_b = [[None] * 8, [None] * 8]
    for p in range(2):
        for j in range(8):
            here_a, here_b = a[p][j], b[p][j]
            product = length * (here_a * here_b * here_b)
            near_a = neighbours(a[p], p, j, a[1 - p])
            near_b = neighbours(b[p], p, j, b[1 - p])
            keep_a = coefs[which, 0, p, j]
            gain = coefs[which, 1, p, j]
            keep_b = coefs[which, 2, p, j]
            new_a[p][j] = here_a * keep_a + (length * spread_fast) * near_a + (gain - product)
            new_b[p][j] = here_b * keep_b + (length * spread_slow) * near_b + product
    return [new_a, new_b]


def combine(op, left, right):
    return [[[op(left[c][p][j], right[c][p][j]) for j in range(8)] for p in range(2)] for c in range(2)]


def add(left, right):
    return combine(lambda l, r: l + r, left, right)


def subtract(left, right):
    return combine(lambda l, r: l - r, left, right)


def sweep_kernel(windows, rates, out, coefs, starts, terms, coarse_ends, rows):
    lane = lane_index()
    for which, length in enumerate((fine_step, coarse_step)):
        for p in range(2):
            for j in range(8):
                feed = rates[0, p, pl.ds(j, 8, stride=8), :]
                kill = rates[1, p, pl.ds(j, 8, stride=8), :]
                coefs[which, 0, p, j] = (1.0 - 6.0 * spread_fast * length) - length * feed
                coefs[which, 1, p, j] = length * feed
                coefs[which, 2, p, j] = (1.0 - 6.0 * spread_slow * length) - length * (feed + kill)

    def fine(state):
        for _ in range(FINE):
            state = step(state, coefs, 0, fine_step)
        return state

    def coarse(state):
        return step(state, coefs, 1, coarse_step)

    def first(n, carry):
        state = [
            [[windows[n, c, p, pl.ds(j, 8, stride=8), :] for j in range(8)] for p in range(2)]
            for c in range(2)
        ]
        save_state(starts.at[n], state)
        save_state(coarse_ends.at[n], coarse(state))
        end = fine(load_state(starts.at[n]))
        save_state(terms.at[n], subtract(end, load_state(coarse_ends.at[n])))
        return carry

    lax.fori_loop(0, SLICES - 1, first, 0)

    save_state(starts.at[1], add(load_state(coarse_ends.at[0]), load_state(terms.at[0])))

    def first_sweep(n, carry):
        end = coarse(load_state(starts.at[n]))
        save_state(coarse_ends.at[n], end)
        save_state(starts.at[n + 1], add(end, load_state(terms.at[n])))
        return carry

    lax.fori_loop(1, SLICES - 1, first_sweep, 0)
    save_state(coarse_ends.at[SLICES - 1], coarse(load_state(starts.at[SLICES - 1])))

    def second(n, carry):
        end = fine(load_state(starts.at[n]))
        save_state(terms.at[n], subtract(end, load_state(coarse_ends.at[n])))
        return carry

    lax.fori_loop(1, SLICES, second, 0)

    def put(n, state):
        for c in range(2):
            for j in range(8):
                outer, inner = state[c][0][j], state[c][1][j]
                low = jnp.where(lane < 32, roll(outer, -16, 1), roll(inner, 16, 1))
                high = jnp.where(lane < 96, roll(inner, -16, 1), roll(outer, 16, 1))
                rows[c, pl.ds(j, 8, stride=8), :] = jnp.where(lane < 64, low, high)
            out[n, c] = rows[c, HALO : HALO + SUB, :]

    put(0, load_state(starts.at[1]))
    state = add(load_state(coarse_ends.at[1]), load_state(terms.at[1]))
    put(1, state)
    save_state(starts.at[1], state)

    def second_sweep(n, carry):
        state = add(coarse(load_state(starts.at[n - 1])), load_state(terms.at[n]))
        put(n, state)
        save_state(starts.at[n], state)
        return carry

    lax.fori_loop(2, SLICES, second_sweep, 0)


def merge_kernel(parts, out):
    lane = lane_index()
    for c in range(2):
        for x in range(4):
            for ty in range(2):
                for r in range(4):
                    blocks = [
                        roll(parts[4 * ty + tz, c, 8 * r : 8 * r + 8, :], SUB * (tz - x), 1) for tz in range(4)
                    ]
                    low = jnp.where(lane < 32, blocks[0], blocks[1])
                    high = jnp.where(lane < 96, blocks[2], blocks[3])
                    at = SUB * ty + 8 * r
                    out[c, x, at : at + 8, :] = jnp.where(lane < 64, low, high)


def call(kernel, shapes, scratch=(), scalars=0):
    vmem = pl.BlockSpec(memory_space=pltpu.VMEM)
    smem = pl.BlockSpec(memory_space=pltpu.SMEM)

    def run(*args):
        out_shape = [jax.ShapeDtypeStruct(s, jnp.float32) for s in shapes]
        return pl.pallas_call(
            kernel,
            out_shape=out_shape,
            in_specs=[smem] * scalars + [vmem] * (len(args) - scalars),
            out_specs=[vmem] * len(shapes),
            scratch_shapes=list(scratch),
            compiler_params=pltpu.CompilerParams(vmem_limit_bytes=32 * 1024 * 1024),
        )(*args)

    return run


def shift(block, axis, distance):
    count = lax.axis_size(axis)
    return lax.ppermute(block, axis, [(i, (i + distance) % count) for i in range(count)])


def per_device(iterate, rates):
    state = iterate[0]
    both = jnp.stack([state, rates])
    low = shift(both[:, :, :, ROWS - HALO :, :], "gy", 1)
    high = shift(both[:, :, :, :HALO, :], "gy", -1)
    strip = (2, EXT, LANES)
    to_low, to_high = call(strips_kernel, [strip, strip])(state, rates, low, high)
    left = shift(to_high, "gz", 1)
    right = shift(to_low, "gz", -1)

    me = lax.axis_index("tm").astype(jnp.int32).reshape(1)
    windows, rates_here = call(
        windows_kernel, [(SLICES, 2, 2, WIN, LANES), (2, 2, WIN, LANES)], scalars=1
    )(me, state, rates, low, high, left, right)
    windows = lax.all_to_all(windows, "tm", 0, 0)

    kept = pltpu.VMEM((SLICES, 2, 2, 8, 8, LANES), jnp.float32)
    (ends,) = call(
        sweep_kernel,
        [(SLICES, 2, SUB, LANES)],
        scratch=[
            pltpu.VMEM((2, 3, 2, 8, 8, LANES), jnp.float32),
            kept,
            kept,
            kept,
            pltpu.VMEM((2, WIN, LANES), jnp.float32),
        ],
    )(windows, rates_here)
    ends = lax.all_to_all(ends, "tm", 0, 0)
    (out,) = call(merge_kernel, [(2, 4, ROWS, LANES)])(ends)
    return out[None]


def solution(mesh):
    return jax.shard_map(
        per_device,
        mesh=mesh,
        in_specs=(P("tm", None, None, "gy", "gz"), P(None, None, "gy", "gz")),
        out_specs=P("tm", None, None, "gy", "gz"),
        check_vma=False,
    )
```

time: 719 us -> 108 us (0.15)
  the two profiles are of different devices: /device:TPU:14 before, /device:TPU:3 now
where the time goes in v1:
time: 108 us
  blocking collectives  61.7 us (57%)
  starting transfers between devices  16.8 us (16%)
  waiting for transfers between devices  16.5 us (15%)
  Pallas kernels  11.8 us (11%)
    all_to_all x1, blocking collectives, per_device(): windows = lax.all_to_all(windows, 'tm', 0, 0)  47 us
    ppermute x4, starting transfers between devices, shift(): lax.ppermute(block, axis, [(i, (i + distance) % count) for i in range(cou...  16.8 us
    ppermute x4, waiting for transfers between devices, shift(): lax.ppermute(block, axis, [(i, (i + distance) % count) for i in range(cou...  16.5 us
    all_to_all x1, blocking collectives, per_device(): ends = lax.all_to_all(ends, 'tm', 0, 0)  14.7 us
    pallas_call x4, Pallas kernels, run(): pl.pallas_call(kernel, out_shape=out_shape, in_specs=[smem] * scalars + [...  11.8 us
  transfers between devices with their start and end apart: 4, of which 3 were waited for; matrix products, arithmetic and copies ran while one was open for 0% of the time, Pallas kernels for 0%

profile of v1, /device:TPU:3, one launch (start us, length us, event | category | flops | bytes accessed | tf_op | source)
XLA Modules:
  0.0 108.0 jit_solution(2565869855079935701)
XLA Ops:
  0.0 0.0 copy-start
  0.0 0.0 copy-start.1
  0.0 1.0 pad_maximum_fusion
  1.0 9.9 %collective-permute-start.1 = (f32[2,2,4,16,128]{4,3,2,1,0:T(8,128)S(1)}, f32[2,2,4,16,128]{4,3,2,1,0:T(8,128)S(1)}, u32[]{:S(2)}, u32[]{:S(2)}) collective-permute-start(f32[2,2,4,16,128]{4,3,2,1,0:T(8,128)S(1)} %get-tuple-element.13), channel_id=1, source_target_pairs={{0,120},{8,0},{16,8},{24,16},{32,24},{40,32},{48,40},{56,48},{64,5... | collective-permute-start | bytes 393224 | tf_op jit(solution)/shard_map/ppermute | solution.py:271
  10.9 1.9 %collective-permute-start = (f32[2,2,4,16,128]{4,3,2,1,0:T(8,128)S(1)}, f32[2,2,4,16,128]{4,3,2,1,0:T(8,128)S(1)}, u32[]{:S(2)}, u32[]{:S(2)}) collective-permute-start(f32[2,2,4,16,128]{4,3,2,1,0:T(8,128)S(1)} %get-tuple-element.14), channel_id=1, source_target_pairs={{0,8},{8,16},{16,24},{24,32},{32,40},{40,48},{48,56},{56,64},{64,7... | collective-permute-start | bytes 393224 | tf_op jit(solution)/shard_map/ppermute | solution.py:271
  12.9 3.6 %collective-permute-done.1.high = f32[2,2,4,16,128]{4,3,2,1,0:T(8,128)S(1)} collective-permute-done((f32[2,2,4,16,128]{4,3,2,1,0:T(8,128)S(1)}, f32[2,2,4,16,128]{4,3,2,1,0:T(8,128)S(1)}, u32[]{:S(2)}, u32[]{:S(2)}) %collective-permute-start.1) | collective-permute-done | bytes 131104 | tf_op jit(solution)/shard_map/ppermute | solution.py:271
  16.5 10.0 %collective-permute-done.low = f32[2,2,4,16,128]{4,3,2,1,0:T(8,128)S(1)} collective-permute-done((f32[2,2,4,16,128]{4,3,2,1,0:T(8,128)S(1)}, f32[2,2,4,16,128]{4,3,2,1,0:T(8,128)S(1)}, u32[]{:S(2)}, u32[]{:S(2)}) %collective-permute-start) | collective-permute-done | bytes 131104 | tf_op jit(solution)/shard_map/ppermute | solution.py:271
  26.5 0.0 copy-done
  26.5 0.0 copy-done.1
  26.5 0.4 shard_map.28
  27.0 1.9 %collective-permute-start.2 = (f32[2,96,128]{2,1,0:T(8,128)S(1)}, f32[2,96,128]{2,1,0:T(8,128)S(1)}, u32[]{:S(2)}, u32[]{:S(2)}) collective-permute-start(f32[2,96,128]{2,1,0:T(8,128)S(1)} %get-tuple-element.9), channel_id=1, source_target_pairs={{0,1},{1,2},{2,3},{3,4},{4,5},{5,6},{6,7},{7,0},{8,9},{9,10},{10,1... | collective-permute-start | bytes 294920 | tf_op jit(solution)/shard_map/ppermute | solution.py:271
  28.9 3.0 %collective-permute-start.3 = (f32[2,96,128]{2,1,0:T(8,128)S(1)}, f32[2,96,128]{2,1,0:T(8,128)S(1)}, u32[]{:S(2)}, u32[]{:S(2)}) collective-permute-start(f32[2,96,128]{2,1,0:T(8,128)S(1)} %get-tuple-element.10), channel_id=1, source_target_pairs={{0,7},{1,0},{2,1},{3,2},{4,3},{5,4},{6,5},{7,6},{8,15},{9,8},{10,9... | collective-permute-start | bytes 294920 | tf_op jit(solution)/shard_map/ppermute | solution.py:271
  32.0 0.0 collective-permute-done.2.left
  32.0 2.9 %collective-permute-done.3.right = f32[2,96,128]{2,1,0:T(8,128)S(1)} collective-permute-done((f32[2,96,128]{2,1,0:T(8,128)S(1)}, f32[2,96,128]{2,1,0:T(8,128)S(1)}, u32[]{:S(2)}, u32[]{:S(2)}) %collective-permute-start.3) | collective-permute-done | bytes 98336 | tf_op jit(solution)/shard_map/ppermute | solution.py:271
  34.8 0.9 shard_map.29
  35.7 47.0 %all_to_all.10.windows = f32[8,2,2,64,128]{4,3,2,1,0:T(8,128)S(1)} all-to-all(f32[8,2,2,64,128]{4,3,2,1,0:T(8,128)S(1)} %get-tuple-element.11), channel_id=1, replica_groups=mesh['tm'=8,'gy'=16,'gz'=8] {'tm'}, dimensions={0} | all-to-all | bytes 2097152 | tf_op jit(solution)/shard_map/all_to_all | solution.py:288
  82.7 9.6 %shard_map.30 = f32[8,2,32,128]{3,2,1,0:T(8,128)S(1)} custom-call(f32[8,2,2,64,128]{4,3,2,1,0:T(8,128)S(1)} %all_to_all.10.windows, f32[2,2,64,128]{3,2,1,0:T(8,128)S(1)} %get-tuple-element.12.rates), custom_call_target="tpu_custom_call" | custom-call | tf_op jit(solution)/shard_map/pallas_call | solution.py:257
  92.3 14.7 %all_to_all.11.parts = f32[8,2,32,128]{3,2,1,0:T(8,128)S(1)} all-to-all(f32[8,2,32,128]{3,2,1,0:T(8,128)S(1)} %shard_map.30), channel_id=1, replica_groups=mesh['tm'=8,'gy'=16,'gz'=8] {'tm'}, dimensions={0} | all-to-all | bytes 524288 | tf_op jit(solution)/shard_map/all_to_all | solution.py:302
  107.0 1.0 shard_map.31
Async XLA Ops:
  0.0 26.5 %copy-start = (f32[1,2,4,64,128]{4,3,2,1,0:T(8,128)S(1)}, f32[1,2,4,64,128]{4,3,2,1,0:T(8,128)}, u32[]{:S(2)}) copy-start(f32[1,2,4,64,128]{4,3,2,1,0:T(8,128)} %param.2) | copy-start | bytes 786436
  0.0 26.5 %copy-start.1 = (f32[2,4,64,128]{3,2,1,0:T(8,128)S(1)}, f32[2,4,64,128]{3,2,1,0:T(8,128)}, u32[]{:S(2)}) copy-start(f32[2,4,64,128]{3,2,1,0:T(8,128)} %rates.3) | copy-start | bytes 786436
  1.0 15.5 %collective-permute-start.1 = (f32[2,2,4,16,128]{4,3,2,1,0:T(8,128)S(1)}, f32[2,2,4,16,128]{4,3,2,1,0:T(8,128)S(1)}, u32[]{:S(2)}, u32[]{:S(2)}) collective-permute-start(f32[2,2,4,16,128]{4,3,2,1,0:T(8,128)S(1)} %get-tuple-element.13), channel_id=1, source_target_pairs={{0,120},{8,0},{16,8},{24,16},{32,24},{40,32},{48,40},{56,48},{64,5... | collective-permute-start | bytes 393224 | tf_op jit(solution)/shard_map/ppermute | solution.py:271
  10.9 15.6 %collective-permute-start = (f32[2,2,4,16,128]{4,3,2,1,0:T(8,128)S(1)}, f32[2,2,4,16,128]{4,3,2,1,0:T(8,128)S(1)}, u32[]{:S(2)}, u32[]{:S(2)}) collective-permute-start(f32[2,2,4,16,128]{4,3,2,1,0:T(8,128)S(1)} %get-tuple-element.14), channel_id=1, source_target_pairs={{0,8},{8,16},{16,24},{24,32},{32,40},{40,48},{48,56},{56,64},{64,7... | collective-permute-start | bytes 393224 | tf_op jit(solution)/shard_map/ppermute | solution.py:271
  27.0 5.0 %collective-permute-start.2 = (f32[2,96,128]{2,1,0:T(8,128)S(1)}, f32[2,96,128]{2,1,0:T(8,128)S(1)}, u32[]{:S(2)}, u32[]{:S(2)}) collective-permute-start(f32[2,96,128]{2,1,0:T(8,128)S(1)} %get-tuple-element.9), channel_id=1, source_target_pairs={{0,1},{1,2},{2,3},{3,4},{4,5},{5,6},{6,7},{7,0},{8,9},{9,10},{10,1... | collective-permute-start | bytes 294920 | tf_op jit(solution)/shard_map/ppermute | solution.py:271
  28.9 5.9 %collective-permute-start.3 = (f32[2,96,128]{2,1,0:T(8,128)S(1)}, f32[2,96,128]{2,1,0:T(8,128)S(1)}, u32[]{:S(2)}, u32[]{:S(2)}) collective-permute-start(f32[2,96,128]{2,1,0:T(8,128)S(1)} %get-tuple-element.10), channel_id=1, source_target_pairs={{0,7},{1,0},{2,1},{3,2},{4,3},{5,4},{6,5},{7,6},{8,15},{9,8},{10,9... | collective-permute-start | bytes 294920 | tf_op jit(solution)/shard_map/ppermute | solution.py:271

commit v2 on v1

--- a/solution.py
+++ b/solution.py
@@ -32,40 +32,62 @@
     return block if shift == 0 else pltpu.roll(block, shift, axis)
 
 
-def ext_tile(low, own, high, index):
+def pick(even, if_even, if_odd):
+    return jnp.where(even, if_even, if_odd)
+
+
+def ext_tile(one, two, own, even, index):
     if index < 2:
-        return low[8 * index : 8 * index + 8, :]
+        rows = slice(8 * index, 8 * index + 8)
+        return pick(even, two[rows, :], one[rows, :])
     if index < 10:
         return own[8 * (index - 2) : 8 * (index - 2) + 8, :]
-    return high[8 * (index - 10) : 8 * (index - 10) + 8, :]
-
-
-def strips_kernel(state, rates, low, high, to_low, to_high):
+    rows = slice(8 * (index - 10), 8 * (index - 10) + 8)
+    return pick(even, one[rows, :], two[rows, :])
+
+
+def edges_kernel(me, state, rates, two, one):
+    even = me[1] % 2 == 0
+    for which, source in enumerate((state, rates)):
+        for c in range(2):
+            for x in range(4):
+                for r in range(2):
+                    first = source[c, x, 8 * r : 8 * r + 8, :]
+                    last = source[c, x, ROWS - HALO + 8 * r : ROWS - HALO + 8 * r + 8, :]
+                    one[which, c, x, 8 * r : 8 * r + 8, :] = pick(even, last, first)
+                    two[which, c, x, 8 * r : 8 * r + 8, :] = pick(even, first, last)
+
+
+def strips_kernel(me, state, rates, y_two, y_one, two, one):
     lane = lane_index()
+    even_y = me[1] % 2 == 0
+    even_z = me[2] % 2 == 0
     for which, source in enumerate((state, rates)):
         for tile in range(TILES):
             first = jnp.zeros((8, LANES), jnp.float32)
             last = jnp.zeros((8, LANES), jnp.float32)
             for k in range(8):
                 c, x = k // 4, k % 4
-                rows = ext_tile(low.at[which, c, x], source.at[c, x], high.at[which, c, x], tile)
+                rows = ext_tile(y_one.at[which, c, x], y_two.at[which, c, x], source.at[c, x], even_y, tile)
                 here = (lane >= 16 * k) & (lane < 16 * k + 16)
                 first = jnp.where(here, roll(rows, 16 * k, 1), first)
                 last = jnp.where(here, roll(rows, 16 * k + 16, 1), last)
-            to_low[which, 8 * tile : 8 * tile + 8, :] = first
-            to_high[which, 8 * tile : 8 * tile + 8, :] = last
-
-
-def windows_of(low, own, high, left, right, tile, c, pair, tz, lane):
+            one[which, 8 * tile : 8 * tile + 8, :] = pick(even_z, last, first)
+            two[which, 8 * tile : 8 * tile + 8, :] = pick(even_z, first, last)
+
+
+def windows_of(own, y_one, y_two, z_one, z_two, even_y, even_z, tile, c, pair, tz, lane):
     parts = []
     for half, x in enumerate(PAIRS[pair]):
-        rows = ext_tile(low.at[c, x], own.at[c, x], high.at[c, x], tile)
+        rows = ext_tile(y_one.at[c, x], y_two.at[c, x], own.at[c, x], even_y, tile)
         parts.append(roll(rows, 64 * half - (SUB * tz - HALO), 1))
     block = jnp.where(lane < 64, parts[0], parts[1])
     if tz in (0, 3):
-        edge = left if tz == 0 else right
-        at = 0 if tz == 0 else 48
-        strip = edge[8 * tile : 8 * tile + 8, :]
+        left = tz == 0
+        at = 0 if left else 48
+        rows = slice(8 * tile, 8 * tile + 8)
+        near, far = z_one[rows, :], z_two[rows, :]
+        strip = pick(even_z, far, near) if left else pick(even_z, near, far)
         for half, x in enumerate(PAIRS[pair]):
             k = 4 * c + x
             begin = 64 * half + at
@@ -74,17 +96,21 @@
     return block
 
 
-def windows_kernel(me, state, rates, low, high, left, right, windows, rates_here):
+def windows_kernel(me, state, rates, y_two, y_one, z_two, z_one, windows, rates_here):
     lane = lane_index()
+    even_y = me[1] % 2 == 0
+    even_z = me[2] % 2 == 0
+
+    def halos(which):
+        return y_one.at[which], y_two.at[which], z_one.at[which], z_two.at[which], even_y, even_z
+
     my_y = me[0] // 4
     my_z = me[0] % 4
     for tz in range(4):
         for c in range(2):
             for pair in range(2):
                 for tile in range(TILES):
-                    block = windows_of(
-                        low.at[0], state, high.at[0], left.at[0], right.at[0], tile, c, pair, tz, lane
-                    )
+                    block = windows_of(state, *halos(0), tile, c, pair, tz, lane)
                     for ty in range(2):
                         at = tile - 4 * ty
                         if 0 <= at < 8:
@@ -97,10 +123,7 @@
             for c in range(2):
                 for pair in range(2):
                     blocks = [
-                        windows_of(
-                            low.at[1], rates, high.at[1], left.at[1], right.at[1], tile, c, pair, mine, lane
-                        )
-                        for tile in range(TILES)
+                        windows_of(rates, *halos(1), tile, c, pair, mine, lane) for tile in range(TILES)
                     ]
                     for at in range(8):
                         block = jnp.where(my_y == 0, blocks[at], blocks[at + 4])
@@ -266,25 +289,29 @@
     return run
 
 
-def shift(block, axis, distance):
+def swap(block, axis, begin):
     count = lax.axis_size(axis)
-    return lax.ppermute(block, axis, [(i, (i + distance) % count) for i in range(count)])
+    route = []
+    for i in range(begin, begin + count, 2):
+        a, b = i % count, (i + 1) % count
+        route += [(a, b), (b, a)]
+    return lax.ppermute(block, axis, route)
 
 
 def per_device(iterate, rates):
     state = iterate[0]
-    both = jnp.stack([state, rates])
-    low = shift(both[:, :, :, ROWS - HALO :, :], "gy", 1)
-    high = shift(both[:, :, :, :HALO, :], "gy", -1)
+    me = jnp.stack([lax.axis_index(axis).astype(jnp.int32) for axis in ("tm", "gy", "gz")])
+    strip = (2, 2, 4, HALO, LANES)
+    two, one = call(edges_kernel, [strip, strip], scalars=1)(me, state, rates)
+    y_one = swap(one, "gy", 0)
+    y_two = swap(two, "gy", 1)
     strip = (2, EXT, LANES)
-    to_low, to_high = call(strips_kernel, [strip, strip])(state, rates, low, high)
-    left = shift(to_high, "gz", 1)
-    right = shift(to_low, "gz", -1)
-
-    me = lax.axis_index("tm").astype(jnp.int32).reshape(1)
+    two, one = call(strips_kernel, [strip, strip], scalars=1)(me, state, rates, y_two, y_one)
+    z_one = swap(one, "gz", 0)
+    z_two = swap(two, "gz", 1)
     windows, rates_here = call(
         windows_kernel, [(SLICES, 2, 2, WIN, LANES), (2, 2, WIN, LANES)], scalars=1
-    )(me, state, rates, low, high, left, right)
+    )(me, state, rates, y_two, y_one, z_two, z_one)
     windows = lax.all_to_all(windows, "tm", 0, 0)
 
     kept = pltpu.VMEM((SLICES, 2, 2, 8, 8, LANES), jnp.float32)

time: 108 us -> 101 us (0.935)
  the two profiles are of different devices: /device:TPU:3 before, /device:TPU:14 now
where the time goes in v2:
time: 101 us; the launch traced here: 100 us
  blocking collectives  60.6 us (60%)
  starting transfers between devices  18.1 us (18%)
  Pallas kernels  13.5 us (13%)
  waiting for transfers between devices  5.85 us (6%)
  local copies, waits for them, and re-layouts  1.9 us (2%)
    all_to_all x1, blocking collectives, per_device(): windows = lax.all_to_all(windows, 'tm', 0, 0)  45.8 us
    ppermute x4, starting transfers between devices, swap(): return lax.ppermute(block, axis, route)  18.1 us
    all_to_all x1, blocking collectives, per_device(): ends = lax.all_to_all(ends, 'tm', 0, 0)  14.8 us
    pallas_call x5, Pallas kernels, run(): pl.pallas_call(kernel, out_shape=out_shape, in_specs=[smem] * scalars + [...  13.5 us
    ppermute x4, waiting for transfers between devices, swap(): return lax.ppermute(block, axis, route)  5.85 us
  transfers between devices with their start and end apart: 4, of which 3 were waited for; matrix products, arithmetic and copies ran while one was open for 0% of the time, Pallas kernels for 0%

profile of v2, /device:TPU:14, one launch (start us, length us, event | category | flops | bytes accessed | tf_op | source)
XLA Modules:
  0.0 100.1 jit_solution(4537918419418374493)
XLA Ops:
  0.0 0.1 pad_add_fusion.me
  0.1 0.0 copy-start
  0.1 0.9 copy-done
  1.0 0.0 copy-start.1
  1.0 0.9 copy-done.1
  2.0 0.6 shard_map.28
  2.6 8.8 %collective-permute-start = (f32[2,2,4,16,128]{4,3,2,1,0:T(8,128)S(1)}, f32[2,2,4,16,128]{4,3,2,1,0:T(8,128)S(1)}, u32[]{:S(2)}, u32[]{:S(2)}) collective-permute-start(f32[2,2,4,16,128]{4,3,2,1,0:T(8,128)S(1)} %get-tuple-element.11), channel_id=1, source_target_pairs={{8,16},{16,8},{24,32},{32,24},{40,48},{48,40},{56,64},{64,56},{72,... | collective-permute-start | bytes 393224 | tf_op jit(solution)/shard_map/ppermute | solution.py:298
  11.3 1.9 %collective-permute-start.1 = (f32[2,2,4,16,128]{4,3,2,1,0:T(8,128)S(1)}, f32[2,2,4,16,128]{4,3,2,1,0:T(8,128)S(1)}, u32[]{:S(2)}, u32[]{:S(2)}) collective-permute-start(f32[2,2,4,16,128]{4,3,2,1,0:T(8,128)S(1)} %get-tuple-element.12), channel_id=1, source_target_pairs={{0,8},{8,0},{16,24},{24,16},{32,40},{40,32},{48,56},{56,48},{64,72... | collective-permute-start | bytes 393224 | tf_op jit(solution)/shard_map/ppermute | solution.py:298
  13.2 4.0 %collective-permute-done.y_two = f32[2,2,4,16,128]{4,3,2,1,0:T(8,128)S(1)} collective-permute-done((f32[2,2,4,16,128]{4,3,2,1,0:T(8,128)S(1)}, f32[2,2,4,16,128]{4,3,2,1,0:T(8,128)S(1)}, u32[]{:S(2)}, u32[]{:S(2)}) %collective-permute-start) | collective-permute-done | bytes 131104 | tf_op jit(solution)/shard_map/ppermute | solution.py:298
  17.3 0.9 collective-permute-done.1.y_one
  18.2 1.0 shard_map.29
  19.2 1.9 %collective-permute-start.2 = (f32[2,96,128]{2,1,0:T(8,128)S(1)}, f32[2,96,128]{2,1,0:T(8,128)S(1)}, u32[]{:S(2)}, u32[]{:S(2)}) collective-permute-start(f32[2,96,128]{2,1,0:T(8,128)S(1)} %get-tuple-element.13), channel_id=1, source_target_pairs={{1,2},{2,1},{3,4},{4,3},{5,6},{6,5},{7,0},{0,7},{9,10},{10,9},{11,... | collective-permute-start | bytes 294920 | tf_op jit(solution)/shard_map/ppermute | solution.py:298
  21.1 5.5 %collective-permute-start.3 = (f32[2,96,128]{2,1,0:T(8,128)S(1)}, f32[2,96,128]{2,1,0:T(8,128)S(1)}, u32[]{:S(2)}, u32[]{:S(2)}) collective-permute-start(f32[2,96,128]{2,1,0:T(8,128)S(1)} %get-tuple-element.14), channel_id=1, source_target_pairs={{0,1},{1,0},{2,3},{3,2},{4,5},{5,4},{6,7},{7,6},{8,9},{9,8},{10,11... | collective-permute-start | bytes 294920 | tf_op jit(solution)/shard_map/ppermute | solution.py:298
  26.6 0.0 collective-permute-done.2.z_two
  26.6 0.9 collective-permute-done.3.z_one
  27.5 1.4 %shard_map.30 = (f32[8,2,2,64,128]{4,3,2,1,0:T(8,128)S(1)}, f32[2,2,64,128]{3,2,1,0:T(8,128)S(1)}) custom-call(s32[3]{0:T(128)S(1)} %pad_add_fusion.me, f32[2,4,64,128]{3,2,1,0:T(8,128)S(1)} %bitcast.7, f32[2,4,64,128]{3,2,1,0:T(8,128)S(1)} %copy-done.1, f32[2,2,4,16,128]{4,3,2,1,0:T(8,128)S(1)} %collective-permute-done.y_two, ...), custom_call_target="tpu_custom_call" | custom-call | tf_op jit(solution)/shard_map/pallas_call | solution.py:280
  28.9 45.8 %all_to_all.10.windows = f32[8,2,2,64,128]{4,3,2,1,0:T(8,128)S(1)} all-to-all(f32[8,2,2,64,128]{4,3,2,1,0:T(8,128)S(1)} %get-tuple-element.15), channel_id=1, replica_groups=mesh['tm'=8,'gy'=16,'gz'=8] {'tm'}, dimensions={0} | all-to-all | bytes 2097152 | tf_op jit(solution)/shard_map/all_to_all | solution.py:315
  74.8 9.6 %shard_map.31 = f32[8,2,32,128]{3,2,1,0:T(8,128)S(1)} custom-call(f32[8,2,2,64,128]{4,3,2,1,0:T(8,128)S(1)} %all_to_all.10.windows, f32[2,2,64,128]{3,2,1,0:T(8,128)S(1)} %get-tuple-element.16.rates), custom_call_target="tpu_custom_call" | custom-call | tf_op jit(solution)/shard_map/pallas_call | solution.py:280
  84.3 14.8 %all_to_all.11.parts = f32[8,2,32,128]{3,2,1,0:T(8,128)S(1)} all-to-all(f32[8,2,32,128]{3,2,1,0:T(8,128)S(1)} %shard_map.31), channel_id=1, replica_groups=mesh['tm'=8,'gy'=16,'gz'=8] {'tm'}, dimensions={0} | all-to-all | bytes 524288 | tf_op jit(solution)/shard_map/all_to_all | solution.py:329
  99.1 1.0 shard_map.32
Async XLA Ops:
  0.1 1.0 copy-start
  1.0 0.9 copy-start.1
  2.6 14.7 %collective-permute-start = (f32[2,2,4,16,128]{4,3,2,1,0:T(8,128)S(1)}, f32[2,2,4,16,128]{4,3,2,1,0:T(8,128)S(1)}, u32[]{:S(2)}, u32[]{:S(2)}) collective-permute-start(f32[2,2,4,16,128]{4,3,2,1,0:T(8,128)S(1)} %get-tuple-element.11), channel_id=1, source_target_pairs={{8,16},{16,8},{24,32},{32,24},{40,48},{48,40},{56,64},{64,56},{72,... | collective-permute-start | bytes 393224 | tf_op jit(solution)/shard_map/ppermute | solution.py:298
  11.3 6.9 %collective-permute-start.1 = (f32[2,2,4,16,128]{4,3,2,1,0:T(8,128)S(1)}, f32[2,2,4,16,128]{4,3,2,1,0:T(8,128)S(1)}, u32[]{:S(2)}, u32[]{:S(2)}) collective-permute-start(f32[2,2,4,16,128]{4,3,2,1,0:T(8,128)S(1)} %get-tuple-element.12), channel_id=1, source_target_pairs={{0,8},{8,0},{16,24},{24,16},{32,40},{40,32},{48,56},{56,48},{64,72... | collective-permute-start | bytes 393224 | tf_op jit(solution)/shard_map/ppermute | solution.py:298
  19.2 7.4 %collective-permute-start.2 = (f32[2,96,128]{2,1,0:T(8,128)S(1)}, f32[2,96,128]{2,1,0:T(8,128)S(1)}, u32[]{:S(2)}, u32[]{:S(2)}) collective-permute-start(f32[2,96,128]{2,1,0:T(8,128)S(1)} %get-tuple-element.13), channel_id=1, source_target_pairs={{1,2},{2,1},{3,4},{4,3},{5,6},{6,5},{7,0},{0,7},{9,10},{10,9},{11,... | collective-permute-start | bytes 294920 | tf_op jit(solution)/shard_map/ppermute | solution.py:298
  21.1 6.4 %collective-permute-start.3 = (f32[2,96,128]{2,1,0:T(8,128)S(1)}, f32[2,96,128]{2,1,0:T(8,128)S(1)}, u32[]{:S(2)}, u32[]{:S(2)}) collective-permute-start(f32[2,96,128]{2,1,0:T(8,128)S(1)} %get-tuple-element.14), channel_id=1, source_target_pairs={{0,1},{1,0},{2,3},{3,2},{4,5},{5,4},{6,7},{7,6},{8,9},{9,8},{10,11... | collective-permute-start | bytes 294920 | tf_op jit(solution)/shard_map/ppermute | solution.py:298

commit v3 on v2

v3 whole, which is shorter than its diff:
```python
import jax
import jax.numpy as jnp
from jax import lax
from jax.experimental import pallas as pl
from jax.experimental.pallas import tpu as pltpu
from jax.sharding import PartitionSpec as P

FINE = 4
SLICES = 8
HALO = 16
SUB = 32
MARGIN = 12
WIN = SUB + 2 * MARGIN
ROWS = 64
LANES = 128
EXT = ROWS + 2 * HALO
TILES = EXT // 8
BLOCK = WIN // 8

spread_fast = 0.2
spread_slow = 0.1
fine_step = 0.125
coarse_step = 0.5

PAIRS = ((0, 3), (1, 2))


def lane_index():
    return lax.broadcasted_iota(jnp.int32, (8, LANES), 1)


def roll(block, shift, axis):
    shift = shift % block.shape[axis]
    return block if shift == 0 else pltpu.roll(block, shift, axis)


def pick(even, if_even, if_odd):
    return jnp.where(even, if_even, if_odd)


def ext_tile(one, two, own, even, index):
    if index < 2:
        rows = slice(8 * index, 8 * index + 8)
        return pick(even, two[rows, :], one[rows, :])
    if index < 10:
        return own[8 * (index - 2) : 8 * (index - 2) + 8, :]
    rows = slice(8 * (index - 10), 8 * (index - 10) + 8)
    return pick(even, one[rows, :], two[rows, :])


def edges_kernel(me, state, rates, two, one, sems):
    odd = me[1] % 2
    copies = []
    for which, source in enumerate((state, rates)):
        for k, (target, at) in enumerate(((two, odd), (one, 1 - odd))):
            begin = pl.multiple_of(at * (ROWS - HALO), HALO)
            copies.append(
                pltpu.make_async_copy(
                    source.at[:, :, pl.ds(begin, HALO), :], target.at[which], sems.at[2 * which + k]
                )
            )
    for copy in copies:
        copy.start()
    for copy in copies:
        copy.wait()


def strips_kernel(me, state, rates, y_two, y_one, two, one):
    lane = lane_index()
    even_y = me[1] % 2 == 0
    even_z = me[2] % 2 == 0
    for which, source in enumerate((state, rates)):
        for tile in range(TILES):
            first = jnp.zeros((8, LANES), jnp.float32)
            last = jnp.zeros((8, LANES), jnp.float32)
            for k in range(8):
                c, x = k // 4, k % 4
                rows = ext_tile(y_one.at[which, c, x], y_two.at[which, c, x], source.at[c, x], even_y, tile)
                here = (lane >= 16 * k) & (lane < 16 * k + 16)
                first = jnp.where(here, roll(rows, 16 * k, 1), first)
                last = jnp.where(here, roll(rows, 16 * k + 16, 1), last)
            one[which, 8 * tile : 8 * tile + 8, :] = pick(even_z, last, first)
            two[which, 8 * tile : 8 * tile + 8, :] = pick(even_z, first, last)


def lay_out(own, y_one, y_two, z_one, z_two, even_y, even_z, wide, lane):
    for tile in range(TILES):
        rows = slice(8 * tile, 8 * tile + 8)
        near, far = z_one[rows, :], z_two[rows, :]
        left = pick(even_z, far, near)
        right = pick(even_z, near, far)
        for k in range(8):
            c, x = k // 4, k % 4
            here = ext_tile(y_one.at[c, x], y_two.at[c, x], own.at[c, x], even_y, tile)
            wide[0, c, x, rows, :] = jnp.where(lane < 16, roll(left, -16 * k, 1), roll(here, 16, 1))
            wide[1, c, x, rows, :] = jnp.where(lane >= 112, roll(right, 112 - 16 * k, 1), roll(here, -16, 1))


def window_tile(wide, c, pair, ty, tz, r, lane):
    block, moved = ((0, 0), (1, 0), (0, 1), (1, 1))[tz]
    begin = SUB * ty + HALO - MARGIN + 8 * r
    parts = [wide[block, c, x, begin : begin + 8, :] for x in PAIRS[pair]]
    parts[1 - moved] = roll(parts[1 - moved], 64, 1)
    return jnp.where(lane < 64, parts[0], parts[1])


def tile_step(source, target, coefs_of, length):
    for x in range(4):
        for j in range(TILES):
            keep_a, gain, keep_b = coefs_of(x, j)
            here = [source[c, x, j] for c in range(2)]
            near = []
            for c in range(2):
                below = source[c, max(x - 1, 0), j]
                above = source[c, min(x + 1, 3), j]
                before = source[c, x, j - 1] if j > 0 else roll(source[c, x, TILES - 1], 1, 0)
                after = source[c, x, j + 1] if j < TILES - 1 else roll(source[c, x, 0], -1, 0)
                along_z = roll(here[c], 1, 1) + roll(here[c], -1, 1)
                near.append(((below + above) + (before + after)) + along_z)
            a, b = here
            product = length * (a * b * b)
            target[0, x, j] = a * keep_a + (length * spread_fast) * near[0] + (gain - product)
            target[1, x, j] = b * keep_b + (length * spread_slow) * near[1] + product


def coefs_from(feed, kill, length):
    gain = length * feed
    keep_a = (1.0 - 6.0 * spread_fast * length) - gain
    keep_b = (1.0 - 6.0 * spread_slow * length) - length * (feed + kill)
    return keep_a, gain, keep_b


def first_kernel(
    me, state, rates, y_two, y_one, z_two, z_one, windows, rates_here, wide, wide_rates, coefs, even, odd, slow
):
    lane = lane_index()
    even_y = me[1] % 2 == 0
    even_z = me[2] % 2 == 0
    for which, source, target in ((0, state, wide), (1, rates, wide_rates)):
        lay_out(
            source,
            y_one.at[which],
            y_two.at[which],
            z_one.at[which],
            z_two.at[which],
            even_y,
            even_z,
            target,
            lane,
        )

    def rows_of(j):
        return pl.ds(j, 8, stride=TILES)

    def block(w, carry):
        for x in range(4):
            for j in range(TILES):
                feed = wide_rates[w, 0, x, rows_of(j), :]
                kill = wide_rates[w, 1, x, rows_of(j), :]
                for i, value in enumerate(coefs_from(feed, kill, fine_step)):
                    coefs[i, x, j] = value
                for c in range(2):
                    even[c, x, j] = wide[w, c, x, rows_of(j), :]

        def coarse_coefs(x, j):
            feed = wide_rates[w, 0, x, rows_of(j), :]
            kill = wide_rates[w, 1, x, rows_of(j), :]
            return coefs_from(feed, kill, coarse_step)

        def fine_coefs(x, j):
            return [coefs[i, x, j] for i in range(3)]

        tile_step(even, slow, coarse_coefs, coarse_step)

        def two_steps(_, inner):
            tile_step(even, odd, fine_coefs, fine_step)
            tile_step(odd, even, fine_coefs, fine_step)
            return inner

        lax.fori_loop(0, FINE // 2, two_steps, 0)
        leading = me[0] == 0
        for c in range(2):
            for x in range(4):
                for j in range(TILES):
                    coarse_end = slow[c, x, j]
                    difference = even[c, x, j] - coarse_end
                    wide[w, c, x, rows_of(j), :] = jnp.where(leading, coarse_end + difference, difference)
        return carry

    lax.fori_loop(0, 2, block, 0)

    my_y = me[0] // 4
    my_z = me[0] % 4
    for c in range(2):
        for pair in range(2):
            for r in range(BLOCK):
                for tz in range(4):
                    for ty in range(2):
                        windows[4 * ty + tz, c, pair, 8 * r : 8 * r + 8, :] = window_tile(
                            wide, c, pair, ty, tz, r, lane
                        )

    for tz in range(4):

        @pl.when(my_z == tz)
        def _():
            for c in range(2):
                for pair in range(2):
                    for r in range(BLOCK):
                        tiles = [window_tile(wide_rates, c, pair, ty, tz, r, lane) for ty in range(2)]
                        rates_here[c, pair, 8 * r : 8 * r + 8, :] = jnp.where(my_y == 0, tiles[0], tiles[1])


def load_state(ref):
    return [[[ref[c, p, j] for j in range(BLOCK)] for p in range(2)] for c in range(2)]


def save_state(ref, state):
    for c in range(2):
        for p in range(2):
            for j in range(BLOCK):
                ref[c, p, j] = state[c][p][j]


def neighbours(s, p, j, other):
    here = s[j]
    if p == 0:
        along_x = here + other[j]
    else:
        along_x = other[j] + roll(here, 64, 1)
    before = s[j - 1] if j > 0 else roll(s[BLOCK - 1], 1, 0)
    after = s[j + 1] if j < BLOCK - 1 else roll(s[0], -1, 0)
    along_z = roll(here, 1, 1) + roll(here, -1, 1)
    return (along_x + (before + after)) + along_z


def step(state, coefs, which, length):
    a, b = state
    new_a = [[None] * BLOCK, [None] * BLOCK]
    new_b = [[None] * BLOCK, [None] * BLOCK]
    for p in range(2):
        for j in range(BLOCK):
            here_a, here_b = a[p][j], b[p][j]
            product = length * (here_a * here_b * here_b)
            near_a = neighbours(a[p], p, j, a[1 - p])
            near_b = neighbours(b[p], p, j, b[1 - p])
            keep_a = coefs[which, 0, p, j]
            gain = coefs[which, 1, p, j]
            keep_b = coefs[which, 2, p, j]
            new_a[p][j] = here_a * keep_a + (length * spread_fast) * near_a + (gain - product)
            new_b[p][j] = here_b * keep_b + (length * spread_slow) * near_b + product
    return [new_a, new_b]


def combine(op, left, right):
    return [[[op(left[c][p][j], right[c][p][j]) for j in range(BLOCK)] for p in range(2)] for c in range(2)]


def add(left, right):
    return combine(lambda l, r: l + r, left, right)


def subtract(left, right):
    return combine(lambda l, r: l - r, left, right)


def sweep_kernel(windows, rates, out, coefs, starts, terms, coarse_ends, rows):
    lane = lane_index()

    def rows_of(j):
        return pl.ds(j, 8, stride=BLOCK)

    for p in range(2):
        for j in range(BLOCK):
            feed = rates[0, p, rows_of(j), :]
            kill = rates[1, p, rows_of(j), :]
            for which, length in enumerate((fine_step, coarse_step)):
                for i, value in enumerate(coefs_from(feed, kill, length)):
                    coefs[which, i, p, j] = value

    def fine(state):
        for _ in range(FINE):
            state = step(state, coefs, 0, fine_step)
        return state

    def coarse(state):
        return step(state, coefs, 1, coarse_step)

    def received(n):
        return [
            [[windows[n, c, p, rows_of(j), :] for j in range(BLOCK)] for p in range(2)] for c in range(2)
        ]

    save_state(starts.at[1], received(0))

    def first_sweep(n, carry):
        end = coarse(load_state(starts.at[n]))
        save_state(coarse_ends.at[n], end)
        save_state(starts.at[n + 1], add(end, received(n)))
        return carry

    lax.fori_loop(1, SLICES - 1, first_sweep, 0)
    save_state(coarse_ends.at[SLICES - 1], coarse(load_state(starts.at[SLICES - 1])))

    def second(n, carry):
        end = fine(load_state(starts.at[n]))
        save_state(terms.at[n], subtract(end, load_state(coarse_ends.at[n])))
        return carry

    lax.fori_loop(1, SLICES, second, 0)

    def put(n, state):
        for c in range(2):
            for j in range(BLOCK):
                outer, inner = state[c][0][j], state[c][1][j]
                low = jnp.where(lane < 32, roll(outer, -16, 1), roll(inner, 16, 1))
                high = jnp.where(lane < 96, roll(inner, -16, 1), roll(outer, 16, 1))
                rows[c, rows_of(j), :] = jnp.where(lane < 64, low, high)
            out[n, c] = rows[c, MARGIN : MARGIN + SUB, :]

    put(0, load_state(starts.at[1]))
    state = add(load_state(coarse_ends.at[1]), load_state(terms.at[1]))
    put(1, state)
    save_state(starts.at[1], state)

    def second_sweep(n, carry):
        state = add(coarse(load_state(starts.at[n - 1])), load_state(terms.at[n]))
        put(n, state)
        save_state(starts.at[n], state)
        return carry

    lax.fori_loop(2, SLICES, second_sweep, 0)


def merge_kernel(parts, out):
    lane = lane_index()
    for c in range(2):
        for x in range(4):
            for ty in range(2):
                for r in range(4):
                    blocks = [
                        roll(parts[4 * ty + tz, c, 8 * r : 8 * r + 8, :], SUB * (tz - x), 1) for tz in range(4)
                    ]
                    low = jnp.where(lane < 32, blocks[0], blocks[1])
                    high = jnp.where(lane < 96, blocks[2], blocks[3])
                    at = SUB * ty + 8 * r
                    out[c, x, at : at + 8, :] = jnp.where(lane < 64, low, high)


def call(kernel, shapes, scratch=(), scalars=0, inputs=pltpu.VMEM):
    vmem = pl.BlockSpec(memory_space=pltpu.VMEM)
    given = pl.BlockSpec(memory_space=inputs)
    smem = pl.BlockSpec(memory_space=pltpu.SMEM)

    def run(*args):
        out_shape = [jax.ShapeDtypeStruct(s, jnp.float32) for s in shapes]
        return pl.pallas_call(
            kernel,
            out_shape=out_shape,
            in_specs=[smem] * scalars + [given] * (len(args) - scalars),
            out_specs=[vmem] * len(shapes),
            scratch_shapes=list(scratch),
            compiler_params=pltpu.CompilerParams(vmem_limit_bytes=32 * 1024 * 1024),
        )(*args)

    return run


def swap(block, axis, begin):
    count = lax.axis_size(axis)
    route = []
    for i in range(begin, begin + count, 2):
        a, b = i % count, (i + 1) % count
        route += [(a, b), (b, a)]
    return lax.ppermute(block, axis, route)


def per_device(iterate, rates):
    state = iterate[0]
    me = jnp.stack([lax.axis_index(axis).astype(jnp.int32) for axis in ("tm", "gy", "gz")])
    strip = (2, 2, 4, HALO, LANES)
    two, one = call(
        edges_kernel, [strip, strip], scratch=[pltpu.SemaphoreType.DMA((4,))], scalars=1, inputs=pltpu.HBM
    )(me, state, rates)
    y_one = swap(one, "gy", 0)
    y_two = swap(two, "gy", 1)
    strip = (2, EXT, LANES)
    two, one = call(strips_kernel, [strip, strip], scalars=1)(me, state, rates, y_two, y_one)
    z_one = swap(one, "gz", 0)
    z_two = swap(two, "gz", 1)
    tile_state = pltpu.VMEM((2, 4, TILES, 8, LANES), jnp.float32)
    windows, rates_here = call(
        first_kernel,
        [(SLICES, 2, 2, WIN, LANES), (2, 2, WIN, LANES)],
        scratch=[
            pltpu.VMEM((2, 2, 4, EXT, LANES), jnp.float32),
            pltpu.VMEM((2, 2, 4, EXT, LANES), jnp.float32),
            pltpu.VMEM((3, 4, TILES, 8, LANES), jnp.float32),
            tile_state,
            tile_state,
            tile_state,
        ],
        scalars=1,
    )(me, state, rates, y_two, y_one, z_two, z_one)
    windows = lax.all_to_all(windows, "tm", 0, 0)

    kept = pltpu.VMEM((SLICES, 2, 2, BLOCK, 8, LANES), jnp.float32)
    (ends,) = call(
        sweep_kernel,
        [(SLICES, 2, SUB, LANES)],
        scratch=[
            pltpu.VMEM((2, 3, 2, BLOCK, 8, LANES), jnp.float32),
            kept,
            kept,
            kept,
            pltpu.VMEM((2, WIN, LANES), jnp.float32),
        ],
    )(windows, rates_here)
    ends = lax.all_to_all(ends, "tm", 0, 0)
    (out,) = call(merge_kernel, [(2, 4, ROWS, LANES)])(ends)
    return out[None]


def solution(mesh):
    return jax.shard_map(
        per_device,
        mesh=mesh,
        in_specs=(P("tm", None, None, "gy", "gz"), P(None, None, "gy", "gz")),
        out_specs=P("tm", None, None, "gy", "gz"),
        check_vma=False,
    )
```

time: 101 us -> 97.1 us (0.961)
  blocking collectives: 60.6 us -> 57.8 us
    all_to_all x1, blocking collectives: 45.8 us -> 43 us  [per_device(): windows = lax.all_to_all(windows, 'tm', 0, 0)]
where the time goes in v3:
time: 97.1 us; the launch traced here: 96.5 us
  blocking collectives  57.8 us (60%)
  starting transfers between devices  18.1 us (19%)
  Pallas kernels  12.8 us (13%)
  waiting for transfers between devices  5.85 us (6%)
  local copies, waits for them, and re-layouts  1.9 us (2%)
    all_to_all x1, blocking collectives, per_device(): windows = lax.all_to_all(windows, 'tm', 0, 0)  43 us
    ppermute x4, starting transfers between devices, swap(): return lax.ppermute(block, axis, route)  18.1 us
    all_to_all x1, blocking collectives, per_device(): ends = lax.all_to_all(ends, 'tm', 0, 0)  14.8 us
    pallas_call x5, Pallas kernels, run(): pl.pallas_call(kernel, out_shape=out_shape, in_specs=[smem] * scalars + [...  12.8 us
    ppermute x4, waiting for transfers between devices, swap(): return lax.ppermute(block, axis, route)  5.85 us
  transfers between devices with their start and end apart: 4, of which 3 were waited for; matrix products, arithmetic and copies ran while one was open for 0% of the time, Pallas kernels for 0%

profile of v3, /device:TPU:14, one launch (start us, length us, event | category | flops | bytes accessed | tf_op | source)
XLA Modules:
  0.0 96.5 jit_solution(9102682074676900716)
XLA Ops:
  0.0 0.1 pad_add_fusion.me
  0.1 0.0 copy-start
  0.1 0.9 copy-done
  1.0 0.0 copy-start.1
  1.0 0.9 copy-done.1
  2.0 0.6 shard_map.28
  2.6 8.8 %collective-permute-start = (f32[2,2,4,16,128]{4,3,2,1,0:T(8,128)S(1)}, f32[2,2,4,16,128]{4,3,2,1,0:T(8,128)S(1)}, u32[]{:S(2)}, u32[]{:S(2)}) collective-permute-start(f32[2,2,4,16,128]{4,3,2,1,0:T(8,128)S(1)} %get-tuple-element.11), channel_id=1, source_target_pairs={{8,16},{16,8},{24,32},{32,24},{40,48},{48,40},{56,64},{64,56},{72,... | collective-permute-start | bytes 393224 | tf_op jit(solution)/shard_map/ppermute | solution.py:375
  11.4 1.9 %collective-permute-start.1 = (f32[2,2,4,16,128]{4,3,2,1,0:T(8,128)S(1)}, f32[2,2,4,16,128]{4,3,2,1,0:T(8,128)S(1)}, u32[]{:S(2)}, u32[]{:S(2)}) collective-permute-start(f32[2,2,4,16,128]{4,3,2,1,0:T(8,128)S(1)} %get-tuple-element.12), channel_id=1, source_target_pairs={{0,8},{8,0},{16,24},{24,16},{32,40},{40,32},{48,56},{56,48},{64,72... | collective-permute-start | bytes 393224 | tf_op jit(solution)/shard_map/ppermute | solution.py:375
  13.3 4.0 %collective-permute-done.y_two = f32[2,2,4,16,128]{4,3,2,1,0:T(8,128)S(1)} collective-permute-done((f32[2,2,4,16,128]{4,3,2,1,0:T(8,128)S(1)}, f32[2,2,4,16,128]{4,3,2,1,0:T(8,128)S(1)}, u32[]{:S(2)}, u32[]{:S(2)}) %collective-permute-start) | collective-permute-done | bytes 131104 | tf_op jit(solution)/shard_map/ppermute | solution.py:375
  17.3 0.9 collective-permute-done.1.y_one
  18.3 1.0 %shard_map.29 = (f32[2,96,128]{2,1,0:T(8,128)S(1)}, f32[2,96,128]{2,1,0:T(8,128)S(1)}) custom-call(s32[3]{0:T(128)S(1)} %pad_add_fusion.me, f32[2,4,64,128]{3,2,1,0:T(8,128)S(1)} %bitcast.6, f32[2,4,64,128]{3,2,1,0:T(8,128)S(1)} %copy-done.1, f32[2,2,4,16,128]{4,3,2,1,0:T(8,128)S(1)} %collective-permute-done.y_two, ...), custom_call_target="tpu_custom_call" | custom-call | tf_op jit(solution)/shard_map/pallas_call | solution.py:357
  19.2 1.9 %collective-permute-start.2 = (f32[2,96,128]{2,1,0:T(8,128)S(1)}, f32[2,96,128]{2,1,0:T(8,128)S(1)}, u32[]{:S(2)}, u32[]{:S(2)}) collective-permute-start(f32[2,96,128]{2,1,0:T(8,128)S(1)} %get-tuple-element.13), channel_id=1, source_target_pairs={{1,2},{2,1},{3,4},{4,3},{5,6},{6,5},{7,0},{0,7},{9,10},{10,9},{11,... | collective-permute-start | bytes 294920 | tf_op jit(solution)/shard_map/ppermute | solution.py:375
  21.2 5.5 %collective-permute-start.3 = (f32[2,96,128]{2,1,0:T(8,128)S(1)}, f32[2,96,128]{2,1,0:T(8,128)S(1)}, u32[]{:S(2)}, u32[]{:S(2)}) collective-permute-start(f32[2,96,128]{2,1,0:T(8,128)S(1)} %get-tuple-element.14), channel_id=1, source_target_pairs={{0,1},{1,0},{2,3},{3,2},{4,5},{5,4},{6,7},{7,6},{8,9},{9,8},{10,11... | collective-permute-start | bytes 294920 | tf_op jit(solution)/shard_map/ppermute | solution.py:375
  26.6 0.0 collective-permute-done.2.z_two
  26.6 0.9 collective-permute-done.3.z_one
  27.5 4.7 %shard_map.30 = (f32[8,2,2,56,128]{4,3,2,1,0:T(8,128)S(1)}, f32[2,2,56,128]{3,2,1,0:T(8,128)S(1)}) custom-call(s32[3]{0:T(128)S(1)} %pad_add_fusion.me, f32[2,4,64,128]{3,2,1,0:T(8,128)S(1)} %bitcast.7, f32[2,4,64,128]{3,2,1,0:T(8,128)S(1)} %copy-done.1, f32[2,2,4,16,128]{4,3,2,1,0:T(8,128)S(1)} %collective-permute-done.y_two, ...), custom_call_target="tpu_custom_call" | custom-call | tf_op jit(solution)/shard_map/pallas_call | solution.py:357
  32.2 43.0 %all_to_all.10.windows = f32[8,2,2,56,128]{4,3,2,1,0:T(8,128)S(1)} all-to-all(f32[8,2,2,56,128]{4,3,2,1,0:T(8,128)S(1)} %get-tuple-element.15), channel_id=1, replica_groups=mesh['tm'=8,'gy'=16,'gz'=8] {'tm'}, dimensions={0} | all-to-all | bytes 1835008 | tf_op jit(solution)/shard_map/all_to_all | solution.py:405
  75.2 5.6 %shard_map.31 = f32[8,2,32,128]{3,2,1,0:T(8,128)S(1)} custom-call(f32[8,2,2,56,128]{4,3,2,1,0:T(8,128)S(1)} %all_to_all.10.windows, f32[2,2,56,128]{3,2,1,0:T(8,128)S(1)} %get-tuple-element.16.rates), custom_call_target="tpu_custom_call" | custom-call | tf_op jit(solution)/shard_map/pallas_call | solution.py:357
  80.8 14.8 %all_to_all.11.parts = f32[8,2,32,128]{3,2,1,0:T(8,128)S(1)} all-to-all(f32[8,2,32,128]{3,2,1,0:T(8,128)S(1)} %shard_map.31), channel_id=1, replica_groups=mesh['tm'=8,'gy'=16,'gz'=8] {'tm'}, dimensions={0} | all-to-all | bytes 524288 | tf_op jit(solution)/shard_map/all_to_all | solution.py:419
  95.6 1.0 %shard_map.32 = f32[2,4,64,128]{3,2,1,0:T(8,128)} custom-call(f32[8,2,32,128]{3,2,1,0:T(8,128)S(1)} %all_to_all.11.parts), custom_call_target="tpu_custom_call" | custom-call | tf_op jit(solution)/shard_map/pallas_call | solution.py:357
Async XLA Ops:
  0.1 1.0 copy-start
  1.0 0.9 copy-start.1
  2.6 14.7 %collective-permute-start = (f32[2,2,4,16,128]{4,3,2,1,0:T(8,128)S(1)}, f32[2,2,4,16,128]{4,3,2,1,0:T(8,128)S(1)}, u32[]{:S(2)}, u32[]{:S(2)}) collective-permute-start(f32[2,2,4,16,128]{4,3,2,1,0:T(8,128)S(1)} %get-tuple-element.11), channel_id=1, source_target_pairs={{8,16},{16,8},{24,32},{32,24},{40,48},{48,40},{56,64},{64,56},{72,... | collective-permute-start | bytes 393224 | tf_op jit(solution)/shard_map/ppermute | solution.py:375
  11.4 6.9 %collective-permute-start.1 = (f32[2,2,4,16,128]{4,3,2,1,0:T(8,128)S(1)}, f32[2,2,4,16,128]{4,3,2,1,0:T(8,128)S(1)}, u32[]{:S(2)}, u32[]{:S(2)}) collective-permute-start(f32[2,2,4,16,128]{4,3,2,1,0:T(8,128)S(1)} %get-tuple-element.12), channel_id=1, source_target_pairs={{0,8},{8,0},{16,24},{24,16},{32,40},{40,32},{48,56},{56,48},{64,72... | collective-permute-start | bytes 393224 | tf_op jit(solution)/shard_map/ppermute | solution.py:375
  19.2 7.4 %collective-permute-start.2 = (f32[2,96,128]{2,1,0:T(8,128)S(1)}, f32[2,96,128]{2,1,0:T(8,128)S(1)}, u32[]{:S(2)}, u32[]{:S(2)}) collective-permute-start(f32[2,96,128]{2,1,0:T(8,128)S(1)} %get-tuple-element.13), channel_id=1, source_target_pairs={{1,2},{2,1},{3,4},{4,3},{5,6},{6,5},{7,0},{0,7},{9,10},{10,9},{11,... | collective-permute-start | bytes 294920 | tf_op jit(solution)/shard_map/ppermute | solution.py:375
  21.2 6.4 %collective-permute-start.3 = (f32[2,96,128]{2,1,0:T(8,128)S(1)}, f32[2,96,128]{2,1,0:T(8,128)S(1)}, u32[]{:S(2)}, u32[]{:S(2)}) collective-permute-start(f32[2,96,128]{2,1,0:T(8,128)S(1)} %get-tuple-element.14), channel_id=1, source_target_pairs={{0,1},{1,0},{2,3},{3,2},{4,5},{5,4},{6,7},{7,6},{8,9},{9,8},{10,11... | collective-permute-start | bytes 294920 | tf_op jit(solution)/shard_map/ppermute | solution.py:375

commit v4 on v3

--- a/solution.py
+++ b/solution.py
@@ -3,15 +3,17 @@
 from jax import lax
 from jax.experimental import pallas as pl
 from jax.experimental.pallas import tpu as pltpu
+from jax.sharding import Mesh
 from jax.sharding import PartitionSpec as P
 
 FINE = 4
-SLICES = 8
+GROUP = 4
 HALO = 16
 SUB = 32
+ROWS = 64
 MARGIN = 12
-WIN = SUB + 2 * MARGIN
-ROWS = 64
+WIN = ROWS + 2 * MARGIN
+SENT = 80
 LANES = 128
 EXT = ROWS + 2 * HALO
 TILES = EXT // 8
@@ -46,23 +48,6 @@
         return own[8 * (index - 2) : 8 * (index - 2) + 8, :]
     rows = slice(8 * (index - 10), 8 * (index - 10) + 8)
     return pick(even, one[rows, :], two[rows, :])
-
-
-def edges_kernel(me, state, rates, two, one, sems):
-    odd = me[1] % 2
-    copies = []
-    for which, source in enumerate((state, rates)):
-        for k, (target, at) in enumerate(((two, odd), (one, 1 - odd))):
-            begin = pl.multiple_of(at * (ROWS - HALO), HALO)
-            copies.append(
-                pltpu.make_async_copy(
-                    source.at[:, :, pl.ds(begin, HALO), :], target.at[which], sems.at[2 * which + k]
-                )
-            )
-    for copy in copies:
-        copy.start()
-    for copy in copies:
-        copy.wait()
 
 
 def strips_kernel(me, state, rates, y_two, y_one, two, one):
@@ -96,9 +81,9 @@
             wide[1, c, x, rows, :] = jnp.where(lane >= 112, roll(right, 112 - 16 * k, 1), roll(here, -16, 1))
 
 
-def window_tile(wide, c, pair, ty, tz, r, lane):
-    block, moved = ((0, 0), (1, 0), (0, 1), (1, 1))[tz]
-    begin = SUB * ty + HALO - MARGIN + 8 * r
+def window_tile(wide, c, pair, sub, r, lane):
+    block, moved = ((0, 0), (1, 0), (0, 1), (1, 1))[sub]
+    begin = HALO - MARGIN + 8 * r
     parts = [wide[block, c, x, begin : begin + 8, :] for x in PAIRS[pair]]
     parts[1 - moved] = roll(parts[1 - moved], 64, 1)
     return jnp.where(lane < 64, parts[0], parts[1])
@@ -189,26 +174,22 @@
 
     lax.fori_loop(0, 2, block, 0)
 
-    my_y = me[0] // 4
-    my_z = me[0] % 4
-    for c in range(2):
-        for pair in range(2):
-            for r in range(BLOCK):
-                for tz in range(4):
-                    for ty in range(2):
-                        windows[4 * ty + tz, c, pair, 8 * r : 8 * r + 8, :] = window_tile(
-                            wide, c, pair, ty, tz, r, lane
-                        )
-
-    for tz in range(4):
-
-        @pl.when(my_z == tz)
+    early = me[0] < GROUP
+    for sub in range(GROUP):
+        worker = jnp.where(early, sub, GROUP - 1 - sub)
+        for c in range(2):
+            for pair in range(2):
+                for r in range(BLOCK):
+                    windows[worker, c, pair, 8 * r : 8 * r + 8, :] = window_tile(wide, c, pair, sub, r, lane)
+
+        @pl.when(worker == me[0] % GROUP)
         def _():
             for c in range(2):
                 for pair in range(2):
                     for r in range(BLOCK):
-                        tiles = [window_tile(wide_rates, c, pair, ty, tz, r, lane) for ty in range(2)]
-                        rates_here[c, pair, 8 * r : 8 * r + 8, :] = jnp.where(my_y == 0, tiles[0], tiles[1])
+                        rates_here[c, pair, 8 * r : 8 * r + 8, :] = window_tile(
+                            wide_rates, c, pair, sub, r, lane
+                        )
 
 
 def load_state(ref):
@@ -264,12 +245,15 @@
     return combine(lambda l, r: l - r, left, right)
 
 
-def sweep_kernel(windows, rates, out, coefs, starts, terms, coarse_ends, rows):
-    lane = lane_index()
-
-    def rows_of(j):
-        return pl.ds(j, 8, stride=BLOCK)
-
+def rows_of(j):
+    return pl.ds(j, 8, stride=BLOCK)
+
+
+def load_window(ref):
+    return [[[ref[c, p, rows_of(j), :] for j in range(BLOCK)] for p in range(2)] for c in range(2)]
+
+
+def save_coefs(coefs, rates):
     for p in range(2):
         for j in range(BLOCK):
             feed = rates[0, p, rows_of(j), :]
@@ -278,73 +262,120 @@
                 for i, value in enumerate(coefs_from(feed, kill, length)):
                     coefs[which, i, p, j] = value
 
-    def fine(state):
-        for _ in range(FINE):
-            state = step(state, coefs, 0, fine_step)
-        return state
-
-    def coarse(state):
-        return step(state, coefs, 1, coarse_step)
-
-    def received(n):
-        return [
-            [[windows[n, c, p, rows_of(j), :] for j in range(BLOCK)] for p in range(2)] for c in range(2)
-        ]
-
-    save_state(starts.at[1], received(0))
-
-    def first_sweep(n, carry):
-        end = coarse(load_state(starts.at[n]))
-        save_state(coarse_ends.at[n], end)
-        save_state(starts.at[n + 1], add(end, received(n)))
-        return carry
-
-    lax.fori_loop(1, SLICES - 1, first_sweep, 0)
-    save_state(coarse_ends.at[SLICES - 1], coarse(load_state(starts.at[SLICES - 1])))
-
-    def second(n, carry):
-        end = fine(load_state(starts.at[n]))
-        save_state(terms.at[n], subtract(end, load_state(coarse_ends.at[n])))
-        return carry
-
-    lax.fori_loop(1, SLICES, second, 0)
-
-    def put(n, state):
-        for c in range(2):
-            for j in range(BLOCK):
-                outer, inner = state[c][0][j], state[c][1][j]
-                low = jnp.where(lane < 32, roll(outer, -16, 1), roll(inner, 16, 1))
-                high = jnp.where(lane < 96, roll(inner, -16, 1), roll(outer, 16, 1))
-                rows[c, rows_of(j), :] = jnp.where(lane < 64, low, high)
-            out[n, c] = rows[c, MARGIN : MARGIN + SUB, :]
-
-    put(0, load_state(starts.at[1]))
-    state = add(load_state(coarse_ends.at[1]), load_state(terms.at[1]))
-    put(1, state)
-    save_state(starts.at[1], state)
-
-    def second_sweep(n, carry):
-        state = add(coarse(load_state(starts.at[n - 1])), load_state(terms.at[n]))
-        put(n, state)
-        save_state(starts.at[n], state)
-        return carry
-
-    lax.fori_loop(2, SLICES, second_sweep, 0)
-
-
-def merge_kernel(parts, out):
+
+def fine(state, coefs):
+    for _ in range(FINE):
+        state = step(state, coefs, 0, fine_step)
+    return state
+
+
+def coarse(state, coefs):
+    return step(state, coefs, 1, coarse_step)
+
+
+def put(out, rows, m, state):
     lane = lane_index()
     for c in range(2):
-        for x in range(4):
-            for ty in range(2):
-                for r in range(4):
-                    blocks = [
-                        roll(parts[4 * ty + tz, c, 8 * r : 8 * r + 8, :], SUB * (tz - x), 1) for tz in range(4)
-                    ]
-                    low = jnp.where(lane < 32, blocks[0], blocks[1])
-                    high = jnp.where(lane < 96, blocks[2], blocks[3])
-                    at = SUB * ty + 8 * r
-                    out[c, x, at : at + 8, :] = jnp.where(lane < 64, low, high)
+        for j in range(BLOCK):
+            outer, inner = state[c][0][j], state[c][1][j]
+            low = jnp.where(lane < 32, roll(outer, -16, 1), roll(inner, 16, 1))
+            high = jnp.where(lane < 96, roll(inner, -16, 1), roll(outer, 16, 1))
+            rows[c, rows_of(j), :] = jnp.where(lane < 64, low, high)
+        out[m, c] = rows[c, MARGIN : MARGIN + ROWS, :]
+
+
+def sweep(first, windows, coefs, starts, coarse_ends):
+    def turn(m, carry):
+        end = coarse(load_state(starts.at[m]), coefs)
+        save_state(coarse_ends.at[m], end)
+        save_state(starts.at[m + 1], add(end, load_window(windows.at[m])))
+        return carry
+
+    lax.fori_loop(first, GROUP, turn, 0)
+
+
+def second_terms(first, coefs, starts, coarse_ends):
+    def turn(m, carry):
+        end = fine(load_state(starts.at[m]), coefs)
+        save_state(starts.at[m], subtract(end, load_state(coarse_ends.at[m])))
+        return carry
+
+    lax.fori_loop(first, GROUP, turn, 0)
+
+
+def second_sweep(first, coefs, current, terms, rows, out):
+    def turn(m, carry):
+        state = add(coarse(load_state(current), coefs), load_state(terms.at[m]))
+        put(out, rows, m, state)
+        save_state(current, state)
+        return carry
+
+    lax.fori_loop(first, GROUP, turn, 0)
+
+
+def early_kernel(me, windows, rates, ends, sent, coefs, starts, coarse_ends, current, rows, kept):
+    @pl.when(me[0] < GROUP)
+    def _():
+        save_coefs(coefs, rates)
+        save_state(starts.at[1], load_window(windows.at[0]))
+        sweep(1, windows, coefs, starts, coarse_ends)
+        put(ends, rows, 0, load_state(starts.at[1]))
+        pack(sent, 0, kept, load_state(starts.at[GROUP]))
+        second_terms(1, coefs, starts, coarse_ends)
+        state = add(load_state(coarse_ends.at[1]), load_state(starts.at[1]))
+        put(ends, rows, 1, state)
+        save_state(current, state)
+        second_sweep(2, coefs, current, starts, rows, ends)
+        pack(sent, 1, kept, load_state(current))
+
+
+def pack(sent, which, kept, state):
+    for c in range(2):
+        for p in range(2):
+            for j in range(BLOCK):
+                kept[c, p, rows_of(j), :] = state[c][p][j]
+            begin = MARGIN + (ROWS - SENT) // 2
+            sent[which, c, p] = kept[c, p, begin : begin + SENT, :]
+
+
+def unpack(sent, which, kept, target):
+    for c in range(2):
+        for p in range(2):
+            begin = MARGIN + (ROWS - SENT) // 2
+            kept[c, p, begin : begin + SENT, :] = sent[which, c, p]
+    save_state(target, load_window(kept))
+
+
+def late_kernel(me, windows, rates, received, early_ends, ends, coefs, starts, coarse_ends, current, rows, kept):
+    @pl.when(me[0] < GROUP)
+    def _():
+        for m in range(GROUP):
+            ends[m] = early_ends[m]
+
+    @pl.when(me[0] >= GROUP)
+    def _():
+        save_coefs(coefs, rates)
+        kept[...] = jnp.zeros_like(kept)
+        unpack(received, 0, kept, starts.at[0])
+        unpack(received, 1, kept, current)
+        sweep(0, windows, coefs, starts, coarse_ends)
+        second_terms(0, coefs, starts, coarse_ends)
+        second_sweep(0, coefs, current, starts, rows, ends)
+
+
+def merge_kernel(me, parts, out):
+    lane = lane_index()
+    early = me[0] < GROUP
+    workers = [jnp.where(early, sub, GROUP - 1 - sub) for sub in range(GROUP)]
+    for c in range(2):
+        for r in range(ROWS // 8):
+            rows = slice(8 * r, 8 * r + 8)
+            strips = [parts[workers[sub], c, rows, :] for sub in range(GROUP)]
+            for x in range(4):
+                blocks = [roll(strips[sub], SUB * (sub - x), 1) for sub in range(GROUP)]
+                low = jnp.where(lane < 32, blocks[0], blocks[1])
+                high = jnp.where(lane < 96, blocks[2], blocks[3])
+                out[c, x, rows, :] = jnp.where(lane < 64, low, high)
 
 
 def call(kernel, shapes, scratch=(), scalars=0, inputs=pltpu.VMEM):
@@ -375,23 +406,28 @@
     return lax.ppermute(block, axis, route)
 
 
+def edge(blocks, begin):
+    return jnp.stack([lax.dynamic_slice_in_dim(block, begin, HALO, 2) for block in blocks])
+
+
 def per_device(iterate, rates):
     state = iterate[0]
-    me = jnp.stack([lax.axis_index(axis).astype(jnp.int32) for axis in ("tm", "gy", "gz")])
-    strip = (2, 2, 4, HALO, LANES)
-    two, one = call(
-        edges_kernel, [strip, strip], scratch=[pltpu.SemaphoreType.DMA((4,))], scalars=1, inputs=pltpu.HBM
-    )(me, state, rates)
+    slice_index = GROUP * lax.axis_index("th") + lax.axis_index("tl")
+    gy, gz = lax.axis_index("gy"), lax.axis_index("gz")
+    me = jnp.stack([slice_index, gy, gz]).astype(jnp.int32)
+    odd = gy % 2
+    two = edge((state, rates), odd * (ROWS - HALO))
+    one = edge((state, rates), (1 - odd) * (ROWS - HALO))
+    y_two = swap(two, "gy", 1)
     y_one = swap(one, "gy", 0)
-    y_two = swap(two, "gy", 1)
     strip = (2, EXT, LANES)
     two, one = call(strips_kernel, [strip, strip], scalars=1)(me, state, rates, y_two, y_one)
+    z_two = swap(two, "gz", 1)
     z_one = swap(one, "gz", 0)
-    z_two = swap(two, "gz", 1)
     tile_state = pltpu.VMEM((2, 4, TILES, 8, LANES), jnp.float32)
     windows, rates_here = call(
         first_kernel,
-        [(SLICES, 2, 2, WIN, LANES), (2, 2, WIN, LANES)],
+        [(GROUP, 2, 2, WIN, LANES), (2, 2, WIN, LANES)],
         scratch=[
             pltpu.VMEM((2, 2, 4, EXT, LANES), jnp.float32),
             pltpu.VMEM((2, 2, 4, EXT, LANES), jnp.float32),
@@ -402,30 +438,37 @@
         ],
         scalars=1,
     )(me, state, rates, y_two, y_one, z_two, z_one)
-    windows = lax.all_to_all(windows, "tm", 0, 0)
-
-    kept = pltpu.VMEM((SLICES, 2, 2, BLOCK, 8, LANES), jnp.float32)
-    (ends,) = call(
-        sweep_kernel,
-        [(SLICES, 2, SUB, LANES)],
-        scratch=[
-            pltpu.VMEM((2, 3, 2, BLOCK, 8, LANES), jnp.float32),
-            kept,
-            kept,
-            kept,
-            pltpu.VMEM((2, WIN, LANES), jnp.float32),
-        ],
-    )(windows, rates_here)
-    ends = lax.all_to_all(ends, "tm", 0, 0)
-    (out,) = call(merge_kernel, [(2, 4, ROWS, LANES)])(ends)
+    windows = lax.all_to_all(windows, "tl", 0, 0)
+
+    scratch = [
+        pltpu.VMEM((2, 3, 2, BLOCK, 8, LANES), jnp.float32),
+        pltpu.VMEM((GROUP + 1, 2, 2, BLOCK, 8, LANES), jnp.float32),
+        pltpu.VMEM((GROUP, 2, 2, BLOCK, 8, LANES), jnp.float32),
+        pltpu.VMEM((2, 2, BLOCK, 8, LANES), jnp.float32),
+        pltpu.VMEM((2, WIN, LANES), jnp.float32),
+        pltpu.VMEM((2, 2, WIN, LANES), jnp.float32),
+    ]
+    ends_shape = (GROUP, 2, ROWS, LANES)
+    early_ends, sent = call(
+        early_kernel, [ends_shape, (2, 2, 2, SENT, LANES)], scratch=scratch, scalars=1
+    )(me, windows, rates_here)
+    last = 2 * GROUP - 1
+    received = lax.ppermute(sent, ("th", "tl"), [(t, last - t) for t in range(GROUP)])
+    (ends,) = call(late_kernel, [ends_shape], scratch=scratch, scalars=1)(
+        me, windows, rates_here, received, early_ends
+    )
+    ends = lax.all_to_all(ends, "tl", 0, 0)
+    (out,) = call(merge_kernel, [(2, 4, ROWS, LANES)], scalars=1)(me, ends)
     return out[None]
 
 
 def solution(mesh):
+    shape = mesh.devices.shape
+    split = Mesh(mesh.devices.reshape(shape[0] // GROUP, GROUP, *shape[1:]), ("th", "tl", "gy", "gz"))
     return jax.shard_map(
         per_device,
-        mesh=mesh,
-        in_specs=(P("tm", None, None, "gy", "gz"), P(None, None, "gy", "gz")),
-        out_specs=P("tm", None, None, "gy", "gz"),
+        mesh=split,
+        in_specs=(P(("th", "tl"), None, None, "gy", "gz"), P(None, None, "gy", "gz")),
+        out_specs=P(("th", "tl"), None, None, "gy", "gz"),
         check_vma=False,
     )

time: 97.1 us -> 98.3 us (1.012)
  blocking collectives: 57.8 us -> 40.5 us
  waiting for transfers between devices: 5.85 us -> 19.6 us
  starting transfers between devices: 18.1 us -> 25 us
  Pallas kernels: 12.8 us -> 11.6 us
    all_to_all x2, blocking collectives: 57.8 us -> 40.5 us  [the longest x1 29.1 us: per_device(): windows = lax.all_to_all(windows, 'tl', 0, 0)]
    ppermute x0 -> x1, waiting for transfers between devices: none -> 13.9 us  [per_device(): lax.ppermute(sent, ('th', 'tl'), [(t, last - t) for t in range(GROUP)])]
    ppermute x0 -> x1, starting transfers between devices: none -> 6.83 us  [per_device(): lax.ppermute(sent, ('th', 'tl'), [(t, last - t) for t in range(GROUP)])]
    unnamed x4, local copies, waits for them, and re-layouts: 1.9 us -> 0.09 us
    pallas_call x5, Pallas kernels: 12.8 us -> 11.6 us  [run(): pl.pallas_call(kernel, out_shape=out_shape, in_specs=[smem] * scalars + [...]
  transfers between devices with their start and end apart: 4 -> 5, of which waited for: 3 -> 4; matrix products, arithmetic and copies ran while one was open for 0% -> 0% of each run, Pallas kernels for 0% -> 0%
where the time goes in v4:
time: 98.3 us; the launch traced here: 98 us
  blocking collectives  40.5 us (41%)
  starting transfers between devices  25 us (25%)
  waiting for transfers between devices  19.6 us (20%)
  Pallas kernels  11.6 us (12%)
  local copies, waits for them, and re-layouts  1.03 us (1%)
    all_to_all x1, blocking collectives, per_device(): windows = lax.all_to_all(windows, 'tl', 0, 0)  29.1 us
    ppermute x4, starting transfers between devices, swap(): return lax.ppermute(block, axis, route)  18.2 us
    ppermute x1, waiting for transfers between devices, per_device(): lax.ppermute(sent, ('th', 'tl'), [(t, last - t) for t in range(GROUP)])  13.9 us
    pallas_call x5, Pallas kernels, run(): pl.pallas_call(kernel, out_shape=out_shape, in_specs=[smem] * scalars + [...  11.6 us
    all_to_all x1, blocking collectives, per_device(): ends = lax.all_to_all(ends, 'tl', 0, 0)  11.4 us
    ppermute x1, starting transfers between devices, per_device(): lax.ppermute(sent, ('th', 'tl'), [(t, last - t) for t in range(GROUP)])  6.83 us
    ppermute x4, waiting for transfers between devices, swap(): return lax.ppermute(block, axis, route)  5.76 us
  transfers between devices with their start and end apart: 5, of which 4 were waited for; matrix products, arithmetic and copies ran while one was open for 0% of the time, Pallas kernels for 0%

profile of v4, /device:TPU:14, one launch (start us, length us, event | category | flops | bytes accessed | tf_op | source)
XLA Modules:
  0.0 98.0 jit_solution(8677002760950976522)
XLA Ops:
  0.0 0.0 copy-start.1
  0.0 0.9 constant_dynamic-slice_fusion
  0.9 0.1 copy-done.1
  1.0 0.0 copy-start
  1.1 8.9 %collective-permute-start = (f32[2,2,4,16,128]{4,3,2,1,0:T(8,128)S(1)}, f32[2,2,4,16,128]{4,3,2,1,0:T(8,128)S(1)}, u32[]{:S(2)}, u32[]{:S(2)}) collective-permute-start(f32[2,2,4,16,128]{4,3,2,1,0:T(8,128)S(1)} %pad_maximum_fusion), channel_id=1, source_target_pairs={{8,16},{16,8},{24,32},{32,24},{40,48},{48,40},{56,64},{64,56},{72,... | collective-permute-start | bytes 393224 | tf_op jit(solution)/shard_map/ppermute | solution.py:406
  10.0 1.9 %collective-permute-start.1 = (f32[2,2,4,16,128]{4,3,2,1,0:T(8,128)S(1)}, f32[2,2,4,16,128]{4,3,2,1,0:T(8,128)S(1)}, u32[]{:S(2)}, u32[]{:S(2)}) collective-permute-start(f32[2,2,4,16,128]{4,3,2,1,0:T(8,128)S(1)} %pad_maximum_fusion.1), channel_id=1, source_target_pairs={{0,8},{8,0},{16,24},{24,16},{32,40},{40,32},{48,56},{56,48},{64,72... | collective-permute-start | bytes 393224 | tf_op jit(solution)/shard_map/ppermute | solution.py:406
  11.9 0.1 pad_add_fusion.me
  12.0 3.9 %collective-permute-done.y_two = f32[2,2,4,16,128]{4,3,2,1,0:T(8,128)S(1)} collective-permute-done((f32[2,2,4,16,128]{4,3,2,1,0:T(8,128)S(1)}, f32[2,2,4,16,128]{4,3,2,1,0:T(8,128)S(1)}, u32[]{:S(2)}, u32[]{:S(2)}) %collective-permute-start) | collective-permute-done | bytes 131104 | tf_op jit(solution)/shard_map/ppermute | solution.py:406
  15.9 0.9 collective-permute-done.1.y_one
  16.8 0.0 copy-done
  16.8 1.0 shard_map.28
  17.8 1.9 %collective-permute-start.2 = (f32[2,96,128]{2,1,0:T(8,128)S(1)}, f32[2,96,128]{2,1,0:T(8,128)S(1)}, u32[]{:S(2)}, u32[]{:S(2)}) collective-permute-start(f32[2,96,128]{2,1,0:T(8,128)S(1)} %get-tuple-element.11), channel_id=1, source_target_pairs={{1,2},{2,1},{3,4},{4,3},{5,6},{6,5},{7,0},{0,7},{9,10},{10,9},{11,... | collective-permute-start | bytes 294920 | tf_op jit(solution)/shard_map/ppermute | solution.py:406
  19.7 5.4 %collective-permute-start.3 = (f32[2,96,128]{2,1,0:T(8,128)S(1)}, f32[2,96,128]{2,1,0:T(8,128)S(1)}, u32[]{:S(2)}, u32[]{:S(2)}) collective-permute-start(f32[2,96,128]{2,1,0:T(8,128)S(1)} %get-tuple-element.12), channel_id=1, source_target_pairs={{0,1},{1,0},{2,3},{3,2},{4,5},{5,4},{6,7},{7,6},{8,9},{9,8},{10,11... | collective-permute-start | bytes 294920 | tf_op jit(solution)/shard_map/ppermute | solution.py:406
  25.2 0.0 collective-permute-done.2.z_two
  25.2 0.9 collective-permute-done.3.z_one
  26.1 4.8 %shard_map.29 = (f32[4,2,2,88,128]{4,3,2,1,0:T(8,128)S(1)}, f32[2,2,88,128]{3,2,1,0:T(8,128)S(1)}) custom-call(s32[3]{0:T(128)S(1)} %pad_add_fusion.me, f32[2,4,64,128]{3,2,1,0:T(8,128)S(1)} %bitcast.10, f32[2,4,64,128]{3,2,1,0:T(8,128)S(1)} %copy-done.1, f32[2,2,4,16,128]{4,3,2,1,0:T(8,128)S(1)} %collective-permute-done.y_two, ...), custom_call_target="tpu_custom_call" | custom-call | tf_op jit(solution)/shard_map/pallas_call | solution.py:388
  30.9 29.1 %all_to_all.10.windows = f32[4,2,2,88,128]{4,3,2,1,0:T(8,128)S(1)} all-to-all(f32[4,2,2,88,128]{4,3,2,1,0:T(8,128)S(1)} %get-tuple-element.13), channel_id=1, replica_groups=mesh['th'=2,'tl'=4,'gy'=16,'gz'=8] {'tl'}, dimensions={0} | all-to-all | bytes 1441792 | tf_op jit(solution)/shard_map/all_to_all | solution.py:441
  60.0 3.8 %shard_map.30 = (f32[4,2,64,128]{3,2,1,0:T(8,128)S(1)}, f32[2,2,2,80,128]{4,3,2,1,0:T(8,128)S(1)}) custom-call(s32[3]{0:T(128)S(1)} %pad_add_fusion.me, f32[4,2,2,88,128]{4,3,2,1,0:T(8,128)S(1)} %all_to_all.10.windows, f32[2,2,88,128]{3,2,1,0:T(8,128)S(1)} %get-tuple-element.14.rates), custom_call_target="tpu_custom_call" | custom-call | tf_op jit(solution)/shard_map/pallas_call | solution.py:388
  63.8 6.8 %collective-permute-start.4 = (f32[2,2,2,80,128]{4,3,2,1,0:T(8,128)S(1)}, f32[2,2,2,80,128]{4,3,2,1,0:T(8,128)S(1)}, u32[]{:S(2)}, u32[]{:S(2)}) collective-permute-start(f32[2,2,2,80,128]{4,3,2,1,0:T(8,128)S(1)} %get-tuple-element.15), channel_id=1, source_target_pairs={{0,896},{128,768},{256,640},{384,512},{1,897},{129,769},{257,641},... | collective-permute-start | bytes 983048 | tf_op jit(solution)/shard_map/ppermute | solution.py:456
  70.6 13.9 %collective-permute-done.4.received = f32[2,2,2,80,128]{4,3,2,1,0:T(8,128)S(1)} collective-permute-done((f32[2,2,2,80,128]{4,3,2,1,0:T(8,128)S(1)}, f32[2,2,2,80,128]{4,3,2,1,0:T(8,128)S(1)}, u32[]{:S(2)}, u32[]{:S(2)}) %collective-permute-start.4) | collective-permute-done | bytes 327712 | tf_op jit(solution)/shard_map/ppermute | solution.py:456
  84.5 0.6 shard_map.31
  85.1 11.4 %all_to_all.11.parts = f32[4,2,64,128]{3,2,1,0:T(8,128)S(1)} all-to-all(f32[4,2,64,128]{3,2,1,0:T(8,128)S(1)} %shard_map.31), channel_id=1, replica_groups=mesh['th'=2,'tl'=4,'gy'=16,'gz'=8] {'tl'}, dimensions={0} | all-to-all | bytes 524288 | tf_op jit(solution)/shard_map/all_to_all | solution.py:460
  96.5 1.5 %shard_map.32 = f32[2,4,64,128]{3,2,1,0:T(8,128)} custom-call(s32[3]{0:T(128)S(1)} %pad_add_fusion.me, f32[4,2,64,128]{3,2,1,0:T(8,128)S(1)} %all_to_all.11.parts), custom_call_target="tpu_custom_call" | custom-call | tf_op jit(solution)/shard_map/pallas_call | solution.py:388
  (3 shorter events, 0.0 us)
Async XLA Ops:
  0.0 1.0 %copy-start.1 = (f32[2,4,64,128]{3,2,1,0:T(8,128)S(1)}, f32[2,4,64,128]{3,2,1,0:T(8,128)}, u32[]{:S(2)}) copy-start(f32[2,4,64,128]{3,2,1,0:T(8,128)} %rates.3) | copy-start | bytes 786436
  1.0 15.8 %copy-start = (f32[1,2,4,64,128]{4,3,2,1,0:T(8,128)S(1)}, f32[1,2,4,64,128]{4,3,2,1,0:T(8,128)}, u32[]{:S(2)}) copy-start(f32[1,2,4,64,128]{4,3,2,1,0:T(8,128)} %param.2) | copy-start | bytes 786436
  1.1 14.8 %collective-permute-start = (f32[2,2,4,16,128]{4,3,2,1,0:T(8,128)S(1)}, f32[2,2,4,16,128]{4,3,2,1,0:T(8,128)S(1)}, u32[]{:S(2)}, u32[]{:S(2)}) collective-permute-start(f32[2,2,4,16,128]{4,3,2,1,0:T(8,128)S(1)} %pad_maximum_fusion), channel_id=1, source_target_pairs={{8,16},{16,8},{24,32},{32,24},{40,48},{48,40},{56,64},{64,56},{72,... | collective-permute-start | bytes 393224 | tf_op jit(solution)/shard_map/ppermute | solution.py:406
  10.0 6.9 %collective-permute-start.1 = (f32[2,2,4,16,128]{4,3,2,1,0:T(8,128)S(1)}, f32[2,2,4,16,128]{4,3,2,1,0:T(8,128)S(1)}, u32[]{:S(2)}, u32[]{:S(2)}) collective-permute-start(f32[2,2,4,16,128]{4,3,2,1,0:T(8,128)S(1)} %pad_maximum_fusion.1), channel_id=1, source_target_pairs={{0,8},{8,0},{16,24},{24,16},{32,40},{40,32},{48,56},{56,48},{64,72... | collective-permute-start | bytes 393224 | tf_op jit(solution)/shard_map/ppermute | solution.py:406
  17.8 7.4 %collective-permute-start.2 = (f32[2,96,128]{2,1,0:T(8,128)S(1)}, f32[2,96,128]{2,1,0:T(8,128)S(1)}, u32[]{:S(2)}, u32[]{:S(2)}) collective-permute-start(f32[2,96,128]{2,1,0:T(8,128)S(1)} %get-tuple-element.11), channel_id=1, source_target_pairs={{1,2},{2,1},{3,4},{4,3},{5,6},{6,5},{7,0},{0,7},{9,10},{10,9},{11,... | collective-permute-start | bytes 294920 | tf_op jit(solution)/shard_map/ppermute | solution.py:406
  19.7 6.4 %collective-permute-start.3 = (f32[2,96,128]{2,1,0:T(8,128)S(1)}, f32[2,96,128]{2,1,0:T(8,128)S(1)}, u32[]{:S(2)}, u32[]{:S(2)}) collective-permute-start(f32[2,96,128]{2,1,0:T(8,128)S(1)} %get-tuple-element.12), channel_id=1, source_target_pairs={{0,1},{1,0},{2,3},{3,2},{4,5},{5,4},{6,7},{7,6},{8,9},{9,8},{10,11... | collective-permute-start | bytes 294920 | tf_op jit(solution)/shard_map/ppermute | solution.py:406
  63.8 20.7 %collective-permute-start.4 = (f32[2,2,2,80,128]{4,3,2,1,0:T(8,128)S(1)}, f32[2,2,2,80,128]{4,3,2,1,0:T(8,128)S(1)}, u32[]{:S(2)}, u32[]{:S(2)}) collective-permute-start(f32[2,2,2,80,128]{4,3,2,1,0:T(8,128)S(1)} %get-tuple-element.15), channel_id=1, source_target_pairs={{0,896},{128,768},{256,640},{384,512},{1,897},{129,769},{257,641},... | collective-permute-start | bytes 983048 | tf_op jit(solution)/shard_map/ppermute | solution.py:456

commit v5 on v4

--- a/solution.py
+++ b/solution.py
@@ -13,7 +13,7 @@
 ROWS = 64
 MARGIN = 12
 WIN = ROWS + 2 * MARGIN
-SENT = 80
+SENT = (80, 72)
 LANES = 128
 EXT = ROWS + 2 * HALO
 TILES = EXT // 8
@@ -313,54 +313,67 @@
     lax.fori_loop(first, GROUP, turn, 0)
 
 
-def early_kernel(me, windows, rates, ends, sent, coefs, starts, coarse_ends, current, rows, kept):
+def pack(sent, which, kept, state):
+    begin = MARGIN + (ROWS - SENT[which]) // 2
+    for c in range(2):
+        for p in range(2):
+            for j in range(BLOCK):
+                kept[c, p, rows_of(j), :] = state[c][p][j]
+            sent[c, p] = kept[c, p, begin : begin + SENT[which], :]
+
+
+def unpack(sent, which, kept, target):
+    begin = MARGIN + (ROWS - SENT[which]) // 2
+    for c in range(2):
+        for p in range(2):
+            kept[c, p, begin : begin + SENT[which], :] = sent[c, p]
+    save_state(target, load_window(kept))
+
+
+def early_kernel(
+    me, windows, rates, ends, sent_one, sent_two, coefs, starts, coarse_ends, current, rows, kept
+):
     @pl.when(me[0] < GROUP)
     def _():
         save_coefs(coefs, rates)
         save_state(starts.at[1], load_window(windows.at[0]))
         sweep(1, windows, coefs, starts, coarse_ends)
         put(ends, rows, 0, load_state(starts.at[1]))
-        pack(sent, 0, kept, load_state(starts.at[GROUP]))
+        pack(sent_one, 0, kept, load_state(starts.at[GROUP]))
         second_terms(1, coefs, starts, coarse_ends)
         state = add(load_state(coarse_ends.at[1]), load_state(starts.at[1]))
         put(ends, rows, 1, state)
         save_state(current, state)
         second_sweep(2, coefs, current, starts, rows, ends)
-        pack(sent, 1, kept, load_state(current))
-
-
-def pack(sent, which, kept, state):
-    for c in range(2):
-        for p in range(2):
-            for j in range(BLOCK):
-                kept[c, p, rows_of(j), :] = state[c][p][j]
-            begin = MARGIN + (ROWS - SENT) // 2
-            sent[which, c, p] = kept[c, p, begin : begin + SENT, :]
-
-
-def unpack(sent, which, kept, target):
-    for c in range(2):
-        for p in range(2):
-            begin = MARGIN + (ROWS - SENT) // 2
-            kept[c, p, begin : begin + SENT, :] = sent[which, c, p]
-    save_state(target, load_window(kept))
-
-
-def late_kernel(me, windows, rates, received, early_ends, ends, coefs, starts, coarse_ends, current, rows, kept):
-    @pl.when(me[0] < GROUP)
-    def _():
-        for m in range(GROUP):
-            ends[m] = early_ends[m]
+        pack(sent_two, 1, kept, load_state(current))
+
+
+def late_terms_kernel(me, windows, rates, received, after, terms, coefs, starts, coarse_ends, kept):
+    del after
 
     @pl.when(me[0] >= GROUP)
     def _():
         save_coefs(coefs, rates)
         kept[...] = jnp.zeros_like(kept)
         unpack(received, 0, kept, starts.at[0])
-        unpack(received, 1, kept, current)
         sweep(0, windows, coefs, starts, coarse_ends)
         second_terms(0, coefs, starts, coarse_ends)
-        second_sweep(0, coefs, current, starts, rows, ends)
+        for m in range(GROUP):
+            terms[m] = starts[m]
+
+
+def late_ends_kernel(me, terms, rates, received, early_ends, ends, coefs, current, rows, kept):
+    @pl.when(me[0] < GROUP)
+    def _():
+        for m in range(GROUP):
+            ends[m] = early_ends[m]
+
+    @pl.when(me[0] >= GROUP)
+    def _():
+        save_coefs(coefs, rates)
+        kept[...] = jnp.zeros_like(kept)
+        unpack(received, 1, kept, current)
+        second_sweep(0, coefs, current, terms, rows, ends)
 
 
 def merge_kernel(me, parts, out):
@@ -378,17 +391,17 @@
                 out[c, x, rows, :] = jnp.where(lane < 64, low, high)
 
 
-def call(kernel, shapes, scratch=(), scalars=0, inputs=pltpu.VMEM):
+def call(kernel, shapes, scratch=(), scalars=0, unread=0):
     vmem = pl.BlockSpec(memory_space=pltpu.VMEM)
-    given = pl.BlockSpec(memory_space=inputs)
     smem = pl.BlockSpec(memory_space=pltpu.SMEM)
+    anywhere = pl.BlockSpec(memory_space=pl.ANY)
 
     def run(*args):
-        out_shape = [jax.ShapeDtypeStruct(s, jnp.float32) for s in shapes]
+        read = len(args) - scalars - unread
         return pl.pallas_call(
             kernel,
-            out_shape=out_shape,
-            in_specs=[smem] * scalars + [given] * (len(args) - scalars),
+            out_shape=[jax.ShapeDtypeStruct(s, jnp.float32) for s in shapes],
+            in_specs=[smem] * scalars + [vmem] * read + [anywhere] * unread,
             out_specs=[vmem] * len(shapes),
             scratch_shapes=list(scratch),
             compiler_params=pltpu.CompilerParams(vmem_limit_bytes=32 * 1024 * 1024),
@@ -440,24 +453,40 @@
     )(me, state, rates, y_two, y_one, z_two, z_one)
     windows = lax.all_to_all(windows, "tl", 0, 0)
 
-    scratch = [
-        pltpu.VMEM((2, 3, 2, BLOCK, 8, LANES), jnp.float32),
-        pltpu.VMEM((GROUP + 1, 2, 2, BLOCK, 8, LANES), jnp.float32),
-        pltpu.VMEM((GROUP, 2, 2, BLOCK, 8, LANES), jnp.float32),
-        pltpu.VMEM((2, 2, BLOCK, 8, LANES), jnp.float32),
-        pltpu.VMEM((2, WIN, LANES), jnp.float32),
-        pltpu.VMEM((2, 2, WIN, LANES), jnp.float32),
-    ]
+    states = (2, 2, BLOCK, 8, LANES)
+    coefs = pltpu.VMEM((2, 3, *states[1:]), jnp.float32)
+    starts = pltpu.VMEM((GROUP + 1, *states), jnp.float32)
+    coarse_ends = pltpu.VMEM((GROUP, *states), jnp.float32)
+    current = pltpu.VMEM(states, jnp.float32)
+    rows = pltpu.VMEM((2, WIN, LANES), jnp.float32)
+    kept = pltpu.VMEM((2, 2, WIN, LANES), jnp.float32)
     ends_shape = (GROUP, 2, ROWS, LANES)
-    early_ends, sent = call(
-        early_kernel, [ends_shape, (2, 2, 2, SENT, LANES)], scratch=scratch, scalars=1
+    early_ends, sent_one, sent_two = call(
+        early_kernel,
+        [ends_shape] + [(2, 2, count, LANES) for count in SENT],
+        scratch=[coefs, starts, coarse_ends, current, rows, kept],
+        scalars=1,
     )(me, windows, rates_here)
     last = 2 * GROUP - 1
-    received = lax.ppermute(sent, ("th", "tl"), [(t, last - t) for t in range(GROUP)])
-    (ends,) = call(late_kernel, [ends_shape], scratch=scratch, scalars=1)(
-        me, windows, rates_here, received, early_ends
+    route = [(t, last - t) for t in range(GROUP)]
+    received_one = lax.ppermute(sent_one, ("th", "tl"), route)
+    received_two = lax.ppermute(sent_two, ("th", "tl"), route)
+
+    def hand_back(ends):
+        return lax.all_to_all(ends, "tl", 0, 0)
+
+    def leave(ends):
+        return ends
+
+    early = slice_index < GROUP
+    ends = lax.cond(early, hand_back, leave, early_ends)
+    (terms,) = call(
+        late_terms_kernel, [(GROUP, *states)], scratch=[coefs, starts, coarse_ends, kept], scalars=1, unread=1
+    )(me, windows, rates_here, received_one, ends)
+    (ends,) = call(late_ends_kernel, [ends_shape], scratch=[coefs, current, rows, kept], scalars=1)(
+        me, terms, rates_here, received_two, ends
     )
-    ends = lax.all_to_all(ends, "tl", 0, 0)
+    ends = lax.cond(early, leave, hand_back, ends)
     (out,) = call(merge_kernel, [(2, 4, ROWS, LANES)], scalars=1)(me, ends)
     return out[None]
 

time: 98.3 us -> 92.2 us (0.938)
  the two profiles are of different devices: /device:TPU:14 before, /device:TPU:526 now
where the time goes in v5:
time: 92.2 us; the launch traced here: 91.8 us
  blocking collectives  37.4 us (41%)
  starting transfers between devices  20.8 us (23%)
  waiting for transfers between devices  19.1 us (21%)
  Pallas kernels  13.3 us (14%)
  local copies, waits for them, and re-layouts  1.04 us (1%)
    all_to_all x1, blocking collectives, per_device(): windows = lax.all_to_all(windows, 'tl', 0, 0)  26.4 us
    ppermute x4, starting transfers between devices, swap(): return lax.ppermute(block, axis, route)  18.2 us
    ppermute x1, waiting for transfers between devices, per_device(): received_one = lax.ppermute(sent_one, ('th', 'tl'), route)  13.3 us
    pallas_call x6, Pallas kernels, run(): pl.pallas_call(kernel, out_shape=[jax.ShapeDtypeStruct(s, jnp.float32) fo...  13.3 us
    all_to_all x1, blocking collectives, hand_back(): return lax.all_to_all(ends, 'tl', 0, 0)  11 us
    ppermute x4, waiting for transfers between devices, swap(): return lax.ppermute(block, axis, route)  5.76 us
  transfers between devices with their start and end apart: 6, of which 4 were waited for; matrix products, arithmetic and copies ran while one was open for 0% of the time, Pallas kernels for 4%

profile of v5, /device:TPU:526, one launch (start us, length us, event | category | flops | bytes accessed | tf_op | source)
XLA Modules:
  0.0 91.8 jit_solution(336968930766339352)
XLA Ops:
  0.0 0.0 copy-start.1
  0.0 0.9 %constant_dynamic-slice_fusion = (f32[1,2,4,16,128]{4,3,2,1,0:T(8,128)S(1)}, f32[1,2,4,16,128]{4,3,2,1,0:T(8,128)S(1)}) fusion(f32[1,2,4,64,128]{4,3,2,1,0:T(8,128)} %param.6, s32[]{:T(128)S(6)} %select_n.17, s32[]{:T(128)S(6)} %select_n.16), kind=kLoop, calls=%fused_computation.4 | loop fusion | bytes 262152 | tf_op jit(solution)/shard_map/dynamic_slice | solution.py:423
  0.9 0.1 copy-done.1
  1.0 0.0 copy-start
  1.1 8.9 %collective-permute-start = (f32[2,2,4,16,128]{4,3,2,1,0:T(8,128)S(1)}, f32[2,2,4,16,128]{4,3,2,1,0:T(8,128)S(1)}, u32[]{:S(2)}, u32[]{:S(2)}) collective-permute-start(f32[2,2,4,16,128]{4,3,2,1,0:T(8,128)S(1)} %pad_maximum_fusion), channel_id=1, source_target_pairs={{8,16},{16,8},{24,32},{32,24},{40,48},{48,40},{56,64},{64,56},{72,... | collective-permute-start | bytes 393224 | tf_op jit(solution)/shard_map/ppermute | solution.py:419
  10.0 1.9 %collective-permute-start.1 = (f32[2,2,4,16,128]{4,3,2,1,0:T(8,128)S(1)}, f32[2,2,4,16,128]{4,3,2,1,0:T(8,128)S(1)}, u32[]{:S(2)}, u32[]{:S(2)}) collective-permute-start(f32[2,2,4,16,128]{4,3,2,1,0:T(8,128)S(1)} %pad_maximum_fusion.1), channel_id=1, source_target_pairs={{0,8},{8,0},{16,24},{24,16},{32,40},{40,32},{48,56},{56,48},{64,72... | collective-permute-start | bytes 393224 | tf_op jit(solution)/shard_map/ppermute | solution.py:419
  11.9 0.1 pad_add_fusion.me
  12.0 3.9 %collective-permute-done.y_two = f32[2,2,4,16,128]{4,3,2,1,0:T(8,128)S(1)} collective-permute-done((f32[2,2,4,16,128]{4,3,2,1,0:T(8,128)S(1)}, f32[2,2,4,16,128]{4,3,2,1,0:T(8,128)S(1)}, u32[]{:S(2)}, u32[]{:S(2)}) %collective-permute-start) | collective-permute-done | bytes 131104 | tf_op jit(solution)/shard_map/ppermute | solution.py:419
  15.9 0.9 %collective-permute-done.1.y_one = f32[2,2,4,16,128]{4,3,2,1,0:T(8,128)S(1)} collective-permute-done((f32[2,2,4,16,128]{4,3,2,1,0:T(8,128)S(1)}, f32[2,2,4,16,128]{4,3,2,1,0:T(8,128)S(1)}, u32[]{:S(2)}, u32[]{:S(2)}) %collective-permute-start.1) | collective-permute-done | bytes 131104 | tf_op jit(solution)/shard_map/ppermute | solution.py:419
  16.8 0.0 copy-done
  16.8 1.0 %shard_map.28 = (f32[2,96,128]{2,1,0:T(8,128)S(1)}, f32[2,96,128]{2,1,0:T(8,128)S(1)}) custom-call(s32[3]{0:T(128)S(1)} %pad_add_fusion.me, f32[2,4,64,128]{3,2,1,0:T(8,128)S(1)} %bitcast.9, f32[2,4,64,128]{3,2,1,0:T(8,128)S(1)} %copy-done.1, f32[2,2,4,16,128]{4,3,2,1,0:T(8,128)S(1)} %collective-permute-done.y_two, ...), custom_call_target="tpu_custom_call" | custom-call | tf_op jit(solution)/shard_map/pallas_call | solution.py:401
  17.8 1.9 %collective-permute-start.2 = (f32[2,96,128]{2,1,0:T(8,128)S(1)}, f32[2,96,128]{2,1,0:T(8,128)S(1)}, u32[]{:S(2)}, u32[]{:S(2)}) collective-permute-start(f32[2,96,128]{2,1,0:T(8,128)S(1)} %get-tuple-element.22), channel_id=1, source_target_pairs={{1,2},{2,1},{3,4},{4,3},{5,6},{6,5},{7,0},{0,7},{9,10},{10,9},{11,... | collective-permute-start | bytes 294920 | tf_op jit(solution)/shard_map/ppermute | solution.py:419
  19.7 5.4 %collective-permute-start.3 = (f32[2,96,128]{2,1,0:T(8,128)S(1)}, f32[2,96,128]{2,1,0:T(8,128)S(1)}, u32[]{:S(2)}, u32[]{:S(2)}) collective-permute-start(f32[2,96,128]{2,1,0:T(8,128)S(1)} %get-tuple-element.23), channel_id=1, source_target_pairs={{0,1},{1,0},{2,3},{3,2},{4,5},{5,4},{6,7},{7,6},{8,9},{9,8},{10,11... | collective-permute-start | bytes 294920 | tf_op jit(solution)/shard_map/ppermute | solution.py:419
  25.2 0.0 collective-permute-done.2.z_two
  25.2 0.9 collective-permute-done.3.z_one
  26.1 4.8 %shard_map.29 = (f32[4,2,2,88,128]{4,3,2,1,0:T(8,128)S(1)}, f32[2,2,88,128]{3,2,1,0:T(8,128)S(1)}) custom-call(s32[3]{0:T(128)S(1)} %pad_add_fusion.me, f32[2,4,64,128]{3,2,1,0:T(8,128)S(1)} %bitcast.10, f32[2,4,64,128]{3,2,1,0:T(8,128)S(1)} %copy-done.1, f32[2,2,4,16,128]{4,3,2,1,0:T(8,128)S(1)} %collective-permute-done.y_two, ...), custom_call_target="tpu_custom_call" | custom-call | tf_op jit(solution)/shard_map/pallas_call | solution.py:401
  30.9 26.4 %all_to_all.15.windows = f32[4,2,2,88,128]{4,3,2,1,0:T(8,128)S(1)} all-to-all(f32[4,2,2,88,128]{4,3,2,1,0:T(8,128)S(1)} %get-tuple-element.24), channel_id=1, replica_groups=mesh['th'=2,'tl'=4,'gy'=16,'gz'=8] {'tl'}, dimensions={0} | all-to-all | bytes 1441792 | tf_op jit(solution)/shard_map/all_to_all | solution.py:454
  57.3 0.5 shard_map.30
  57.8 1.3 %collective-permute-start.4 = (f32[2,2,80,128]{3,2,1,0:T(8,128)S(1)}, f32[2,2,80,128]{3,2,1,0:T(8,128)S(1)}, u32[]{:S(2)}, u32[]{:S(2)}) collective-permute-start(f32[2,2,80,128]{3,2,1,0:T(8,128)S(1)} %get-tuple-element.26), channel_id=1, source_target_pairs={{0,896},{128,768},{256,640},{384,512},{1,897},{129,769},{257,641},... | collective-permute-start | bytes 491528 | tf_op jit(solution)/shard_map/ppermute | solution.py:472
  59.1 1.3 %collective-permute-start.5 = (f32[2,2,72,128]{3,2,1,0:T(8,128)S(1)}, f32[2,2,72,128]{3,2,1,0:T(8,128)S(1)}, u32[]{:S(2)}, u32[]{:S(2)}) collective-permute-start(f32[2,2,72,128]{3,2,1,0:T(8,128)S(1)} %get-tuple-element.28), channel_id=1, source_target_pairs={{0,896},{128,768},{256,640},{384,512},{1,897},{129,769},{257,641},... | collective-permute-start | bytes 442376 | tf_op jit(solution)/shard_map/ppermute | solution.py:473
  60.5 13.3 %collective-permute-done.4.received = f32[2,2,80,128]{3,2,1,0:T(8,128)S(1)} collective-permute-done((f32[2,2,80,128]{3,2,1,0:T(8,128)S(1)}, f32[2,2,80,128]{3,2,1,0:T(8,128)S(1)}, u32[]{:S(2)}, u32[]{:S(2)}) %collective-permute-start.4) | collective-permute-done | bytes 163872 | tf_op jit(solution)/shard_map/ppermute | solution.py:472
  73.8 3.6 %shard_map.31.terms = f32[4,2,2,11,8,128]{5,4,3,2,1,0:T(8,128)S(1)} custom-call(s32[3]{0:T(128)S(1)} %pad_add_fusion.me, f32[4,2,2,88,128]{4,3,2,1,0:T(8,128)S(1)} %all_to_all.15.windows, f32[2,2,88,128]{3,2,1,0:T(8,128)S(1)} %get-tuple-element.25.rates, f32[2,2,80,128]{3,2,1,0:T(8,128)S(1)} %collective-permute-done.4.received, ...), custom_call_target="tpu_custom_call" | custom-call | tf_op jit(solution)/shard_map/pallas_call | solution.py:401
  77.3 0.0 collective-permute-done.5.received
  77.3 1.9 %shard_map.32 = f32[4,2,64,128]{3,2,1,0:T(8,128)S(1)} custom-call(s32[3]{0:T(128)S(1)} %pad_add_fusion.me, f32[4,2,2,11,8,128]{5,4,3,2,1,0:T(8,128)S(1)} %shard_map.31.terms, f32[2,2,88,128]{3,2,1,0:T(8,128)S(1)} %get-tuple-element.25.rates, f32[2,2,72,128]{3,2,1,0:T(8,128)S(1)} %collective-permute-done.5.received, ...), custom_call_target="tpu_custom_call" | custom-call | tf_op jit(solution)/shard_map/pallas_call | solution.py:401
  79.2 11.1 %conditional.3 = (f32[4,2,64,128]{3,2,1,0:T(8,128)S(1)}) conditional(s32[]{:T(128)} %convert_element_type.4, f32[4,2,64,128]{3,2,1,0:T(8,128)S(1)} %shard_map.32, f32[4,2,64,128]{3,2,1,0:T(8,128)S(1)} %shard_map.32), branch_computations={%region_2.3_spmd, %region_3.4_spmd} | conditional | bytes 1048584 | solution.py:489
  79.3 11.0 %all_to_all.14 = f32[4,2,64,128]{3,2,1,0:T(8,128)S(1)} all-to-all(f32[4,2,64,128]{3,2,1,0:T(8,128)S(1)} %copy.8), channel_id=1, replica_groups=mesh['th'=2,'tl'=4,'gy'=16,'gz'=8] {'tl'}, dimensions={0} | all-to-all | bytes 524288 | tf_op jit(solution)/shard_map/cond/branch_0_fun/all_to_all | solution.py:476
  90.3 1.5 %shard_map.33 = f32[2,4,64,128]{3,2,1,0:T(8,128)} custom-call(s32[3]{0:T(128)S(1)} %pad_add_fusion.me, f32[4,2,64,128]{3,2,1,0:T(8,128)S(1)} %get-tuple-element.34.parts), custom_call_target="tpu_custom_call" | custom-call | tf_op jit(solution)/shard_map/pallas_call | solution.py:401
  (5 shorter events, 0.1 us)
Async XLA Ops:
  0.0 1.0 %copy-start.1 = (f32[2,4,64,128]{3,2,1,0:T(8,128)S(1)}, f32[2,4,64,128]{3,2,1,0:T(8,128)}, u32[]{:S(2)}) copy-start(f32[2,4,64,128]{3,2,1,0:T(8,128)} %rates.3) | copy-start | bytes 786436
  1.0 15.8 %copy-start = (f32[1,2,4,64,128]{4,3,2,1,0:T(8,128)S(1)}, f32[1,2,4,64,128]{4,3,2,1,0:T(8,128)}, u32[]{:S(2)}) copy-start(f32[1,2,4,64,128]{4,3,2,1,0:T(8,128)} %param.6) | copy-start | bytes 786436
  1.1 14.8 %collective-permute-start = (f32[2,2,4,16,128]{4,3,2,1,0:T(8,128)S(1)}, f32[2,2,4,16,128]{4,3,2,1,0:T(8,128)S(1)}, u32[]{:S(2)}, u32[]{:S(2)}) collective-permute-start(f32[2,2,4,16,128]{4,3,2,1,0:T(8,128)S(1)} %pad_maximum_fusion), channel_id=1, source_target_pairs={{8,16},{16,8},{24,32},{32,24},{40,48},{48,40},{56,64},{64,56},{72,... | collective-permute-start | bytes 393224 | tf_op jit(solution)/shard_map/ppermute | solution.py:419
  10.0 6.9 %collective-permute-start.1 = (f32[2,2,4,16,128]{4,3,2,1,0:T(8,128)S(1)}, f32[2,2,4,16,128]{4,3,2,1,0:T(8,128)S(1)}, u32[]{:S(2)}, u32[]{:S(2)}) collective-permute-start(f32[2,2,4,16,128]{4,3,2,1,0:T(8,128)S(1)} %pad_maximum_fusion.1), channel_id=1, source_target_pairs={{0,8},{8,0},{16,24},{24,16},{32,40},{40,32},{48,56},{56,48},{64,72... | collective-permute-start | bytes 393224 | tf_op jit(solution)/shard_map/ppermute | solution.py:419
  17.8 7.4 %collective-permute-start.2 = (f32[2,96,128]{2,1,0:T(8,128)S(1)}, f32[2,96,128]{2,1,0:T(8,128)S(1)}, u32[]{:S(2)}, u32[]{:S(2)}) collective-permute-start(f32[2,96,128]{2,1,0:T(8,128)S(1)} %get-tuple-element.22), channel_id=1, source_target_pairs={{1,2},{2,1},{3,4},{4,3},{5,6},{6,5},{7,0},{0,7},{9,10},{10,9},{11,... | collective-permute-start | bytes 294920 | tf_op jit(solution)/shard_map/ppermute | solution.py:419
  19.7 6.4 %collective-permute-start.3 = (f32[2,96,128]{2,1,0:T(8,128)S(1)}, f32[2,96,128]{2,1,0:T(8,128)S(1)}, u32[]{:S(2)}, u32[]{:S(2)}) collective-permute-start(f32[2,96,128]{2,1,0:T(8,128)S(1)} %get-tuple-element.23), channel_id=1, source_target_pairs={{0,1},{1,0},{2,3},{3,2},{4,5},{5,4},{6,7},{7,6},{8,9},{9,8},{10,11... | collective-permute-start | bytes 294920 | tf_op jit(solution)/shard_map/ppermute | solution.py:419
  57.8 15.9 %collective-permute-start.4 = (f32[2,2,80,128]{3,2,1,0:T(8,128)S(1)}, f32[2,2,80,128]{3,2,1,0:T(8,128)S(1)}, u32[]{:S(2)}, u32[]{:S(2)}) collective-permute-start(f32[2,2,80,128]{3,2,1,0:T(8,128)S(1)} %get-tuple-element.26), channel_id=1, source_target_pairs={{0,896},{128,768},{256,640},{384,512},{1,897},{129,769},{257,641},... | collective-permute-start | bytes 491528 | tf_op jit(solution)/shard_map/ppermute | solution.py:472
  59.1 18.2 %collective-permute-start.5 = (f32[2,2,72,128]{3,2,1,0:T(8,128)S(1)}, f32[2,2,72,128]{3,2,1,0:T(8,128)S(1)}, u32[]{:S(2)}, u32[]{:S(2)}) collective-permute-start(f32[2,2,72,128]{3,2,1,0:T(8,128)S(1)} %get-tuple-element.28), channel_id=1, source_target_pairs={{0,896},{128,768},{256,640},{384,512},{1,897},{129,769},{257,641},... | collective-permute-start | bytes 442376 | tf_op jit(solution)/shard_map/ppermute | solution.py:473

commit v6 on v4

--- a/solution.py
+++ b/solution.py
@@ -313,40 +313,68 @@
     lax.fori_loop(first, GROUP, turn, 0)
 
 
-def early_kernel(me, windows, rates, ends, sent, coefs, starts, coarse_ends, current, rows, kept):
+def between(lane, begin, end):
+    return (lane >= begin) & (lane < end)
+
+
+def pack(sent, one, two):
+    lane = lane_index()
+    begin = MARGIN + (ROWS - SENT) // 2
+    for r in range(SENT // 8):
+        rows = slice(8 * r, 8 * r + 8)
+        there = slice(begin + 8 * r, begin + 8 * r + 8)
+        for k in range(4):
+            second = two[k // 2, k % 2, there, :]
+            half = k % 2
+            first = roll(one[0, k // 2, there, :], 93 - (64 * half + 9), 1)
+            block = jnp.where(between(lane, 52, 92), roll(second, -24, 1), first)
+            sent[k, rows, :] = jnp.where(between(lane, 12, 52), second, block)
+        for p in range(2):
+            sent[4 + p, rows, :] = one[1, p, there, :]
+
+
+def unpack(sent, one, two):
+    lane = lane_index()
+    begin = MARGIN + (ROWS - SENT) // 2
+    for r in range(SENT // 8):
+        rows = slice(8 * r, 8 * r + 8)
+        there = slice(begin + 8 * r, begin + 8 * r + 8)
+        blocks = [sent[k, rows, :] for k in range(4)]
+        for k in range(4):
+            two[k // 2, k % 2, there, :] = jnp.where(lane < 64, blocks[k], roll(blocks[k], 24, 1))
+        for p in range(2):
+            low, high = roll(blocks[2 * p], 9 - 93, 1), roll(blocks[2 * p + 1], 64 + 9 - 93, 1)
+            one[0, p, there, :] = jnp.where(lane < 64, low, high)
+            one[1, p, there, :] = sent[4 + p, rows, :]
+
+
+def save_window(ref, state):
+    for c in range(2):
+        for p in range(2):
+            for j in range(BLOCK):
+                ref[c, p, rows_of(j), :] = state[c][p][j]
+
+
+def early_kernel(me, windows, rates, ends, sent, coefs, starts, coarse_ends, current, rows, one, two):
     @pl.when(me[0] < GROUP)
     def _():
         save_coefs(coefs, rates)
         save_state(starts.at[1], load_window(windows.at[0]))
         sweep(1, windows, coefs, starts, coarse_ends)
         put(ends, rows, 0, load_state(starts.at[1]))
-        pack(sent, 0, kept, load_state(starts.at[GROUP]))
+        save_window(one, load_state(starts.at[GROUP]))
         second_terms(1, coefs, starts, coarse_ends)
         state = add(load_state(coarse_ends.at[1]), load_state(starts.at[1]))
         put(ends, rows, 1, state)
         save_state(current, state)
         second_sweep(2, coefs, current, starts, rows, ends)
-        pack(sent, 1, kept, load_state(current))
-
-
-def pack(sent, which, kept, state):
-    for c in range(2):
-        for p in range(2):
-            for j in range(BLOCK):
-                kept[c, p, rows_of(j), :] = state[c][p][j]
-            begin = MARGIN + (ROWS - SENT) // 2
-            sent[which, c, p] = kept[c, p, begin : begin + SENT, :]
-
-
-def unpack(sent, which, kept, target):
-    for c in range(2):
-        for p in range(2):
-            begin = MARGIN + (ROWS - SENT) // 2
-            kept[c, p, begin : begin + SENT, :] = sent[which, c, p]
-    save_state(target, load_window(kept))
-
-
-def late_kernel(me, windows, rates, received, early_ends, ends, coefs, starts, coarse_ends, current, rows, kept):
+        save_window(two, load_state(current))
+        pack(sent, one, two)
+
+
+def late_kernel(
+    me, windows, rates, received, early_ends, ends, coefs, starts, coarse_ends, current, rows, one, two
+):
     @pl.when(me[0] < GROUP)
     def _():
         for m in range(GROUP):
@@ -355,9 +383,11 @@
     @pl.when(me[0] >= GROUP)
     def _():
         save_coefs(coefs, rates)
-        kept[...] = jnp.zeros_like(kept)
-        unpack(received, 0, kept, starts.at[0])
-        unpack(received, 1, kept, current)
+        one[...] = jnp.zeros_like(one)
+        two[...] = jnp.zeros_like(two)
+        unpack(received, one, two)
+        save_state(starts.at[0], load_window(one))
+        save_state(current, load_window(two))
         sweep(0, windows, coefs, starts, coarse_ends)
         second_terms(0, coefs, starts, coarse_ends)
         second_sweep(0, coefs, current, starts, rows, ends)
@@ -378,17 +408,15 @@
                 out[c, x, rows, :] = jnp.where(lane < 64, low, high)
 
 
-def call(kernel, shapes, scratch=(), scalars=0, inputs=pltpu.VMEM):
+def call(kernel, shapes, scratch=(), scalars=0):
     vmem = pl.BlockSpec(memory_space=pltpu.VMEM)
-    given = pl.BlockSpec(memory_space=inputs)
     smem = pl.BlockSpec(memory_space=pltpu.SMEM)
 
     def run(*args):
-        out_shape = [jax.ShapeDtypeStruct(s, jnp.float32) for s in shapes]
         return pl.pallas_call(
             kernel,
-            out_shape=out_shape,
-            in_specs=[smem] * scalars + [given] * (len(args) - scalars),
+            out_shape=[jax.ShapeDtypeStruct(s, jnp.float32) for s in shapes],
+            in_specs=[smem] * scalars + [vmem] * (len(args) - scalars),
             out_specs=[vmem] * len(shapes),
             scratch_shapes=list(scratch),
             compiler_params=pltpu.CompilerParams(vmem_limit_bytes=32 * 1024 * 1024),
@@ -440,24 +468,33 @@
     )(me, state, rates, y_two, y_one, z_two, z_one)
     windows = lax.all_to_all(windows, "tl", 0, 0)
 
-    scratch = [
-        pltpu.VMEM((2, 3, 2, BLOCK, 8, LANES), jnp.float32),
-        pltpu.VMEM((GROUP + 1, 2, 2, BLOCK, 8, LANES), jnp.float32),
-        pltpu.VMEM((GROUP, 2, 2, BLOCK, 8, LANES), jnp.float32),
-        pltpu.VMEM((2, 2, BLOCK, 8, LANES), jnp.float32),
-        pltpu.VMEM((2, WIN, LANES), jnp.float32),
-        pltpu.VMEM((2, 2, WIN, LANES), jnp.float32),
-    ]
+    states = (2, 2, BLOCK, 8, LANES)
+    coefs = pltpu.VMEM((2, 3, *states[1:]), jnp.float32)
+    starts = pltpu.VMEM((GROUP + 1, *states), jnp.float32)
+    coarse_ends = pltpu.VMEM((GROUP, *states), jnp.float32)
+    current = pltpu.VMEM(states, jnp.float32)
+    rows = pltpu.VMEM((2, WIN, LANES), jnp.float32)
+    window = pltpu.VMEM((2, 2, WIN, LANES), jnp.float32)
+    scratch = [coefs, starts, coarse_ends, current, rows, window, window]
     ends_shape = (GROUP, 2, ROWS, LANES)
-    early_ends, sent = call(
-        early_kernel, [ends_shape, (2, 2, 2, SENT, LANES)], scratch=scratch, scalars=1
-    )(me, windows, rates_here)
+    early_ends, sent = call(early_kernel, [ends_shape, (6, SENT, LANES)], scratch=scratch, scalars=1)(
+        me, windows, rates_here
+    )
     last = 2 * GROUP - 1
     received = lax.ppermute(sent, ("th", "tl"), [(t, last - t) for t in range(GROUP)])
+
+    def hand_back(ends):
+        return lax.all_to_all(ends, "tl", 0, 0)
+
+    def leave(ends):
+        return ends
+
+    early = slice_index < GROUP
+    ends = lax.cond(early, hand_back, leave, early_ends)
     (ends,) = call(late_kernel, [ends_shape], scratch=scratch, scalars=1)(
-        me, windows, rates_here, received, early_ends
+        me, windows, rates_here, received, ends
     )
-    ends = lax.all_to_all(ends, "tl", 0, 0)
+    ends = lax.cond(early, leave, hand_back, ends)
     (out,) = call(merge_kernel, [(2, 4, ROWS, LANES)], scalars=1)(me, ends)
     return out[None]
 

time: 98.3 us -> 91.9 us (0.935)
  the two profiles are of different devices: /device:TPU:14 before, /device:TPU:526 now
where the time goes in v6:
time: 91.9 us; the launch traced here: 91.6 us
  blocking collectives  38.4 us (42%)
  waiting for transfers between devices  19.7 us (21%)
  starting transfers between devices  19.5 us (21%)
  Pallas kernels  12.7 us (14%)
  local copies, waits for them, and re-layouts  1.04 us (1%)
    all_to_all x1, blocking collectives, per_device(): windows = lax.all_to_all(windows, 'tl', 0, 0)  26.4 us
    ppermute x4, starting transfers between devices, swap(): return lax.ppermute(block, axis, route)  18.2 us
    ppermute x1, waiting for transfers between devices, per_device(): lax.ppermute(sent, ('th', 'tl'), [(t, last - t) for t in range(GROUP)])  13.9 us
    pallas_call x5, Pallas kernels, run(): pl.pallas_call(kernel, out_shape=[jax.ShapeDtypeStruct(s, jnp.float32) fo...  12.7 us
    all_to_all x1, blocking collectives, hand_back(): return lax.all_to_all(ends, 'tl', 0, 0)  12 us
    ppermute x4, waiting for transfers between devices, swap(): return lax.ppermute(block, axis, route)  5.76 us
  transfers between devices with their start and end apart: 5, of which 4 were waited for; matrix products, arithmetic and copies ran while one was open for 0% of the time, Pallas kernels for 0%

profile of v6, /device:TPU:526, one launch (start us, length us, event | category | flops | bytes accessed | tf_op | source)
XLA Modules:
  0.0 91.6 jit_solution(9282365020317421678)
XLA Ops:
  0.0 0.0 copy-start.1
  0.0 0.9 %constant_dynamic-slice_fusion = (f32[1,2,4,16,128]{4,3,2,1,0:T(8,128)S(1)}, f32[1,2,4,16,128]{4,3,2,1,0:T(8,128)S(1)}) fusion(f32[1,2,4,64,128]{4,3,2,1,0:T(8,128)} %param.6, s32[]{:T(128)S(6)} %select_n.17, s32[]{:T(128)S(6)} %select_n.16), kind=kLoop, calls=%fused_computation.4 | loop fusion | bytes 262152 | tf_op jit(solution)/shard_map/dynamic_slice | solution.py:438
  0.9 0.1 copy-done.1
  1.0 0.0 copy-start
  1.1 8.9 %collective-permute-start = (f32[2,2,4,16,128]{4,3,2,1,0:T(8,128)S(1)}, f32[2,2,4,16,128]{4,3,2,1,0:T(8,128)S(1)}, u32[]{:S(2)}, u32[]{:S(2)}) collective-permute-start(f32[2,2,4,16,128]{4,3,2,1,0:T(8,128)S(1)} %pad_maximum_fusion), channel_id=1, source_target_pairs={{8,16},{16,8},{24,32},{32,24},{40,48},{48,40},{56,64},{64,56},{72,... | collective-permute-start | bytes 393224 | tf_op jit(solution)/shard_map/ppermute | solution.py:434
  10.0 1.9 %collective-permute-start.1 = (f32[2,2,4,16,128]{4,3,2,1,0:T(8,128)S(1)}, f32[2,2,4,16,128]{4,3,2,1,0:T(8,128)S(1)}, u32[]{:S(2)}, u32[]{:S(2)}) collective-permute-start(f32[2,2,4,16,128]{4,3,2,1,0:T(8,128)S(1)} %pad_maximum_fusion.1), channel_id=1, source_target_pairs={{0,8},{8,0},{16,24},{24,16},{32,40},{40,32},{48,56},{56,48},{64,72... | collective-permute-start | bytes 393224 | tf_op jit(solution)/shard_map/ppermute | solution.py:434
  11.9 0.1 pad_add_fusion.me
  12.0 3.9 %collective-permute-done.y_two = f32[2,2,4,16,128]{4,3,2,1,0:T(8,128)S(1)} collective-permute-done((f32[2,2,4,16,128]{4,3,2,1,0:T(8,128)S(1)}, f32[2,2,4,16,128]{4,3,2,1,0:T(8,128)S(1)}, u32[]{:S(2)}, u32[]{:S(2)}) %collective-permute-start) | collective-permute-done | bytes 131104 | tf_op jit(solution)/shard_map/ppermute | solution.py:434
  15.9 0.9 %collective-permute-done.1.y_one = f32[2,2,4,16,128]{4,3,2,1,0:T(8,128)S(1)} collective-permute-done((f32[2,2,4,16,128]{4,3,2,1,0:T(8,128)S(1)}, f32[2,2,4,16,128]{4,3,2,1,0:T(8,128)S(1)}, u32[]{:S(2)}, u32[]{:S(2)}) %collective-permute-start.1) | collective-permute-done | bytes 131104 | tf_op jit(solution)/shard_map/ppermute | solution.py:434
  16.8 0.0 copy-done
  16.8 1.0 %shard_map.28 = (f32[2,96,128]{2,1,0:T(8,128)S(1)}, f32[2,96,128]{2,1,0:T(8,128)S(1)}) custom-call(s32[3]{0:T(128)S(1)} %pad_add_fusion.me, f32[2,4,64,128]{3,2,1,0:T(8,128)S(1)} %bitcast.9, f32[2,4,64,128]{3,2,1,0:T(8,128)S(1)} %copy-done.1, f32[2,2,4,16,128]{4,3,2,1,0:T(8,128)S(1)} %collective-permute-done.y_two, ...), custom_call_target="tpu_custom_call" | custom-call | tf_op jit(solution)/shard_map/pallas_call | solution.py:416
  17.8 1.9 %collective-permute-start.2 = (f32[2,96,128]{2,1,0:T(8,128)S(1)}, f32[2,96,128]{2,1,0:T(8,128)S(1)}, u32[]{:S(2)}, u32[]{:S(2)}) collective-permute-start(f32[2,96,128]{2,1,0:T(8,128)S(1)} %get-tuple-element.21), channel_id=1, source_target_pairs={{1,2},{2,1},{3,4},{4,3},{5,6},{6,5},{7,0},{0,7},{9,10},{10,9},{11,... | collective-permute-start | bytes 294920 | tf_op jit(solution)/shard_map/ppermute | solution.py:434
  19.7 5.4 %collective-permute-start.3 = (f32[2,96,128]{2,1,0:T(8,128)S(1)}, f32[2,96,128]{2,1,0:T(8,128)S(1)}, u32[]{:S(2)}, u32[]{:S(2)}) collective-permute-start(f32[2,96,128]{2,1,0:T(8,128)S(1)} %get-tuple-element.22), channel_id=1, source_target_pairs={{0,1},{1,0},{2,3},{3,2},{4,5},{5,4},{6,7},{7,6},{8,9},{9,8},{10,11... | collective-permute-start | bytes 294920 | tf_op jit(solution)/shard_map/ppermute | solution.py:434
  25.2 0.0 collective-permute-done.2.z_two
  25.2 0.9 collective-permute-done.3.z_one
  26.1 4.8 %shard_map.29 = (f32[4,2,2,88,128]{4,3,2,1,0:T(8,128)S(1)}, f32[2,2,88,128]{3,2,1,0:T(8,128)S(1)}) custom-call(s32[3]{0:T(128)S(1)} %pad_add_fusion.me, f32[2,4,64,128]{3,2,1,0:T(8,128)S(1)} %bitcast.10, f32[2,4,64,128]{3,2,1,0:T(8,128)S(1)} %copy-done.1, f32[2,2,4,16,128]{4,3,2,1,0:T(8,128)S(1)} %collective-permute-done.y_two, ...), custom_call_target="tpu_custom_call" | custom-call | tf_op jit(solution)/shard_map/pallas_call | solution.py:416
  30.9 26.4 %all_to_all.15.windows = f32[4,2,2,88,128]{4,3,2,1,0:T(8,128)S(1)} all-to-all(f32[4,2,2,88,128]{4,3,2,1,0:T(8,128)S(1)} %get-tuple-element.23), channel_id=1, replica_groups=mesh['th'=2,'tl'=4,'gy'=16,'gz'=8] {'tl'}, dimensions={0} | all-to-all | bytes 1441792 | tf_op jit(solution)/shard_map/all_to_all | solution.py:469
  57.3 0.5 shard_map.30
  57.8 1.3 %collective-permute-start.4 = (f32[6,80,128]{2,1,0:T(8,128)S(1)}, f32[6,80,128]{2,1,0:T(8,128)S(1)}, u32[]{:S(2)}, u32[]{:S(2)}) collective-permute-start(f32[6,80,128]{2,1,0:T(8,128)S(1)} %get-tuple-element.25), channel_id=1, source_target_pairs={{0,896},{128,768},{256,640},{384,512},{1,897},{129,769},{257,641},... | collective-permute-start | bytes 737288 | tf_op jit(solution)/shard_map/ppermute | solution.py:484
  59.2 13.9 %collective-permute-done.4.received = f32[6,80,128]{2,1,0:T(8,128)S(1)} collective-permute-done((f32[6,80,128]{2,1,0:T(8,128)S(1)}, f32[6,80,128]{2,1,0:T(8,128)S(1)}, u32[]{:S(2)}, u32[]{:S(2)}) %collective-permute-start.4) | collective-permute-done | bytes 245792 | tf_op jit(solution)/shard_map/ppermute | solution.py:484
  73.1 4.9 %shard_map.31 = f32[4,2,64,128]{3,2,1,0:T(8,128)S(1)} custom-call(s32[3]{0:T(128)S(1)} %pad_add_fusion.me, f32[4,2,2,88,128]{4,3,2,1,0:T(8,128)S(1)} %all_to_all.15.windows, f32[2,2,88,128]{3,2,1,0:T(8,128)S(1)} %get-tuple-element.24.rates, f32[6,80,128]{2,1,0:T(8,128)S(1)} %collective-permute-done.4.received, f32[4,2,64,128]{3,2,1,0:T(8,128)S(1)} %get-tuple-element.31.early_ends), custom_call_target="tpu_custom_call" | custom-call | tf_op jit(solution)/shard_map/pallas_call | solution.py:416
  78.0 12.1 %conditional.3 = (f32[4,2,64,128]{3,2,1,0:T(8,128)S(1)}) conditional(s32[]{:T(128)} %convert_element_type.4, f32[4,2,64,128]{3,2,1,0:T(8,128)S(1)} %shard_map.31, f32[4,2,64,128]{3,2,1,0:T(8,128)S(1)} %shard_map.31), branch_computations={%region_2.3_spmd, %region_3.4_spmd} | conditional | bytes 1048584 | solution.py:497
  78.1 12.0 %all_to_all.14 = f32[4,2,64,128]{3,2,1,0:T(8,128)S(1)} all-to-all(f32[4,2,64,128]{3,2,1,0:T(8,128)S(1)} %copy.8), channel_id=1, replica_groups=mesh['th'=2,'tl'=4,'gy'=16,'gz'=8] {'tl'}, dimensions={0} | all-to-all | bytes 524288 | tf_op jit(solution)/shard_map/cond/branch_0_fun/all_to_all | solution.py:487
  90.1 1.5 %shard_map.32 = f32[2,4,64,128]{3,2,1,0:T(8,128)} custom-call(s32[3]{0:T(128)S(1)} %pad_add_fusion.me, f32[4,2,64,128]{3,2,1,0:T(8,128)S(1)} %get-tuple-element.32.parts), custom_call_target="tpu_custom_call" | custom-call | tf_op jit(solution)/shard_map/pallas_call | solution.py:416
  (5 shorter events, 0.1 us)
Async XLA Ops:
  0.0 1.0 %copy-start.1 = (f32[2,4,64,128]{3,2,1,0:T(8,128)S(1)}, f32[2,4,64,128]{3,2,1,0:T(8,128)}, u32[]{:S(2)}) copy-start(f32[2,4,64,128]{3,2,1,0:T(8,128)} %rates.3) | copy-start | bytes 786436
  1.0 15.8 %copy-start = (f32[1,2,4,64,128]{4,3,2,1,0:T(8,128)S(1)}, f32[1,2,4,64,128]{4,3,2,1,0:T(8,128)}, u32[]{:S(2)}) copy-start(f32[1,2,4,64,128]{4,3,2,1,0:T(8,128)} %param.6) | copy-start | bytes 786436
  1.1 14.8 %collective-permute-start = (f32[2,2,4,16,128]{4,3,2,1,0:T(8,128)S(1)}, f32[2,2,4,16,128]{4,3,2,1,0:T(8,128)S(1)}, u32[]{:S(2)}, u32[]{:S(2)}) collective-permute-start(f32[2,2,4,16,128]{4,3,2,1,0:T(8,128)S(1)} %pad_maximum_fusion), channel_id=1, source_target_pairs={{8,16},{16,8},{24,32},{32,24},{40,48},{48,40},{56,64},{64,56},{72,... | collective-permute-start | bytes 393224 | tf_op jit(solution)/shard_map/ppermute | solution.py:434
  10.0 6.9 %collective-permute-start.1 = (f32[2,2,4,16,128]{4,3,2,1,0:T(8,128)S(1)}, f32[2,2,4,16,128]{4,3,2,1,0:T(8,128)S(1)}, u32[]{:S(2)}, u32[]{:S(2)}) collective-permute-start(f32[2,2,4,16,128]{4,3,2,1,0:T(8,128)S(1)} %pad_maximum_fusion.1), channel_id=1, source_target_pairs={{0,8},{8,0},{16,24},{24,16},{32,40},{40,32},{48,56},{56,48},{64,72... | collective-permute-start | bytes 393224 | tf_op jit(solution)/shard_map/ppermute | solution.py:434
  17.8 7.4 %collective-permute-start.2 = (f32[2,96,128]{2,1,0:T(8,128)S(1)}, f32[2,96,128]{2,1,0:T(8,128)S(1)}, u32[]{:S(2)}, u32[]{:S(2)}) collective-permute-start(f32[2,96,128]{2,1,0:T(8,128)S(1)} %get-tuple-element.21), channel_id=1, source_target_pairs={{1,2},{2,1},{3,4},{4,3},{5,6},{6,5},{7,0},{0,7},{9,10},{10,9},{11,... | collective-permute-start | bytes 294920 | tf_op jit(solution)/shard_map/ppermute | solution.py:434
  19.7 6.4 %collective-permute-start.3 = (f32[2,96,128]{2,1,0:T(8,128)S(1)}, f32[2,96,128]{2,1,0:T(8,128)S(1)}, u32[]{:S(2)}, u32[]{:S(2)}) collective-permute-start(f32[2,96,128]{2,1,0:T(8,128)S(1)} %get-tuple-element.22), channel_id=1, source_target_pairs={{0,1},{1,0},{2,3},{3,2},{4,5},{5,4},{6,7},{7,6},{8,9},{9,8},{10,11... | collective-permute-start | bytes 294920 | tf_op jit(solution)/shard_map/ppermute | solution.py:434
  57.8 15.3 %collective-permute-start.4 = (f32[6,80,128]{2,1,0:T(8,128)S(1)}, f32[6,80,128]{2,1,0:T(8,128)S(1)}, u32[]{:S(2)}, u32[]{:S(2)}) collective-permute-start(f32[6,80,128]{2,1,0:T(8,128)S(1)} %get-tuple-element.25), channel_id=1, source_target_pairs={{0,896},{128,768},{256,640},{384,512},{1,897},{129,769},{257,641},... | collective-permute-start | bytes 737288 | tf_op jit(solution)/shard_map/ppermute | solution.py:484

commit v7 on v4

--- a/solution.py
+++ b/solution.py
@@ -11,13 +11,12 @@
 HALO = 16
 SUB = 32
 ROWS = 64
-MARGIN = 12
-WIN = ROWS + 2 * MARGIN
-SENT = 80
+WIN = ROWS + 2 * 12
+LATE_WIN = ROWS + 2 * 8
+SENT_TWO = ROWS + 2 * 4
 LANES = 128
 EXT = ROWS + 2 * HALO
 TILES = EXT // 8
-BLOCK = WIN // 8
 
 spread_fast = 0.2
 spread_slow = 0.1
@@ -81,9 +80,8 @@
             wide[1, c, x, rows, :] = jnp.where(lane >= 112, roll(right, 112 - 16 * k, 1), roll(here, -16, 1))
 
 
-def window_tile(wide, c, pair, sub, r, lane):
+def window_tile(wide, c, pair, sub, begin, lane):
     block, moved = ((0, 0), (1, 0), (0, 1), (1, 1))[sub]
-    begin = HALO - MARGIN + 8 * r
     parts = [wide[block, c, x, begin : begin + 8, :] for x in PAIRS[pair]]
     parts[1 - moved] = roll(parts[1 - moved], 64, 1)
     return jnp.where(lane < 64, parts[0], parts[1])
@@ -116,7 +114,22 @@
 
 
 def first_kernel(
-    me, state, rates, y_two, y_one, z_two, z_one, windows, rates_here, wide, wide_rates, coefs, even, odd, slow
+    me,
+    state,
+    rates,
+    y_two,
+    y_one,
+    z_two,
+    z_one,
+    early_windows,
+    late_windows,
+    rates_here,
+    wide,
+    wide_rates,
+    coefs,
+    even,
+    odd,
+    slow,
 ):
     lane = lane_index()
     even_y = me[1] % 2 == 0
@@ -174,33 +187,70 @@
 
     lax.fori_loop(0, 2, block, 0)
 
-    early = me[0] < GROUP
-    for sub in range(GROUP):
-        worker = jnp.where(early, sub, GROUP - 1 - sub)
+    def cut(source, sub, target):
+        rows = target.shape[2]
         for c in range(2):
             for pair in range(2):
-                for r in range(BLOCK):
-                    windows[worker, c, pair, 8 * r : 8 * r + 8, :] = window_tile(wide, c, pair, sub, r, lane)
-
-        @pl.when(worker == me[0] % GROUP)
+                for at in range(0, rows, 8):
+                    begin = (EXT - rows) // 2 + at
+                    target[c, pair, at : at + 8, :] = window_tile(source, c, pair, sub, begin, lane)
+
+    @pl.when(me[0] < GROUP)
+    def _():
+        for sub in range(GROUP):
+            cut(wide, sub, early_windows.at[sub])
+
+    @pl.when(me[0] >= GROUP)
+    def _():
+        for sub in range(GROUP):
+            cut(wide, sub, late_windows.at[GROUP - 1 - sub])
+
+    worker = me[0] % GROUP
+    for sub in range(GROUP):
+
+        @pl.when(jnp.where(me[0] < GROUP, worker, GROUP - 1 - worker) == sub)
         def _():
-            for c in range(2):
-                for pair in range(2):
-                    for r in range(BLOCK):
-                        rates_here[c, pair, 8 * r : 8 * r + 8, :] = window_tile(
-                            wide_rates, c, pair, sub, r, lane
-                        )
+            cut(wide_rates, sub, rates_here)
+
+
+def over(op, count):
+    return [[[op(c, p, j) for j in range(count)] for p in range(2)] for c in range(2)]
 
 
 def load_state(ref):
-    return [[[ref[c, p, j] for j in range(BLOCK)] for p in range(2)] for c in range(2)]
+    return over(lambda c, p, j: ref[c, p, j], ref.shape[2])
 
 
 def save_state(ref, state):
     for c in range(2):
         for p in range(2):
-            for j in range(BLOCK):
-                ref[c, p, j] = state[c][p][j]
+            for j, value in enumerate(state[c][p]):
+                ref[c, p, j] = value
+
+
+def load_window(ref):
+    block = ref.shape[2] // 8
+    return over(lambda c, p, j: ref[c, p, pl.ds(j, 8, stride=block), :], block)
+
+
+def save_window(ref, state):
+    block = ref.shape[2] // 8
+    for c in range(2):
+        for p in range(2):
+            for j, value in enumerate(state[c][p]):
+                ref[c, p, pl.ds(j, 8, stride=block), :] = value
+
+
+def combine(op, left, right):
+    return over(lambda c, p, j: op(left[c][p][j], right[c][p][j]), len(left[0][0]))
+
+
+def add(left, right):
+    return combine(lambda l, r: l + r, left, right)
+
+
+def subtract(left, right):
+    return combine(lambda l, r: l - r, left, right)
 
 
 def neighbours(s, p, j, other):
@@ -209,18 +259,17 @@
         along_x = here + other[j]
     else:
         along_x = other[j] + roll(here, 64, 1)
-    before = s[j - 1] if j > 0 else roll(s[BLOCK - 1], 1, 0)
-    after = s[j + 1] if j < BLOCK - 1 else roll(s[0], -1, 0)
+    before = s[j - 1] if j > 0 else roll(s[-1], 1, 0)
+    after = s[j + 1] if j < len(s) - 1 else roll(s[0], -1, 0)
     along_z = roll(here, 1, 1) + roll(here, -1, 1)
     return (along_x + (before + after)) + along_z
 
 
 def step(state, coefs, which, length):
     a, b = state
-    new_a = [[None] * BLOCK, [None] * BLOCK]
-    new_b = [[None] * BLOCK, [None] * BLOCK]
+    new = [[[], []], [[], []]]
     for p in range(2):
-        for j in range(BLOCK):
+        for j in range(len(a[p])):
             here_a, here_b = a[p][j], b[p][j]
             product = length * (here_a * here_b * here_b)
             near_a = neighbours(a[p], p, j, a[1 - p])
@@ -228,37 +277,20 @@
             keep_a = coefs[which, 0, p, j]
             gain = coefs[which, 1, p, j]
             keep_b = coefs[which, 2, p, j]
-            new_a[p][j] = here_a * keep_a + (length * spread_fast) * near_a + (gain - product)
-            new_b[p][j] = here_b * keep_b + (length * spread_slow) * near_b + product
-    return [new_a, new_b]
-
-
-def combine(op, left, right):
-    return [[[op(left[c][p][j], right[c][p][j]) for j in range(BLOCK)] for p in range(2)] for c in range(2)]
-
-
-def add(left, right):
-    return combine(lambda l, r: l + r, left, right)
-
-
-def subtract(left, right):
-    return combine(lambda l, r: l - r, left, right)
-
-
-def rows_of(j):
-    return pl.ds(j, 8, stride=BLOCK)
-
-
-def load_window(ref):
-    return [[[ref[c, p, rows_of(j), :] for j in range(BLOCK)] for p in range(2)] for c in range(2)]
-
-
-def save_coefs(coefs, rates):
+            new[0][p].append(here_a * keep_a + (length * spread_fast) * near_a + (gain - product))
+            new[1][p].append(here_b * keep_b + (length * spread_slow) * near_b + product)
+    return new
+
+
+def save_coefs(coefs, rates, steps):
+    block = coefs.shape[3]
+    begin = (rates.shape[2] - 8 * block) // 2
     for p in range(2):
-        for j in range(BLOCK):
-            feed = rates[0, p, rows_of(j), :]
-            kill = rates[1, p, rows_of(j), :]
-            for which, length in enumerate((fine_step, coarse_step)):
+        for j in range(block):
+            feed = rates[0, p, pl.ds(begin + j, 8, stride=block), :]
+            kill = rates[1, p, pl.ds(begin + j, 8, stride=block), :]
+            for which in steps:
+                length = (fine_step, coarse_step)[which]
                 for i, value in enumerate(coefs_from(feed, kill, length)):
                     coefs[which, i, p, j] = value
 
@@ -275,13 +307,15 @@
 
 def put(out, rows, m, state):
     lane = lane_index()
+    block = len(state[0][0])
+    begin = (8 * block - ROWS) // 2
     for c in range(2):
-        for j in range(BLOCK):
+        for j in range(block):
             outer, inner = state[c][0][j], state[c][1][j]
             low = jnp.where(lane < 32, roll(outer, -16, 1), roll(inner, 16, 1))
             high = jnp.where(lane < 96, roll(inner, -16, 1), roll(outer, 16, 1))
-            rows[c, rows_of(j), :] = jnp.where(lane < 64, low, high)
-        out[m, c] = rows[c, MARGIN : MARGIN + ROWS, :]
+            rows[c, pl.ds(j, 8, stride=block), :] = jnp.where(lane < 64, low, high)
+        out[m, c] = rows[c, begin : begin + ROWS, :]
 
 
 def sweep(first, windows, coefs, starts, coarse_ends):
@@ -294,10 +328,10 @@
     lax.fori_loop(first, GROUP, turn, 0)
 
 
-def second_terms(first, coefs, starts, coarse_ends):
+def second_terms(first, coefs, starts, coarse_ends, terms):
     def turn(m, carry):
         end = fine(load_state(starts.at[m]), coefs)
-        save_state(starts.at[m], subtract(end, load_state(coarse_ends.at[m])))
+        save_state(terms.at[m], subtract(end, load_state(coarse_ends.at[m])))
         return carry
 
     lax.fori_loop(first, GROUP, turn, 0)
@@ -313,40 +347,73 @@
     lax.fori_loop(first, GROUP, turn, 0)
 
 
-def early_kernel(me, windows, rates, ends, sent, coefs, starts, coarse_ends, current, rows, kept):
+def pack_two(sent, window):
+    lane = lane_index()
+    begin = (window.shape[2] - SENT_TWO) // 2
+    for r in range(0, SENT_TWO, 8):
+        for k in range(3):
+            block = jnp.zeros((8, LANES), jnp.float32)
+            for i in range(3):
+                b = 3 * k + i
+                if b < 8:
+                    c, p, half = b // 4, b // 2 % 2, b % 2
+                    rows = window[c, p, begin + r : begin + r + 8, :]
+                    here = (lane >= 40 * i) & (lane < 40 * i + 40)
+                    block = jnp.where(here, roll(rows, 40 * i - 12 - 64 * half, 1), block)
+            sent[k, r : r + 8, :] = block
+
+
+def unpack_two(sent, window):
+    lane = lane_index()
+    begin = (window.shape[2] - SENT_TWO) // 2
+    for r in range(0, SENT_TWO, 8):
+        for c in range(2):
+            for p in range(2):
+                halves = []
+                for half in range(2):
+                    b = 4 * c + 2 * p + half
+                    rows = sent[b // 3, r : r + 8, :]
+                    halves.append(roll(rows, 12 + 64 * half - 40 * (b % 3), 1))
+                window[c, p, begin + r : begin + r + 8, :] = jnp.where(lane < 64, halves[0], halves[1])
+
+
+def early_first_kernel(me, windows, rates, starts, coarse_ends, sent, coefs, window):
     @pl.when(me[0] < GROUP)
     def _():
-        save_coefs(coefs, rates)
+        save_coefs(coefs, rates, (1,))
         save_state(starts.at[1], load_window(windows.at[0]))
         sweep(1, windows, coefs, starts, coarse_ends)
+        save_window(window, load_state(starts.at[GROUP]))
+        begin = (WIN - LATE_WIN) // 2
+        for c in range(2):
+            for p in range(2):
+                sent[c, p] = window[c, p, begin : begin + LATE_WIN, :]
+
+
+def early_second_kernel(me, starts, coarse_ends, rates, ends, sent, coefs, terms, current, rows, window):
+    @pl.when(me[0] < GROUP)
+    def _():
+        save_coefs(coefs, rates, (0, 1))
         put(ends, rows, 0, load_state(starts.at[1]))
-        pack(sent, 0, kept, load_state(starts.at[GROUP]))
-        second_terms(1, coefs, starts, coarse_ends)
-        state = add(load_state(coarse_ends.at[1]), load_state(starts.at[1]))
+        second_terms(1, coefs, starts, coarse_ends, terms)
+        state = add(load_state(coarse_ends.at[1]), load_state(terms.at[1]))
         put(ends, rows, 1, state)
         save_state(current, state)
-        second_sweep(2, coefs, current, starts, rows, ends)
-        pack(sent, 1, kept, load_state(current))
-
-
-def pack(sent, which, kept, state):
-    for c in range(2):
-        for p in range(2):
-            for j in range(BLOCK):
-                kept[c, p, rows_of(j), :] = state[c][p][j]
-            begin = MARGIN + (ROWS - SENT) // 2
-            sent[which, c, p] = kept[c, p, begin : begin + SENT, :]
-
-
-def unpack(sent, which, kept, target):
-    for c in range(2):
-        for p in range(2):
-            begin = MARGIN + (ROWS - SENT) // 2
-            kept[c, p, begin : begin + SENT, :] = sent[which, c, p]
-    save_state(target, load_window(kept))
-
-
-def late_kernel(me, windows, rates, received, early_ends, ends, coefs, starts, coarse_ends, current, rows, kept):
+        second_sweep(2, coefs, current, terms, rows, ends)
+        save_window(window, load_state(current))
+        pack_two(sent, window)
+
+
+def late_first_kernel(me, windows, rates, received, terms, coefs, starts, coarse_ends):
+    @pl.when(me[0] >= GROUP)
+    def _():
+        save_coefs(coefs, rates, (0, 1))
+        save_state(starts.at[0], load_window(received))
+        sweep(0, windows, coefs, starts, coarse_ends)
+        second_terms(0, coefs, starts, coarse_ends, terms)
+
+
+def late_second_kernel(me, terms, rates, received, early_ends, ends, coefs, current, rows, window):
     @pl.when(me[0] < GROUP)
     def _():
         for m in range(GROUP):
@@ -354,13 +421,11 @@
 
     @pl.when(me[0] >= GROUP)
     def _():
-        save_coefs(coefs, rates)
-        kept[...] = jnp.zeros_like(kept)
-        unpack(received, 0, kept, starts.at[0])
-        unpack(received, 1, kept, current)
-        sweep(0, windows, coefs, starts, coarse_ends)
-        second_terms(0, coefs, starts, coarse_ends)
-        second_sweep(0, coefs, current, starts, rows, ends)
+        save_coefs(coefs, rates, (1,))
+        window[...] = jnp.zeros_like(window)
+        unpack_two(received, window)
+        save_state(current, load_window(window))
+        second_sweep(0, coefs, current, terms, rows, ends)
 
 
 def merge_kernel(me, parts, out):
@@ -378,17 +443,15 @@
                 out[c, x, rows, :] = jnp.where(lane < 64, low, high)
 
 
-def call(kernel, shapes, scratch=(), scalars=0, inputs=pltpu.VMEM):
+def call(kernel, shapes, scratch=(), scalars=0):
     vmem = pl.BlockSpec(memory_space=pltpu.VMEM)
-    given = pl.BlockSpec(memory_space=inputs)
     smem = pl.BlockSpec(memory_space=pltpu.SMEM)
 
     def run(*args):
-        out_shape = [jax.ShapeDtypeStruct(s, jnp.float32) for s in shapes]
         return pl.pallas_call(
             kernel,
-            out_shape=out_shape,
-            in_specs=[smem] * scalars + [given] * (len(args) - scalars),
+            out_shape=[jax.ShapeDtypeStruct(s, jnp.float32) for s in shapes],
+            in_specs=[smem] * scalars + [vmem] * (len(args) - scalars),
             out_specs=[vmem] * len(shapes),
             scratch_shapes=list(scratch),
             compiler_params=pltpu.CompilerParams(vmem_limit_bytes=32 * 1024 * 1024),
@@ -425,9 +488,9 @@
     z_two = swap(two, "gz", 1)
     z_one = swap(one, "gz", 0)
     tile_state = pltpu.VMEM((2, 4, TILES, 8, LANES), jnp.float32)
-    windows, rates_here = call(
+    early_windows, late_windows, rates_here = call(
         first_kernel,
-        [(GROUP, 2, 2, WIN, LANES), (2, 2, WIN, LANES)],
+        [(GROUP, 2, 2, WIN, LANES), (GROUP, 2, 2, LATE_WIN, LANES), (2, 2, WIN, LANES)],
         scratch=[
             pltpu.VMEM((2, 2, 4, EXT, LANES), jnp.float32),
             pltpu.VMEM((2, 2, 4, EXT, LANES), jnp.float32),
@@ -438,26 +501,64 @@
         ],
         scalars=1,
     )(me, state, rates, y_two, y_one, z_two, z_one)
-    windows = lax.all_to_all(windows, "tl", 0, 0)
-
-    scratch = [
-        pltpu.VMEM((2, 3, 2, BLOCK, 8, LANES), jnp.float32),
-        pltpu.VMEM((GROUP + 1, 2, 2, BLOCK, 8, LANES), jnp.float32),
-        pltpu.VMEM((GROUP, 2, 2, BLOCK, 8, LANES), jnp.float32),
-        pltpu.VMEM((2, 2, BLOCK, 8, LANES), jnp.float32),
-        pltpu.VMEM((2, WIN, LANES), jnp.float32),
-        pltpu.VMEM((2, 2, WIN, LANES), jnp.float32),
-    ]
+
+    def exchange(block):
+        return lax.all_to_all(block, "tl", 0, 0)
+
+    def leave(block):
+        return block
+
+    early = slice_index < GROUP
+    last = 2 * GROUP - 1
+    route = [(t, last - t) for t in range(GROUP)]
+
+    def hand_over(block):
+        return lax.ppermute(block, ("th", "tl"), route)
+
+    def states_of(rows):
+        return (2, 2, rows // 8, 8, LANES)
+
+    def scratch_of(rows):
+        coefs = pltpu.VMEM((2, 3, *states_of(rows)[1:]), jnp.float32)
+        current = pltpu.VMEM(states_of(rows), jnp.float32)
+        flat = pltpu.VMEM((2, rows, LANES), jnp.float32)
+        window = pltpu.VMEM((2, 2, rows, LANES), jnp.float32)
+        return coefs, current, flat, window
+
+    coefs, current, flat, window = scratch_of(WIN)
+    starts_shape, slices_shape = (GROUP + 1, *states_of(WIN)), (GROUP, *states_of(WIN))
     ends_shape = (GROUP, 2, ROWS, LANES)
-    early_ends, sent = call(
-        early_kernel, [ends_shape, (2, 2, 2, SENT, LANES)], scratch=scratch, scalars=1
+    windows = lax.cond(early, exchange, leave, early_windows)
+    starts, coarse_ends, sent = call(
+        early_first_kernel,
+        [starts_shape, slices_shape, (2, 2, LATE_WIN, LANES)],
+        scratch=[coefs, window],
+        scalars=1,
     )(me, windows, rates_here)
-    last = 2 * GROUP - 1
-    received = lax.ppermute(sent, ("th", "tl"), [(t, last - t) for t in range(GROUP)])
-    (ends,) = call(late_kernel, [ends_shape], scratch=scratch, scalars=1)(
-        me, windows, rates_here, received, early_ends
+    received_one = hand_over(sent)
+    ends, sent = call(
+        early_second_kernel,
+        [ends_shape, (3, SENT_TWO, LANES)],
+        scratch=[coefs, pltpu.VMEM(slices_shape, jnp.float32), current, flat, window],
+        scalars=1,
+    )(me, starts, coarse_ends, rates_here)
+    received_two = hand_over(sent)
+
+    ends, windows = lax.cond(
+        early, lambda e, w: (exchange(e), w), lambda e, w: (e, exchange(w)), ends, late_windows
     )
-    ends = lax.all_to_all(ends, "tl", 0, 0)
+    coefs, current, flat, window = scratch_of(LATE_WIN)
+    starts_shape, slices_shape = (GROUP + 1, *states_of(LATE_WIN)), (GROUP, *states_of(LATE_WIN))
+    (terms,) = call(
+        late_first_kernel,
+        [slices_shape],
+        scratch=[coefs, pltpu.VMEM(starts_shape, jnp.float32), pltpu.VMEM(slices_shape, jnp.float32)],
+        scalars=1,
+    )(me, windows, rates_here, received_one)
+    (ends,) = call(late_second_kernel, [ends_shape], scratch=[coefs, current, flat, window], scalars=1)(
+        me, terms, rates_here, received_two, ends
+    )
+    ends = lax.cond(early, leave, exchange, ends)
     (out,) = call(merge_kernel, [(2, 4, ROWS, LANES)], scalars=1)(me, ends)
     return out[None]
 

time: 98.3 us -> 84 us (0.85)
  blocking collectives: 40.5 us -> 29.1 us
  waiting for transfers between devices: 19.6 us -> 14.1 us
  Pallas kernels: 11.6 us -> 13.8 us
    ppermute x1 -> x2, waiting for transfers between devices: 13.9 us -> 0.01 us  [hand_over(): return lax.ppermute(block, ('th', 'tl'), route)]
    all_to_all x2 -> x1, blocking collectives: 40.5 us -> 29.1 us  [exchange(): return lax.all_to_all(block, 'tl', 0, 0)]
    all_to_all x0 -> x1, waiting for transfers between devices: none -> 8.32 us  [exchange(): return lax.all_to_all(block, 'tl', 0, 0)]
    ppermute x1 -> x2, starting transfers between devices: 6.83 us -> 2.58 us  [hand_over(): return lax.ppermute(block, ('th', 'tl'), route)]
    all_to_all x0 -> x1, starting transfers between devices: none -> 3.42 us  [exchange(): return lax.all_to_all(block, 'tl', 0, 0)]
    pallas_call x5 -> x7, Pallas kernels: 11.6 us -> 13.8 us  [run(): pl.pallas_call(kernel, out_shape=[jax.ShapeDtypeStruct(s, jnp.float32) fo...]
  transfers between devices with their start and end apart: 5 -> 7, of which waited for: 4 -> 4; matrix products, arithmetic and copies ran while one was open for 0% -> 1% of each run, Pallas kernels for 0% -> 5%
where the time goes in v7:
time: 84 us; the launch traced here: 83.3 us
  blocking collectives  29.1 us (35%)
  starting transfers between devices  24.2 us (29%)
  waiting for transfers between devices  14.1 us (17%)
  Pallas kernels  13.8 us (16%)
  local copies, waits for them, and re-layouts  1.78 us (2%)
    all_to_all x1, blocking collectives, exchange(): return lax.all_to_all(block, 'tl', 0, 0)  29.1 us
    ppermute x4, starting transfers between devices, swap(): return lax.ppermute(block, axis, route)  18.2 us
    pallas_call x7, Pallas kernels, run(): pl.pallas_call(kernel, out_shape=[jax.ShapeDtypeStruct(s, jnp.float32) fo...  13.8 us
    all_to_all x1, waiting for transfers between devices, exchange(): return lax.all_to_all(block, 'tl', 0, 0)  8.32 us
    ppermute x4, waiting for transfers between devices, swap(): return lax.ppermute(block, axis, route)  5.76 us
    all_to_all x1, starting transfers between devices, exchange(): return lax.all_to_all(block, 'tl', 0, 0)  3.42 us
    ppermute x2, starting transfers between devices, hand_over(): return lax.ppermute(block, ('th', 'tl'), route)  2.58 us
  transfers between devices with their start and end apart: 7, of which 4 were waited for; matrix products, arithmetic and copies ran while one was open for 1% of the time, Pallas kernels for 5%

profile of v7, /device:TPU:14, one launch (start us, length us, event | category | flops | bytes accessed | tf_op | source)
XLA Modules:
  0.0 83.3 jit_solution(1835019301851324510)
XLA Ops:
  0.0 0.0 copy-start.1
  0.0 0.9 %constant_dynamic-slice_fusion = (f32[1,2,4,16,128]{4,3,2,1,0:T(8,128)S(1)}, f32[1,2,4,16,128]{4,3,2,1,0:T(8,128)S(1)}) fusion(f32[1,2,4,64,128]{4,3,2,1,0:T(8,128)} %param.8, s32[]{:T(128)S(6)} %select_n.17, s32[]{:T(128)S(6)} %select_n.16), kind=kLoop, calls=%fused_computation.4 | loop fusion | bytes 262152 | tf_op jit(solution)/shard_map/dynamic_slice | solution.py:473
  0.9 0.1 copy-done.1
  1.0 0.0 copy-start
  1.1 8.9 %collective-permute-start = (f32[2,2,4,16,128]{4,3,2,1,0:T(8,128)S(1)}, f32[2,2,4,16,128]{4,3,2,1,0:T(8,128)S(1)}, u32[]{:S(2)}, u32[]{:S(2)}) collective-permute-start(f32[2,2,4,16,128]{4,3,2,1,0:T(8,128)S(1)} %pad_maximum_fusion), channel_id=1, source_target_pairs={{8,16},{16,8},{24,32},{32,24},{40,48},{48,40},{56,64},{64,56},{72,... | collective-permute-start | bytes 393224 | tf_op jit(solution)/shard_map/ppermute | solution.py:469
  10.0 1.9 %collective-permute-start.1 = (f32[2,2,4,16,128]{4,3,2,1,0:T(8,128)S(1)}, f32[2,2,4,16,128]{4,3,2,1,0:T(8,128)S(1)}, u32[]{:S(2)}, u32[]{:S(2)}) collective-permute-start(f32[2,2,4,16,128]{4,3,2,1,0:T(8,128)S(1)} %pad_maximum_fusion.1), channel_id=1, source_target_pairs={{0,8},{8,0},{16,24},{24,16},{32,40},{40,32},{48,56},{56,48},{64,72... | collective-permute-start | bytes 393224 | tf_op jit(solution)/shard_map/ppermute | solution.py:469
  11.9 0.1 pad_add_fusion.me
  12.0 3.9 %collective-permute-done.y_two = f32[2,2,4,16,128]{4,3,2,1,0:T(8,128)S(1)} collective-permute-done((f32[2,2,4,16,128]{4,3,2,1,0:T(8,128)S(1)}, f32[2,2,4,16,128]{4,3,2,1,0:T(8,128)S(1)}, u32[]{:S(2)}, u32[]{:S(2)}) %collective-permute-start) | collective-permute-done | bytes 131104 | tf_op jit(solution)/shard_map/ppermute | solution.py:469
  15.9 0.9 %collective-permute-done.1.y_one = f32[2,2,4,16,128]{4,3,2,1,0:T(8,128)S(1)} collective-permute-done((f32[2,2,4,16,128]{4,3,2,1,0:T(8,128)S(1)}, f32[2,2,4,16,128]{4,3,2,1,0:T(8,128)S(1)}, u32[]{:S(2)}, u32[]{:S(2)}) %collective-permute-start.1) | collective-permute-done | bytes 131104 | tf_op jit(solution)/shard_map/ppermute | solution.py:469
  16.8 0.0 copy-done
  16.8 1.0 %shard_map.28 = (f32[2,96,128]{2,1,0:T(8,128)S(1)}, f32[2,96,128]{2,1,0:T(8,128)S(1)}) custom-call(s32[3]{0:T(128)S(1)} %pad_add_fusion.me, f32[2,4,64,128]{3,2,1,0:T(8,128)S(1)} %bitcast.9, f32[2,4,64,128]{3,2,1,0:T(8,128)S(1)} %copy-done.1, f32[2,2,4,16,128]{4,3,2,1,0:T(8,128)S(1)} %collective-permute-done.y_two, ...), custom_call_target="tpu_custom_call" | custom-call | tf_op jit(solution)/shard_map/pallas_call | solution.py:451
  17.8 1.9 %collective-permute-start.2 = (f32[2,96,128]{2,1,0:T(8,128)S(1)}, f32[2,96,128]{2,1,0:T(8,128)S(1)}, u32[]{:S(2)}, u32[]{:S(2)}) collective-permute-start(f32[2,96,128]{2,1,0:T(8,128)S(1)} %get-tuple-element.39), channel_id=1, source_target_pairs={{1,2},{2,1},{3,4},{4,3},{5,6},{6,5},{7,0},{0,7},{9,10},{10,9},{11,... | collective-permute-start | bytes 294920 | tf_op jit(solution)/shard_map/ppermute | solution.py:469
  19.7 5.4 %collective-permute-start.3 = (f32[2,96,128]{2,1,0:T(8,128)S(1)}, f32[2,96,128]{2,1,0:T(8,128)S(1)}, u32[]{:S(2)}, u32[]{:S(2)}) collective-permute-start(f32[2,96,128]{2,1,0:T(8,128)S(1)} %get-tuple-element.40), channel_id=1, source_target_pairs={{0,1},{1,0},{2,3},{3,2},{4,5},{5,4},{6,7},{7,6},{8,9},{9,8},{10,11... | collective-permute-start | bytes 294920 | tf_op jit(solution)/shard_map/ppermute | solution.py:469
  25.2 0.0 collective-permute-done.2.z_two
  25.2 0.9 %collective-permute-done.3.z_one = f32[2,96,128]{2,1,0:T(8,128)S(1)} collective-permute-done((f32[2,96,128]{2,1,0:T(8,128)S(1)}, f32[2,96,128]{2,1,0:T(8,128)S(1)}, u32[]{:S(2)}, u32[]{:S(2)}) %collective-permute-start.3) | collective-permute-done | bytes 98336 | tf_op jit(solution)/shard_map/ppermute | solution.py:469
  26.1 4.6 %shard_map.29 = (f32[4,2,2,88,128]{4,3,2,1,0:T(8,128)S(1)}, f32[4,2,2,80,128]{4,3,2,1,0:T(8,128)S(1)}, f32[2,2,88,128]{3,2,1,0:T(8,128)S(1)}) custom-call(s32[3]{0:T(128)S(1)} %pad_add_fusion.me, f32[2,4,64,128]{3,2,1,0:T(8,128)S(1)} %bitcast.10, f32[2,4,64,128]{3,2,1,0:T(8,128)S(1)} %copy-done.1, f32[2,2,4,16,128]{4,3,2,1,0:T(8,128)S(1)} %collective-permute-done.y_two, ...), custom_call_target="tpu_custom_call" | custom-call | tf_op jit(solution)/shard_map/pallas_call | solution.py:451
  30.7 29.2 %conditional.3 = (f32[4,2,2,88,128]{4,3,2,1,0:T(8,128)S(1)}) conditional(s32[]{:T(128)} %convert_element_type.2, f32[4,2,2,88,128]{4,3,2,1,0:T(8,128)S(1)} %get-tuple-element.42, f32[4,2,2,88,128]{4,3,2,1,0:T(8,128)S(1)} %get-tuple-element.42), branch_computations={%region_0.1_spmd, %region_1.2_spmd} | conditional | bytes 2883592 | solution.py:531
  30.8 29.1 %all_to_all.16 = f32[4,2,2,88,128]{4,3,2,1,0:T(8,128)S(1)} all-to-all(f32[4,2,2,88,128]{4,3,2,1,0:T(8,128)S(1)} %copy.11), channel_id=1, replica_groups=mesh['th'=2,'tl'=4,'gy'=16,'gz'=8] {'tl'}, dimensions={0} | all-to-all | bytes 1441792 | tf_op jit(solution)/shard_map/cond/branch_1_fun/all_to_all | solution.py:506
  59.9 1.2 %shard_map.30 = (f32[5,2,2,11,8,128]{5,4,3,2,1,0:T(8,128)S(1)}, f32[4,2,2,11,8,128]{5,4,3,2,1,0:T(8,128)S(1)}, f32[2,2,80,128]{3,2,1,0:T(8,128)S(1)}) custom-call(s32[3]{0:T(128)S(1)} %pad_add_fusion.me, f32[4,2,2,88,128]{4,3,2,1,0:T(8,128)S(1)} %get-tuple-element.59.windows, f32[2,2,88,128]{3,2,1,0:T(8,128)S(1)} %get-tuple-element.43.rates), custom_call_target="tpu_custom_call" | custom-call | tf_op jit(solution)/shard_map/pallas_call | solution.py:451
  61.1 1.3 %collective-permute-start.4 = (f32[2,2,80,128]{3,2,1,0:T(8,128)S(1)}, f32[2,2,80,128]{3,2,1,0:T(8,128)S(1)}, u32[]{:S(2)}, u32[]{:S(2)}) collective-permute-start(f32[2,2,80,128]{3,2,1,0:T(8,128)S(1)} %get-tuple-element.48), channel_id=1, source_target_pairs={{0,896},{128,768},{256,640},{384,512},{1,897},{129,769},{257,641},... | collective-permute-start | bytes 491528 | tf_op jit(solution)/shard_map/ppermute | solution.py:516
  62.4 4.0 %shard_map.31 = (f32[4,2,64,128]{3,2,1,0:T(8,128)}, f32[3,72,128]{2,1,0:T(8,128)S(1)}) custom-call(s32[3]{0:T(128)S(1)} %pad_add_fusion.me, f32[5,2,2,11,8,128]{5,4,3,2,1,0:T(8,128)S(1)} %get-tuple-element.44.starts, f32[4,2,2,11,8,128]{5,4,3,2,1,0:T(8,128)S(1)} %get-tuple-element.45.coarse_ends, f32[2,2,88,128]{3,2,1,0:T(8,128)S(1)} %get-tuple-element.43.rates), custom_call_target="tpu_custom_call" | custom-call | tf_op jit(solution)/shard_map/pallas_call | solution.py:451
  66.4 1.3 %collective-permute-start.5 = (f32[3,72,128]{2,1,0:T(8,128)S(1)}, f32[3,72,128]{2,1,0:T(8,128)S(1)}, u32[]{:S(2)}, u32[]{:S(2)}) collective-permute-start(f32[3,72,128]{2,1,0:T(8,128)S(1)} %get-tuple-element.49), channel_id=1, source_target_pairs={{0,896},{128,768},{256,640},{384,512},{1,897},{129,769},{257,641},... | collective-permute-start | bytes 331784 | tf_op jit(solution)/shard_map/ppermute | solution.py:516
  67.7 12.5 %conditional.4 = (f32[4,2,64,128]{3,2,1,0:T(8,128)}, f32[4,2,2,80,128]{4,3,2,1,0:T(8,128)S(1)}) conditional(s32[]{:T(128)} %convert_element_type.2, (f32[4,2,2,80,128]{4,3,2,1,0:T(8,128)S(1)}, f32[4,2,64,128]{3,2,1,0:T(8,128)}) %tuple.25, (f32[4,2,64,128]{3,2,1,0:T(8,128)}, f32[4,2,2,80,128]{4,3,2,1,0:T(8,128)S(1)}) %tuple.26), branch_computations={%region_2.3_spmd, %region_3.4_spmd} | conditional | bytes 2621456 | solution.py:547
  67.7 3.4 %all-to-all-start.2 = ((f32[4,2,64,128]{3,2,1,0:T(8,128)}), f32[4,2,64,128]{3,2,1,0:T(8,128)S(1)}, u32[]{:S(2)}, u32[]{:S(2)}) async-start(f32[4,2,64,128]{3,2,1,0:T(8,128)} %get-tuple-element.25), calls=%async_computation.2 | async-start | bytes 524288 | tf_op jit(solution)/shard_map/cond/branch_1_fun/all_to_all | solution.py:506
  71.2 8.3 %all-to-all-done.2 = f32[4,2,64,128]{3,2,1,0:T(8,128)S(1)} async-done(((f32[4,2,64,128]{3,2,1,0:T(8,128)}), f32[4,2,64,128]{3,2,1,0:T(8,128)S(1)}, u32[]{:S(2)}, u32[]{:S(2)}) %all-to-all-start.2) | async-done | bytes 262176 | tf_op jit(solution)/shard_map/cond/branch_1_fun/all_to_all | solution.py:506
  79.5 0.7 copy.7
  80.2 0.0 collective-permute-done.4.received
  80.2 0.5 shard_map.32.terms
  80.7 0.0 collective-permute-done.5.received
  80.8 1.0 %shard_map.33 = f32[4,2,64,128]{3,2,1,0:T(8,128)S(1)} custom-call(s32[3]{0:T(128)S(1)} %pad_add_fusion.me, f32[4,2,2,10,8,128]{5,4,3,2,1,0:T(8,128)S(1)} %shard_map.32.terms, f32[2,2,88,128]{3,2,1,0:T(8,128)S(1)} %get-tuple-element.43.rates, f32[3,72,128]{2,1,0:T(8,128)S(1)} %collective-permute-done.5.received, f32[4,2,64,128]{3,2,1,0:T(8,128)} %get-tuple-element.50.early_ends), custom_call_target="tpu_custom_call" | custom-call | tf_op jit(solution)/shard_map/pallas_call | solution.py:451
  81.8 1.5 %shard_map.34 = f32[2,4,64,128]{3,2,1,0:T(8,128)} custom-call(s32[3]{0:T(128)S(1)} %pad_add_fusion.me, f32[4,2,64,128]{3,2,1,0:T(8,128)S(1)} %get-tuple-element.60.parts), custom_call_target="tpu_custom_call" | custom-call | tf_op jit(solution)/shard_map/pallas_call | solution.py:451
  (5 shorter events, 0.1 us)
Async XLA Ops:
  0.0 1.0 %copy-start.1 = (f32[2,4,64,128]{3,2,1,0:T(8,128)S(1)}, f32[2,4,64,128]{3,2,1,0:T(8,128)}, u32[]{:S(2)}) copy-start(f32[2,4,64,128]{3,2,1,0:T(8,128)} %rates.3) | copy-start | bytes 786436
  1.0 15.8 %copy-start = (f32[1,2,4,64,128]{4,3,2,1,0:T(8,128)S(1)}, f32[1,2,4,64,128]{4,3,2,1,0:T(8,128)}, u32[]{:S(2)}) copy-start(f32[1,2,4,64,128]{4,3,2,1,0:T(8,128)} %param.8) | copy-start | bytes 786436
  1.1 14.8 %collective-permute-start = (f32[2,2,4,16,128]{4,3,2,1,0:T(8,128)S(1)}, f32[2,2,4,16,128]{4,3,2,1,0:T(8,128)S(1)}, u32[]{:S(2)}, u32[]{:S(2)}) collective-permute-start(f32[2,2,4,16,128]{4,3,2,1,0:T(8,128)S(1)} %pad_maximum_fusion), channel_id=1, source_target_pairs={{8,16},{16,8},{24,32},{32,24},{40,48},{48,40},{56,64},{64,56},{72,... | collective-permute-start | bytes 393224 | tf_op jit(solution)/shard_map/ppermute | solution.py:469
  10.0 6.9 %collective-permute-start.1 = (f32[2,2,4,16,128]{4,3,2,1,0:T(8,128)S(1)}, f32[2,2,4,16,128]{4,3,2,1,0:T(8,128)S(1)}, u32[]{:S(2)}, u32[]{:S(2)}) collective-permute-start(f32[2,2,4,16,128]{4,3,2,1,0:T(8,128)S(1)} %pad_maximum_fusion.1), channel_id=1, source_target_pairs={{0,8},{8,0},{16,24},{24,16},{32,40},{40,32},{48,56},{56,48},{64,72... | collective-permute-start | bytes 393224 | tf_op jit(solution)/shard_map/ppermute | solution.py:469
  17.8 7.4 %collective-permute-start.2 = (f32[2,96,128]{2,1,0:T(8,128)S(1)}, f32[2,96,128]{2,1,0:T(8,128)S(1)}, u32[]{:S(2)}, u32[]{:S(2)}) collective-permute-start(f32[2,96,128]{2,1,0:T(8,128)S(1)} %get-tuple-element.39), channel_id=1, source_target_pairs={{1,2},{2,1},{3,4},{4,3},{5,6},{6,5},{7,0},{0,7},{9,10},{10,9},{11,... | collective-permute-start | bytes 294920 | tf_op jit(solution)/shard_map/ppermute | solution.py:469
  19.7 6.4 %collective-permute-start.3 = (f32[2,96,128]{2,1,0:T(8,128)S(1)}, f32[2,96,128]{2,1,0:T(8,128)S(1)}, u32[]{:S(2)}, u32[]{:S(2)}) collective-permute-start(f32[2,96,128]{2,1,0:T(8,128)S(1)} %get-tuple-element.40), channel_id=1, source_target_pairs={{0,1},{1,0},{2,3},{3,2},{4,5},{5,4},{6,7},{7,6},{8,9},{9,8},{10,11... | collective-permute-start | bytes 294920 | tf_op jit(solution)/shard_map/ppermute | solution.py:469
  61.1 19.1 %collective-permute-start.4 = (f32[2,2,80,128]{3,2,1,0:T(8,128)S(1)}, f32[2,2,80,128]{3,2,1,0:T(8,128)S(1)}, u32[]{:S(2)}, u32[]{:S(2)}) collective-permute-start(f32[2,2,80,128]{3,2,1,0:T(8,128)S(1)} %get-tuple-element.48), channel_id=1, source_target_pairs={{0,896},{128,768},{256,640},{384,512},{1,897},{129,769},{257,641},... | collective-permute-start | bytes 491528 | tf_op jit(solution)/shard_map/ppermute | solution.py:516
  66.4 14.3 %collective-permute-start.5 = (f32[3,72,128]{2,1,0:T(8,128)S(1)}, f32[3,72,128]{2,1,0:T(8,128)S(1)}, u32[]{:S(2)}, u32[]{:S(2)}) collective-permute-start(f32[3,72,128]{2,1,0:T(8,128)S(1)} %get-tuple-element.49), channel_id=1, source_target_pairs={{0,896},{128,768},{256,640},{384,512},{1,897},{129,769},{257,641},... | collective-permute-start | bytes 331784 | tf_op jit(solution)/shard_map/ppermute | solution.py:516
  67.7 11.7 %all-to-all-start.2 = ((f32[4,2,64,128]{3,2,1,0:T(8,128)}), f32[4,2,64,128]{3,2,1,0:T(8,128)S(1)}, u32[]{:S(2)}, u32[]{:S(2)}) async-start(f32[4,2,64,128]{3,2,1,0:T(8,128)} %get-tuple-element.25), calls=%async_computation.2 | async-start | bytes 524288 | tf_op jit(solution)/shard_map/cond/branch_1_fun/all_to_all | solution.py:506

commit v8 on v7

--- a/solution.py
+++ b/solution.py
@@ -13,7 +13,7 @@
 ROWS = 64
 WIN = ROWS + 2 * 12
 LATE_WIN = ROWS + 2 * 8
-SENT_TWO = ROWS + 2 * 4
+SENT = LATE_WIN
 LANES = 128
 EXT = ROWS + 2 * HALO
 TILES = EXT // 8
@@ -76,34 +76,41 @@
         for k in range(8):
             c, x = k // 4, k % 4
             here = ext_tile(y_one.at[c, x], y_two.at[c, x], own.at[c, x], even_y, tile)
-            wide[0, c, x, rows, :] = jnp.where(lane < 16, roll(left, -16 * k, 1), roll(here, 16, 1))
-            wide[1, c, x, rows, :] = jnp.where(lane >= 112, roll(right, 112 - 16 * k, 1), roll(here, -16, 1))
+            wide[0, c, x, rows, :] = jnp.where(lane >= 112, roll(left, 112 - 16 * k, 1), here)
+            wide[1, c, x, rows, :] = jnp.where(lane < 16, roll(right, -16 * k, 1), here)
 
 
 def window_tile(wide, c, pair, sub, begin, lane):
-    block, moved = ((0, 0), (1, 0), (0, 1), (1, 1))[sub]
-    parts = [wide[block, c, x, begin : begin + 8, :] for x in PAIRS[pair]]
-    parts[1 - moved] = roll(parts[1 - moved], 64, 1)
-    return jnp.where(lane < 64, parts[0], parts[1])
+    block = (0, 1, 0, 1)[sub]
+    low, high = [
+        roll(wide[block, c, x, begin : begin + 8, :], 64 * half + HALO - SUB * sub, 1)
+        for half, x in enumerate(PAIRS[pair])
+    ]
+    return jnp.where(lane < 64, low, high)
 
 
 def tile_step(source, target, coefs_of, length):
-    for x in range(4):
-        for j in range(TILES):
-            keep_a, gain, keep_b = coefs_of(x, j)
-            here = [source[c, x, j] for c in range(2)]
+    def row(j):
+        return [[source[c, x, j % TILES] for x in range(4)] for c in range(2)]
+
+    first, final = row(0), row(TILES - 1)
+    before, here = final, first
+    for j in range(TILES):
+        after = (row(j + 1) if j < TILES - 2 else final) if j < TILES - 1 else first
+        for x in range(4):
             near = []
             for c in range(2):
-                below = source[c, max(x - 1, 0), j]
-                above = source[c, min(x + 1, 3), j]
-                before = source[c, x, j - 1] if j > 0 else roll(source[c, x, TILES - 1], 1, 0)
-                after = source[c, x, j + 1] if j < TILES - 1 else roll(source[c, x, 0], -1, 0)
-                along_z = roll(here[c], 1, 1) + roll(here[c], -1, 1)
-                near.append(((below + above) + (before + after)) + along_z)
-            a, b = here
+                lower = roll(before[c][x], 1, 0) if j == 0 else before[c][x]
+                upper = roll(after[c][x], -1, 0) if j == TILES - 1 else after[c][x]
+                along_x = here[c][max(x - 1, 0)] + here[c][min(x + 1, 3)]
+                along_z = roll(here[c][x], 1, 1) + roll(here[c][x], -1, 1)
+                near.append((along_x + (lower + upper)) + along_z)
+            a, b = here[0][x], here[1][x]
+            keep_a, gain, keep_b = coefs_of(x, j)
             product = length * (a * b * b)
             target[0, x, j] = a * keep_a + (length * spread_fast) * near[0] + (gain - product)
             target[1, x, j] = b * keep_b + (length * spread_slow) * near[1] + product
+        before, here = here, after
 
 
 def coefs_from(feed, kill, length):
@@ -282,15 +289,14 @@
     return new
 
 
-def save_coefs(coefs, rates, steps):
+def save_coefs(coefs, rates):
     block = coefs.shape[3]
     begin = (rates.shape[2] - 8 * block) // 2
     for p in range(2):
         for j in range(block):
             feed = rates[0, p, pl.ds(begin + j, 8, stride=block), :]
             kill = rates[1, p, pl.ds(begin + j, 8, stride=block), :]
-            for which in steps:
-                length = (fine_step, coarse_step)[which]
+            for which, length in enumerate((fine_step, coarse_step)):
                 for i, value in enumerate(coefs_from(feed, kill, length)):
                     coefs[which, i, p, j] = value
 
@@ -347,85 +353,68 @@
     lax.fori_loop(first, GROUP, turn, 0)
 
 
-def pack_two(sent, window):
+def between(lane, begin, end):
+    return (lane >= begin) & (lane < end)
+
+
+def pack(sent, one, two):
     lane = lane_index()
-    begin = (window.shape[2] - SENT_TWO) // 2
-    for r in range(0, SENT_TWO, 8):
-        for k in range(3):
-            block = jnp.zeros((8, LANES), jnp.float32)
-            for i in range(3):
-                b = 3 * k + i
-                if b < 8:
-                    c, p, half = b // 4, b // 2 % 2, b % 2
-                    rows = window[c, p, begin + r : begin + r + 8, :]
-                    here = (lane >= 40 * i) & (lane < 40 * i + 40)
-                    block = jnp.where(here, roll(rows, 40 * i - 12 - 64 * half, 1), block)
-            sent[k, r : r + 8, :] = block
-
-
-def unpack_two(sent, window):
+    begin = (one.shape[2] - SENT) // 2
+    for r in range(0, SENT, 8):
+        rows, there = slice(r, r + 8), slice(begin + r, begin + r + 8)
+        for k in range(4):
+            second = two[k // 2, k % 2, there, :]
+            half = k % 2
+            first = roll(one[0, k // 2, there, :], 93 - (64 * half + 9), 1)
+            block = jnp.where(between(lane, 52, 92), roll(second, -24, 1), first)
+            sent[k, rows, :] = jnp.where(between(lane, 12, 52), second, block)
+        for p in range(2):
+            sent[4 + p, rows, :] = one[1, p, there, :]
+
+
+def unpack(sent, one, two):
     lane = lane_index()
-    begin = (window.shape[2] - SENT_TWO) // 2
-    for r in range(0, SENT_TWO, 8):
-        for c in range(2):
-            for p in range(2):
-                halves = []
-                for half in range(2):
-                    b = 4 * c + 2 * p + half
-                    rows = sent[b // 3, r : r + 8, :]
-                    halves.append(roll(rows, 12 + 64 * half - 40 * (b % 3), 1))
-                window[c, p, begin + r : begin + r + 8, :] = jnp.where(lane < 64, halves[0], halves[1])
-
-
-def early_first_kernel(me, windows, rates, starts, coarse_ends, sent, coefs, window):
+    begin = (one.shape[2] - SENT) // 2
+    for r in range(0, SENT, 8):
+        rows, there = slice(r, r + 8), slice(begin + r, begin + r + 8)
+        blocks = [sent[k, rows, :] for k in range(4)]
+        for k in range(4):
+            two[k // 2, k % 2, there, :] = jnp.where(lane < 64, blocks[k], roll(blocks[k], 24, 1))
+        for p in range(2):
+            low, high = roll(blocks[2 * p], 9 - 93, 1), roll(blocks[2 * p + 1], 64 + 9 - 93, 1)
+            one[0, p, there, :] = jnp.where(lane < 64, low, high)
+            one[1, p, there, :] = sent[4 + p, rows, :]
+
+
+def early_kernel(
+    me, windows, rates, ends, sent, coefs, starts, coarse_ends, terms, current, rows, one, two
+):
     @pl.when(me[0] < GROUP)
     def _():
-        save_coefs(coefs, rates, (1,))
+        save_coefs(coefs, rates)
         save_state(starts.at[1], load_window(windows.at[0]))
         sweep(1, windows, coefs, starts, coarse_ends)
-        save_window(window, load_state(starts.at[GROUP]))
-        begin = (WIN - LATE_WIN) // 2
-        for c in range(2):
-            for p in range(2):
-                sent[c, p] = window[c, p, begin : begin + LATE_WIN, :]
-
-
-def early_second_kernel(me, starts, coarse_ends, rates, ends, sent, coefs, terms, current, rows, window):
-    @pl.when(me[0] < GROUP)
-    def _():
-        save_coefs(coefs, rates, (0, 1))
         put(ends, rows, 0, load_state(starts.at[1]))
+        save_window(one, load_state(starts.at[GROUP]))
         second_terms(1, coefs, starts, coarse_ends, terms)
         state = add(load_state(coarse_ends.at[1]), load_state(terms.at[1]))
         put(ends, rows, 1, state)
         save_state(current, state)
         second_sweep(2, coefs, current, terms, rows, ends)
-        save_window(window, load_state(current))
-        pack_two(sent, window)
-
-
-def late_first_kernel(me, windows, rates, received, terms, coefs, starts, coarse_ends):
-    @pl.when(me[0] >= GROUP)
-    def _():
-        save_coefs(coefs, rates, (0, 1))
-        save_state(starts.at[0], load_window(received))
-        sweep(0, windows, coefs, starts, coarse_ends)
-        second_terms(0, coefs, starts, coarse_ends, terms)
-
-
-def late_second_kernel(me, terms, rates, received, early_ends, ends, coefs, current, rows, window):
-    @pl.when(me[0] < GROUP)
-    def _():
-        for m in range(GROUP):
-            ends[m] = early_ends[m]
-
-    @pl.when(me[0] >= GROUP)
-    def _():
-        save_coefs(coefs, rates, (1,))
-        window[...] = jnp.zeros_like(window)
-        unpack_two(received, window)
-        save_state(current, load_window(window))
-        second_sweep(0, coefs, current, terms, rows, ends)
+        save_window(two, load_state(current))
+        pack(sent, one, two)
+
+
+def late_kernel(
+    windows, rates, received, ends, coefs, starts, coarse_ends, terms, current, rows, one, two
+):
+    save_coefs(coefs, rates)
+    unpack(received, one, two)
+    save_state(starts.at[0], load_window(one))
+    save_state(current, load_window(two))
+    sweep(0, windows, coefs, starts, coarse_ends)
+    second_terms(0, coefs, starts, coarse_ends, terms)
+    second_sweep(0, coefs, current, terms, rows, ends)
 
 
 def merge_kernel(me, parts, out):
@@ -515,52 +504,37 @@
     def hand_over(block):
         return lax.ppermute(block, ("th", "tl"), route)
 
-    def states_of(rows):
-        return (2, 2, rows // 8, 8, LANES)
-
     def scratch_of(rows):
-        coefs = pltpu.VMEM((2, 3, *states_of(rows)[1:]), jnp.float32)
-        current = pltpu.VMEM(states_of(rows), jnp.float32)
+        states = (2, 2, rows // 8, 8, LANES)
+        coefs = pltpu.VMEM((2, 3, *states[1:]), jnp.float32)
+        starts = pltpu.VMEM((GROUP + 1, *states), jnp.float32)
+        slices = pltpu.VMEM((GROUP, *states), jnp.float32)
+        current = pltpu.VMEM(states, jnp.float32)
         flat = pltpu.VMEM((2, rows, LANES), jnp.float32)
         window = pltpu.VMEM((2, 2, rows, LANES), jnp.float32)
-        return coefs, current, flat, window
-
-    coefs, current, flat, window = scratch_of(WIN)
-    starts_shape, slices_shape = (GROUP + 1, *states_of(WIN)), (GROUP, *states_of(WIN))
+        return [coefs, starts, slices, slices, current, flat, window, window]
+
     ends_shape = (GROUP, 2, ROWS, LANES)
     windows = lax.cond(early, exchange, leave, early_windows)
-    starts, coarse_ends, sent = call(
-        early_first_kernel,
-        [starts_shape, slices_shape, (2, 2, LATE_WIN, LANES)],
-        scratch=[coefs, window],
-        scalars=1,
-    )(me, windows, rates_here)
-    received_one = hand_over(sent)
-    ends, sent = call(
-        early_second_kernel,
-        [ends_shape, (3, SENT_TWO, LANES)],
-        scratch=[coefs, pltpu.VMEM(slices_shape, jnp.float32), current, flat, window],
-        scalars=1,
-    )(me, starts, coarse_ends, rates_here)
-    received_two = hand_over(sent)
-
-    ends, windows = lax.cond(
+    ends, sent = call(early_kernel, [ends_shape, (6, SENT, LANES)], scratch=scratch_of(WIN), scalars=1)(
+        me, windows, rates_here
+    )
+    received = hand_over(sent)
+    parts, windows = lax.cond(
         early, lambda e, w: (exchange(e), w), lambda e, w: (e, exchange(w)), ends, late_windows
     )
-    coefs, current, flat, window = scratch_of(LATE_WIN)
-    starts_shape, slices_shape = (GROUP + 1, *states_of(LATE_WIN)), (GROUP, *states_of(LATE_WIN))
-    (terms,) = call(
-        late_first_kernel,
-        [slices_shape],
-        scratch=[coefs, pltpu.VMEM(starts_shape, jnp.float32), pltpu.VMEM(slices_shape, jnp.float32)],
-        scalars=1,
-    )(me, windows, rates_here, received_one)
-    (ends,) = call(late_second_kernel, [ends_shape], scratch=[coefs, current, flat, window], scalars=1)(
-        me, terms, rates_here, received_two, ends
-    )
-    ends = lax.cond(early, leave, exchange, ends)
-    (out,) = call(merge_kernel, [(2, 4, ROWS, LANES)], scalars=1)(me, ends)
-    return out[None]
+
+    def merge(parts):
+        return call(merge_kernel, [(2, 4, ROWS, LANES)], scalars=1)(me, parts)[0]
+
+    def end_early(parts, windows, received):
+        return merge(parts)
+
+    def end_late(parts, windows, received):
+        (ends,) = call(late_kernel, [ends_shape], scratch=scratch_of(LATE_WIN))(windows, rates_here, received)
+        return merge(exchange(ends))
+
+    return lax.cond(early, end_early, end_late, parts, windows, received)[None]
 
 
 def solution(mesh):

time: 84 us -> 86.3 us (1.027)
  the two profiles are of different devices: /device:TPU:14 before, /device:TPU:638 now
where the time goes in v8:
time: 86.3 us; the launch traced here: 85.9 us
  blocking collectives  35.9 us (42%)
  waiting for transfers between devices  20.8 us (24%)
  starting transfers between devices  15.6 us (18%)
  Pallas kernels  11.6 us (13%)
  local copies, waits for them, and re-layouts  1.77 us (2%)
    all_to_all x2, blocking collectives, exchange(): return lax.all_to_all(block, 'tl', 0, 0)  35.9 us
    ppermute x4, starting transfers between devices, swap(): return lax.ppermute(block, axis, route)  14.3 us
    pallas_call x5, Pallas kernels, run(): pl.pallas_call(kernel, out_shape=[jax.ShapeDtypeStruct(s, jnp.float32) fo...  11.6 us
    ppermute x1, waiting for transfers between devices, hand_over(): return lax.ppermute(block, ('th', 'tl'), route)  11 us
    ppermute x4, waiting for transfers between devices, swap(): return lax.ppermute(block, axis, route)  9.71 us
  transfers between devices with their start and end apart: 5, of which 3 were waited for; matrix products, arithmetic and copies ran while one was open for 0% of the time, Pallas kernels for 0%

profile of v8, /device:TPU:638, one launch (start us, length us, event | category | flops | bytes accessed | tf_op | source)
XLA Modules:
  0.0 85.9 jit_solution(17403600561089744601)
XLA Ops:
  0.0 0.0 copy-start.1
  0.0 0.9 %constant_dynamic-slice_fusion = (f32[1,2,4,16,128]{4,3,2,1,0:T(8,128)S(1)}, f32[1,2,4,16,128]{4,3,2,1,0:T(8,128)S(1)}) fusion(f32[1,2,4,64,128]{4,3,2,1,0:T(8,128)} %param.8, s32[]{:T(128)S(6)} %select_n.17, s32[]{:T(128)S(6)} %select_n.16), kind=kLoop, calls=%fused_computation.4 | loop fusion | bytes 262152 | tf_op jit(solution)/shard_map/dynamic_slice | solution.py:462
  0.9 0.1 copy-done.1
  1.0 0.0 copy-start
  1.1 3.6 %collective-permute-start = (f32[2,2,4,16,128]{4,3,2,1,0:T(8,128)S(1)}, f32[2,2,4,16,128]{4,3,2,1,0:T(8,128)S(1)}, u32[]{:S(2)}, u32[]{:S(2)}) collective-permute-start(f32[2,2,4,16,128]{4,3,2,1,0:T(8,128)S(1)} %pad_maximum_fusion), channel_id=1, source_target_pairs={{8,16},{16,8},{24,32},{32,24},{40,48},{48,40},{56,64},{64,56},{72,... | collective-permute-start | bytes 393224 | tf_op jit(solution)/shard_map/ppermute | solution.py:458
  4.7 2.8 %collective-permute-start.1 = (f32[2,2,4,16,128]{4,3,2,1,0:T(8,128)S(1)}, f32[2,2,4,16,128]{4,3,2,1,0:T(8,128)S(1)}, u32[]{:S(2)}, u32[]{:S(2)}) collective-permute-start(f32[2,2,4,16,128]{4,3,2,1,0:T(8,128)S(1)} %pad_maximum_fusion.1), channel_id=1, source_target_pairs={{0,8},{8,0},{16,24},{24,16},{32,40},{40,32},{48,56},{56,48},{64,72... | collective-permute-start | bytes 393224 | tf_op jit(solution)/shard_map/ppermute | solution.py:458
  7.5 0.1 pad_add_fusion.me
  7.6 8.8 %collective-permute-done.y_two = f32[2,2,4,16,128]{4,3,2,1,0:T(8,128)S(1)} collective-permute-done((f32[2,2,4,16,128]{4,3,2,1,0:T(8,128)S(1)}, f32[2,2,4,16,128]{4,3,2,1,0:T(8,128)S(1)}, u32[]{:S(2)}, u32[]{:S(2)}) %collective-permute-start) | collective-permute-done | bytes 131104 | tf_op jit(solution)/shard_map/ppermute | solution.py:458
  16.4 0.0 collective-permute-done.1.y_one
  16.4 0.0 copy-done
  16.4 1.0 %shard_map.30 = (f32[2,96,128]{2,1,0:T(8,128)S(1)}, f32[2,96,128]{2,1,0:T(8,128)S(1)}) custom-call(s32[3]{0:T(128)S(1)} %pad_add_fusion.me, f32[2,4,64,128]{3,2,1,0:T(8,128)S(1)} %bitcast.10, f32[2,4,64,128]{3,2,1,0:T(8,128)S(1)} %copy-done.1, f32[2,2,4,16,128]{4,3,2,1,0:T(8,128)S(1)} %collective-permute-done.y_two, ...), custom_call_target="tpu_custom_call" | custom-call | tf_op jit(solution)/shard_map/pallas_call | solution.py:440
  17.4 1.9 %collective-permute-start.2 = (f32[2,96,128]{2,1,0:T(8,128)S(1)}, f32[2,96,128]{2,1,0:T(8,128)S(1)}, u32[]{:S(2)}, u32[]{:S(2)}) collective-permute-start(f32[2,96,128]{2,1,0:T(8,128)S(1)} %get-tuple-element.53), channel_id=1, source_target_pairs={{1,2},{2,1},{3,4},{4,3},{5,6},{6,5},{7,0},{0,7},{9,10},{10,9},{11,... | collective-permute-start | bytes 294920 | tf_op jit(solution)/shard_map/ppermute | solution.py:458
  19.3 5.9 %collective-permute-start.3 = (f32[2,96,128]{2,1,0:T(8,128)S(1)}, f32[2,96,128]{2,1,0:T(8,128)S(1)}, u32[]{:S(2)}, u32[]{:S(2)}) collective-permute-start(f32[2,96,128]{2,1,0:T(8,128)S(1)} %get-tuple-element.54), channel_id=1, source_target_pairs={{0,1},{1,0},{2,3},{3,2},{4,5},{5,4},{6,7},{7,6},{8,9},{9,8},{10,11... | collective-permute-start | bytes 294920 | tf_op jit(solution)/shard_map/ppermute | solution.py:458
  25.3 0.0 collective-permute-done.2.z_two
  25.3 0.9 %collective-permute-done.3.z_one = f32[2,96,128]{2,1,0:T(8,128)S(1)} collective-permute-done((f32[2,96,128]{2,1,0:T(8,128)S(1)}, f32[2,96,128]{2,1,0:T(8,128)S(1)}, u32[]{:S(2)}, u32[]{:S(2)}) %collective-permute-start.3) | collective-permute-done | bytes 98336 | tf_op jit(solution)/shard_map/ppermute | solution.py:458
  26.2 4.5 %shard_map.31 = (f32[4,2,2,88,128]{4,3,2,1,0:T(8,128)S(1)}, f32[4,2,2,80,128]{4,3,2,1,0:T(8,128)S(1)}, f32[2,2,88,128]{3,2,1,0:T(8,128)S(1)}) custom-call(s32[3]{0:T(128)S(1)} %pad_add_fusion.me, f32[2,4,64,128]{3,2,1,0:T(8,128)S(1)} %bitcast.11, f32[2,4,64,128]{3,2,1,0:T(8,128)S(1)} %copy-done.1, f32[2,2,4,16,128]{4,3,2,1,0:T(8,128)S(1)} %collective-permute-done.y_two, ...), custom_call_target="tpu_custom_call" | custom-call | tf_op jit(solution)/shard_map/pallas_call | solution.py:440
  30.7 1.3 %shard_map.32 = (f32[4,2,64,128]{3,2,1,0:T(8,128)}, f32[6,80,128]{2,1,0:T(8,128)S(1)}) custom-call(s32[3]{0:T(128)S(1)} %pad_add_fusion.me, f32[4,2,2,88,128]{4,3,2,1,0:T(8,128)S(1)} %get-tuple-element.73.windows, f32[2,2,88,128]{3,2,1,0:T(8,128)S(1)} %get-tuple-element.57.rates), custom_call_target="tpu_custom_call" | custom-call | tf_op jit(solution)/shard_map/pallas_call | solution.py:440
  32.0 1.3 %collective-permute-start.4 = (f32[6,80,128]{2,1,0:T(8,128)S(1)}, f32[6,80,128]{2,1,0:T(8,128)S(1)}, u32[]{:S(2)}, u32[]{:S(2)}) collective-permute-start(f32[6,80,128]{2,1,0:T(8,128)S(1)} %get-tuple-element.60), channel_id=1, source_target_pairs={{0,896},{128,768},{256,640},{384,512},{1,897},{129,769},{257,641},... | collective-permute-start | bytes 737288 | tf_op jit(solution)/shard_map/ppermute | solution.py:505
  33.3 23.5 %conditional.4 = (f32[4,2,64,128]{3,2,1,0:T(8,128)}, f32[4,2,2,80,128]{4,3,2,1,0:T(8,128)S(1)}) conditional(s32[]{:T(128)} %convert_element_type.2, (f32[4,2,2,80,128]{4,3,2,1,0:T(8,128)S(1)}, f32[4,2,64,128]{3,2,1,0:T(8,128)}) %tuple.27, (f32[4,2,64,128]{3,2,1,0:T(8,128)}, f32[4,2,2,80,128]{4,3,2,1,0:T(8,128)S(1)}) %tuple.28), branch_computations={%region_2.3_spmd, %region_3.4_spmd} | conditional | bytes 2621456 | solution.py:523
  33.3 23.5 %all_to_all.17 = f32[4,2,2,80,128]{4,3,2,1,0:T(8,128)S(1)} all-to-all(f32[4,2,2,80,128]{4,3,2,1,0:T(8,128)S(1)} %copy.14), channel_id=1, replica_groups=mesh['th'=2,'tl'=4,'gy'=16,'gz'=8] {'tl'}, dimensions={0} | all-to-all | bytes 1310720 | tf_op jit(solution)/shard_map/cond/branch_0_fun/all_to_all | solution.py:495
  56.8 11.0 %collective-permute-done.4 = f32[6,80,128]{2,1,0:T(8,128)S(1)} collective-permute-done((f32[6,80,128]{2,1,0:T(8,128)S(1)}, f32[6,80,128]{2,1,0:T(8,128)S(1)}, u32[]{:S(2)}, u32[]{:S(2)}) %collective-permute-start.4) | collective-permute-done | bytes 245792 | tf_op jit(solution)/shard_map/ppermute | solution.py:505
  67.9 17.3 %conditional.5 = (f32[1,2,4,64,128]{4,3,2,1,0:T(8,128)S(1)}) conditional(s32[]{:T(128)} %convert_element_type.2, (f32[4,2,2,80,128]{4,3,2,1,0:T(8,128)S(1)}, f32[2,2,88,128]{3,2,1,0:T(8,128)S(1)}, f32[6,80,128]{2,1,0:T(8,128)S(1)}, s32[3]{0:T(128)S(1)}) %tuple.29, (s32[3]{0:T(128)S(1)}, f32[4,2,64,128]{3,2,1,0:T(8,128)}) %tuple.30), branch_computations={%region_4.5_spmd, %region_5.6_spmd} | conditional | bytes 524296 | solution.py:537
  67.9 4.1 %branch_0_fun.2 = f32[4,2,64,128]{3,2,1,0:T(8,128)S(1)} custom-call(f32[4,2,2,80,128]{4,3,2,1,0:T(8,128)S(1)} %get-tuple-element.39.windows, f32[2,2,88,128]{3,2,1,0:T(8,128)S(1)} %get-tuple-element.40.rates, f32[6,80,128]{2,1,0:T(8,128)S(1)} %get-tuple-element.41.received), custom_call_target="tpu_custom_call" | custom-call | tf_op jit(solution)/shard_map/cond/branch_0_fun/pallas_call | solution.py:440
  71.9 12.4 %all_to_all.18.parts = f32[4,2,64,128]{3,2,1,0:T(8,128)S(1)} all-to-all(f32[4,2,64,128]{3,2,1,0:T(8,128)S(1)} %branch_0_fun.2), channel_id=1, replica_groups=mesh['th'=2,'tl'=4,'gy'=16,'gz'=8] {'tl'}, dimensions={0} | all-to-all | bytes 524288 | tf_op jit(solution)/shard_map/cond/branch_0_fun/all_to_all | solution.py:495
  84.3 0.8 branch_0_fun.3
  85.2 0.0 copy-start.2
  85.2 0.7 copy-done.2
  (5 shorter events, 0.1 us)
Async XLA Ops:
  0.0 1.0 %copy-start.1 = (f32[2,4,64,128]{3,2,1,0:T(8,128)S(1)}, f32[2,4,64,128]{3,2,1,0:T(8,128)}, u32[]{:S(2)}) copy-start(f32[2,4,64,128]{3,2,1,0:T(8,128)} %rates.3) | copy-start | bytes 786436
  1.0 15.4 %copy-start = (f32[1,2,4,64,128]{4,3,2,1,0:T(8,128)S(1)}, f32[1,2,4,64,128]{4,3,2,1,0:T(8,128)}, u32[]{:S(2)}) copy-start(f32[1,2,4,64,128]{4,3,2,1,0:T(8,128)} %param.8) | copy-start | bytes 786436
  1.1 15.3 %collective-permute-start = (f32[2,2,4,16,128]{4,3,2,1,0:T(8,128)S(1)}, f32[2,2,4,16,128]{4,3,2,1,0:T(8,128)S(1)}, u32[]{:S(2)}, u32[]{:S(2)}) collective-permute-start(f32[2,2,4,16,128]{4,3,2,1,0:T(8,128)S(1)} %pad_maximum_fusion), channel_id=1, source_target_pairs={{8,16},{16,8},{24,32},{32,24},{40,48},{48,40},{56,64},{64,56},{72,... | collective-permute-start | bytes 393224 | tf_op jit(solution)/shard_map/ppermute | solution.py:458
  4.7 11.7 %collective-permute-start.1 = (f32[2,2,4,16,128]{4,3,2,1,0:T(8,128)S(1)}, f32[2,2,4,16,128]{4,3,2,1,0:T(8,128)S(1)}, u32[]{:S(2)}, u32[]{:S(2)}) collective-permute-start(f32[2,2,4,16,128]{4,3,2,1,0:T(8,128)S(1)} %pad_maximum_fusion.1), channel_id=1, source_target_pairs={{0,8},{8,0},{16,24},{24,16},{32,40},{40,32},{48,56},{56,48},{64,72... | collective-permute-start | bytes 393224 | tf_op jit(solution)/shard_map/ppermute | solution.py:458
  17.4 7.9 %collective-permute-start.2 = (f32[2,96,128]{2,1,0:T(8,128)S(1)}, f32[2,96,128]{2,1,0:T(8,128)S(1)}, u32[]{:S(2)}, u32[]{:S(2)}) collective-permute-start(f32[2,96,128]{2,1,0:T(8,128)S(1)} %get-tuple-element.53), channel_id=1, source_target_pairs={{1,2},{2,1},{3,4},{4,3},{5,6},{6,5},{7,0},{0,7},{9,10},{10,9},{11,... | collective-permute-start | bytes 294920 | tf_op jit(solution)/shard_map/ppermute | solution.py:458
  19.3 6.9 %collective-permute-start.3 = (f32[2,96,128]{2,1,0:T(8,128)S(1)}, f32[2,96,128]{2,1,0:T(8,128)S(1)}, u32[]{:S(2)}, u32[]{:S(2)}) collective-permute-start(f32[2,96,128]{2,1,0:T(8,128)S(1)} %get-tuple-element.54), channel_id=1, source_target_pairs={{0,1},{1,0},{2,3},{3,2},{4,5},{5,4},{6,7},{7,6},{8,9},{9,8},{10,11... | collective-permute-start | bytes 294920 | tf_op jit(solution)/shard_map/ppermute | solution.py:458
  32.0 35.9 %collective-permute-start.4 = (f32[6,80,128]{2,1,0:T(8,128)S(1)}, f32[6,80,128]{2,1,0:T(8,128)S(1)}, u32[]{:S(2)}, u32[]{:S(2)}) collective-permute-start(f32[6,80,128]{2,1,0:T(8,128)S(1)} %get-tuple-element.60), channel_id=1, source_target_pairs={{0,896},{128,768},{256,640},{384,512},{1,897},{129,769},{257,641},... | collective-permute-start | bytes 737288 | tf_op jit(solution)/shard_map/ppermute | solution.py:505
  85.2 0.7 copy-start.2

commit v9 on v7

--- a/solution.py
+++ b/solution.py
@@ -413,19 +413,12 @@
         second_terms(0, coefs, starts, coarse_ends, terms)
 
 
-def late_second_kernel(me, terms, rates, received, early_ends, ends, coefs, current, rows, window):
-    @pl.when(me[0] < GROUP)
-    def _():
-        for m in range(GROUP):
-            ends[m] = early_ends[m]
-
-    @pl.when(me[0] >= GROUP)
-    def _():
-        save_coefs(coefs, rates, (1,))
-        window[...] = jnp.zeros_like(window)
-        unpack_two(received, window)
-        save_state(current, load_window(window))
-        second_sweep(0, coefs, current, terms, rows, ends)
+def late_second_kernel(terms, rates, received, ends, coefs, current, rows, window):
+    save_coefs(coefs, rates, (1,))
+    window[...] = jnp.zeros_like(window)
+    unpack_two(received, window)
+    save_state(current, load_window(window))
+    second_sweep(0, coefs, current, terms, rows, ends)
 
 
 def merge_kernel(me, parts, out):
@@ -544,9 +537,9 @@
     )(me, starts, coarse_ends, rates_here)
     received_two = hand_over(sent)
 
-    ends, windows = lax.cond(
-        early, lambda e, w: (exchange(e), w), lambda e, w: (e, exchange(w)), ends, late_windows
-    )
+    ends, late_windows = lax.optimization_barrier((ends, late_windows))
+    ends = lax.cond(early, exchange, leave, ends)
+    windows = lax.cond(early, leave, exchange, late_windows)
     coefs, current, flat, window = scratch_of(LATE_WIN)
     starts_shape, slices_shape = (GROUP + 1, *states_of(LATE_WIN)), (GROUP, *states_of(LATE_WIN))
     (terms,) = call(
@@ -555,10 +548,13 @@
         scratch=[coefs, pltpu.VMEM(starts_shape, jnp.float32), pltpu.VMEM(slices_shape, jnp.float32)],
         scalars=1,
     )(me, windows, rates_here, received_one)
-    (ends,) = call(late_second_kernel, [ends_shape], scratch=[coefs, current, flat, window], scalars=1)(
-        me, terms, rates_here, received_two, ends
-    )
-    ends = lax.cond(early, leave, exchange, ends)
+
+    def end_late(parts, terms, received):
+        scratch = [coefs, current, flat, window]
+        (ends,) = call(late_second_kernel, [ends_shape], scratch=scratch)(terms, rates_here, received)
+        return exchange(ends)
+
+    ends = lax.cond(early, lambda parts, terms, received: parts, end_late, ends, terms, received_two)
     (out,) = call(merge_kernel, [(2, 4, ROWS, LANES)], scalars=1)(me, ends)
     return out[None]
 

time: 84 us -> 82.3 us (0.980)
  the two profiles are of different devices: /device:TPU:14 before, /device:TPU:638 now
where the time goes in v9:
time: 82.3 us; the launch traced here: 82 us
  blocking collectives  35.8 us (43%)
  starting transfers between devices  16.9 us (21%)
  waiting for transfers between devices  15.1 us (18%)
  Pallas kernels  12.8 us (16%)
  local copies, waits for them, and re-layouts  1.07 us (1%)
    all_to_all x2, blocking collectives, exchange(): return lax.all_to_all(block, 'tl', 0, 0)  35.8 us
    ppermute x4, starting transfers between devices, swap(): return lax.ppermute(block, axis, route)  14.3 us
    pallas_call x7, Pallas kernels, run(): pl.pallas_call(kernel, out_shape=[jax.ShapeDtypeStruct(s, jnp.float32) fo...  12.8 us
    ppermute x4, waiting for transfers between devices, swap(): return lax.ppermute(block, axis, route)  9.71 us
    ppermute x2, waiting for transfers between devices, hand_over(): return lax.ppermute(block, ('th', 'tl'), route)  5.37 us
    ppermute x2, starting transfers between devices, hand_over(): return lax.ppermute(block, ('th', 'tl'), route)  2.58 us
  transfers between devices with their start and end apart: 6, of which 3 were waited for; matrix products, arithmetic and copies ran while one was open for 0% of the time, Pallas kernels for 5%

profile of v9, /device:TPU:638, one launch (start us, length us, event | category | flops | bytes accessed | tf_op | source)
XLA Modules:
  0.0 82.0 jit_solution(13106189806388262071)
XLA Ops:
  0.0 0.0 copy-start.1
  0.0 0.9 %constant_dynamic-slice_fusion = (f32[1,2,4,16,128]{4,3,2,1,0:T(8,128)S(1)}, f32[1,2,4,16,128]{4,3,2,1,0:T(8,128)S(1)}) fusion(f32[1,2,4,64,128]{4,3,2,1,0:T(8,128)} %param.10, s32[]{:T(128)S(6)} %select_n.17, s32[]{:T(128)S(6)} %select_n.16), kind=kLoop, calls=%fused_computation.4 | loop fusion | bytes 262152 | tf_op jit(solution)/shard_map/dynamic_slice | solution.py:466
  0.9 0.1 copy-done.1
  1.0 0.0 copy-start
  1.1 3.6 %collective-permute-start = (f32[2,2,4,16,128]{4,3,2,1,0:T(8,128)S(1)}, f32[2,2,4,16,128]{4,3,2,1,0:T(8,128)S(1)}, u32[]{:S(2)}, u32[]{:S(2)}) collective-permute-start(f32[2,2,4,16,128]{4,3,2,1,0:T(8,128)S(1)} %pad_maximum_fusion), channel_id=1, source_target_pairs={{8,16},{16,8},{24,32},{32,24},{40,48},{48,40},{56,64},{64,56},{72,... | collective-permute-start | bytes 393224 | tf_op jit(solution)/shard_map/ppermute | solution.py:462
  4.7 2.8 %collective-permute-start.1 = (f32[2,2,4,16,128]{4,3,2,1,0:T(8,128)S(1)}, f32[2,2,4,16,128]{4,3,2,1,0:T(8,128)S(1)}, u32[]{:S(2)}, u32[]{:S(2)}) collective-permute-start(f32[2,2,4,16,128]{4,3,2,1,0:T(8,128)S(1)} %pad_maximum_fusion.1), channel_id=1, source_target_pairs={{0,8},{8,0},{16,24},{24,16},{32,40},{40,32},{48,56},{56,48},{64,72... | collective-permute-start | bytes 393224 | tf_op jit(solution)/shard_map/ppermute | solution.py:462
  7.5 0.1 pad_add_fusion.me
  7.6 8.8 %collective-permute-done.y_two = f32[2,2,4,16,128]{4,3,2,1,0:T(8,128)S(1)} collective-permute-done((f32[2,2,4,16,128]{4,3,2,1,0:T(8,128)S(1)}, f32[2,2,4,16,128]{4,3,2,1,0:T(8,128)S(1)}, u32[]{:S(2)}, u32[]{:S(2)}) %collective-permute-start) | collective-permute-done | bytes 131104 | tf_op jit(solution)/shard_map/ppermute | solution.py:462
  16.4 0.0 collective-permute-done.1.y_one
  16.4 0.0 copy-done
  16.4 1.0 %shard_map.28 = (f32[2,96,128]{2,1,0:T(8,128)S(1)}, f32[2,96,128]{2,1,0:T(8,128)S(1)}) custom-call(s32[3]{0:T(128)S(1)} %pad_add_fusion.me, f32[2,4,64,128]{3,2,1,0:T(8,128)S(1)} %bitcast.9, f32[2,4,64,128]{3,2,1,0:T(8,128)S(1)} %copy-done.1, f32[2,2,4,16,128]{4,3,2,1,0:T(8,128)S(1)} %collective-permute-done.y_two, ...), custom_call_target="tpu_custom_call" | custom-call | tf_op jit(solution)/shard_map/pallas_call | solution.py:444
  17.4 1.9 %collective-permute-start.2 = (f32[2,96,128]{2,1,0:T(8,128)S(1)}, f32[2,96,128]{2,1,0:T(8,128)S(1)}, u32[]{:S(2)}, u32[]{:S(2)}) collective-permute-start(f32[2,96,128]{2,1,0:T(8,128)S(1)} %get-tuple-element.45), channel_id=1, source_target_pairs={{1,2},{2,1},{3,4},{4,3},{5,6},{6,5},{7,0},{0,7},{9,10},{10,9},{11,... | collective-permute-start | bytes 294920 | tf_op jit(solution)/shard_map/ppermute | solution.py:462
  19.3 5.9 %collective-permute-start.3 = (f32[2,96,128]{2,1,0:T(8,128)S(1)}, f32[2,96,128]{2,1,0:T(8,128)S(1)}, u32[]{:S(2)}, u32[]{:S(2)}) collective-permute-start(f32[2,96,128]{2,1,0:T(8,128)S(1)} %get-tuple-element.46), channel_id=1, source_target_pairs={{0,1},{1,0},{2,3},{3,2},{4,5},{5,4},{6,7},{7,6},{8,9},{9,8},{10,11... | collective-permute-start | bytes 294920 | tf_op jit(solution)/shard_map/ppermute | solution.py:462
  25.3 0.0 collective-permute-done.2.z_two
  25.3 0.9 %collective-permute-done.3.z_one = f32[2,96,128]{2,1,0:T(8,128)S(1)} collective-permute-done((f32[2,96,128]{2,1,0:T(8,128)S(1)}, f32[2,96,128]{2,1,0:T(8,128)S(1)}, u32[]{:S(2)}, u32[]{:S(2)}) %collective-permute-start.3) | collective-permute-done | bytes 98336 | tf_op jit(solution)/shard_map/ppermute | solution.py:462
  26.2 4.6 %shard_map.29 = (f32[4,2,2,88,128]{4,3,2,1,0:T(8,128)S(1)}, f32[4,2,2,80,128]{4,3,2,1,0:T(8,128)S(1)}, f32[2,2,88,128]{3,2,1,0:T(8,128)S(1)}) custom-call(s32[3]{0:T(128)S(1)} %pad_add_fusion.me, f32[2,4,64,128]{3,2,1,0:T(8,128)S(1)} %bitcast.10, f32[2,4,64,128]{3,2,1,0:T(8,128)S(1)} %copy-done.1, f32[2,2,4,16,128]{4,3,2,1,0:T(8,128)S(1)} %collective-permute-done.y_two, ...), custom_call_target="tpu_custom_call" | custom-call | tf_op jit(solution)/shard_map/pallas_call | solution.py:444
  30.8 0.6 shard_map.30
  31.3 1.3 %collective-permute-start.4 = (f32[2,2,80,128]{3,2,1,0:T(8,128)S(1)}, f32[2,2,80,128]{3,2,1,0:T(8,128)S(1)}, u32[]{:S(2)}, u32[]{:S(2)}) collective-permute-start(f32[2,2,80,128]{3,2,1,0:T(8,128)S(1)} %get-tuple-element.54), channel_id=1, source_target_pairs={{0,896},{128,768},{256,640},{384,512},{1,897},{129,769},{257,641},... | collective-permute-start | bytes 491528 | tf_op jit(solution)/shard_map/ppermute | solution.py:509
  32.6 0.6 shard_map.31
  33.2 1.3 %collective-permute-start.5 = (f32[3,72,128]{2,1,0:T(8,128)S(1)}, f32[3,72,128]{2,1,0:T(8,128)S(1)}, u32[]{:S(2)}, u32[]{:S(2)}) collective-permute-start(f32[3,72,128]{2,1,0:T(8,128)S(1)} %get-tuple-element.55), channel_id=1, source_target_pairs={{0,896},{128,768},{256,640},{384,512},{1,897},{129,769},{257,641},... | collective-permute-start | bytes 331784 | tf_op jit(solution)/shard_map/ppermute | solution.py:509
  34.5 23.5 %conditional.5 = (f32[4,2,2,80,128]{4,3,2,1,0:T(8,128)S(1)}) conditional(s32[]{:T(128)} %convert_element_type.2, f32[4,2,2,80,128]{4,3,2,1,0:T(8,128)S(1)} %get-tuple-element.53, f32[4,2,2,80,128]{4,3,2,1,0:T(8,128)S(1)} %get-tuple-element.53), branch_computations={%region_2.3_spmd, %region_3.4_spmd} | conditional | bytes 2621448 | solution.py:542
  34.6 23.5 %all_to_all.17 = f32[4,2,2,80,128]{4,3,2,1,0:T(8,128)S(1)} all-to-all(f32[4,2,2,80,128]{4,3,2,1,0:T(8,128)S(1)} %copy.12), channel_id=1, replica_groups=mesh['th'=2,'tl'=4,'gy'=16,'gz'=8] {'tl'}, dimensions={0} | all-to-all | bytes 1310720 | tf_op jit(solution)/shard_map/cond/branch_0_fun/all_to_all | solution.py:499
  58.1 5.4 %collective-permute-done.4.received = f32[2,2,80,128]{3,2,1,0:T(8,128)S(1)} collective-permute-done((f32[2,2,80,128]{3,2,1,0:T(8,128)S(1)}, f32[2,2,80,128]{3,2,1,0:T(8,128)S(1)}, u32[]{:S(2)}, u32[]{:S(2)}) %collective-permute-start.4) | collective-permute-done | bytes 163872 | tf_op jit(solution)/shard_map/ppermute | solution.py:509
  63.4 3.3 %shard_map.32 = f32[4,2,2,10,8,128]{5,4,3,2,1,0:T(8,128)S(1)} custom-call(s32[3]{0:T(128)S(1)} %pad_add_fusion.me, f32[4,2,2,80,128]{4,3,2,1,0:T(8,128)S(1)} %get-tuple-element.62.windows, f32[2,2,88,128]{3,2,1,0:T(8,128)S(1)} %get-tuple-element.48.rates, f32[2,2,80,128]{3,2,1,0:T(8,128)S(1)} %collective-permute-done.4.received), custom_call_target="tpu_custom_call" | custom-call | tf_op jit(solution)/shard_map/pallas_call | solution.py:444
  66.7 0.0 collective-permute-done.5
  66.7 13.7 %conditional.7 = (f32[4,2,64,128]{3,2,1,0:T(8,128)S(1)}) conditional(s32[]{:T(128)} %convert_element_type.2, (f32[4,2,2,10,8,128]{5,4,3,2,1,0:T(8,128)S(1)}, f32[2,2,88,128]{3,2,1,0:T(8,128)S(1)}, f32[3,72,128]{2,1,0:T(8,128)S(1)}) %tuple.31, f32[4,2,64,128]{3,2,1,0:T(8,128)S(1)} %get-tuple-element.63), branch_computations={%region_6.7_spmd, %region_7.8_spmd} | conditional | bytes 524296 | solution.py:557
  66.7 1.4 %branch_0_fun.1 = f32[4,2,64,128]{3,2,1,0:T(8,128)S(1)} custom-call(f32[4,2,2,10,8,128]{5,4,3,2,1,0:T(8,128)S(1)} %get-tuple-element.30.terms, f32[2,2,88,128]{3,2,1,0:T(8,128)S(1)} %get-tuple-element.31.rates, f32[3,72,128]{2,1,0:T(8,128)S(1)} %get-tuple-element.32.received), custom_call_target="tpu_custom_call" | custom-call | tf_op jit(solution)/shard_map/cond/branch_0_fun/pallas_call | solution.py:444
  68.1 12.3 %all_to_all.19 = f32[4,2,64,128]{3,2,1,0:T(8,128)S(1)} all-to-all(f32[4,2,64,128]{3,2,1,0:T(8,128)S(1)} %branch_0_fun.1), channel_id=1, replica_groups=mesh['th'=2,'tl'=4,'gy'=16,'gz'=8] {'tl'}, dimensions={0} | all-to-all | bytes 524288 | tf_op jit(solution)/shard_map/cond/branch_0_fun/all_to_all | solution.py:499
  80.5 1.5 %shard_map.33 = f32[2,4,64,128]{3,2,1,0:T(8,128)} custom-call(s32[3]{0:T(128)S(1)} %pad_add_fusion.me, f32[4,2,64,128]{3,2,1,0:T(8,128)S(1)} %get-tuple-element.64.parts), custom_call_target="tpu_custom_call" | custom-call | tf_op jit(solution)/shard_map/pallas_call | solution.py:444
  (6 shorter events, 0.1 us)
Async XLA Ops:
  0.0 1.0 %copy-start.1 = (f32[2,4,64,128]{3,2,1,0:T(8,128)S(1)}, f32[2,4,64,128]{3,2,1,0:T(8,128)}, u32[]{:S(2)}) copy-start(f32[2,4,64,128]{3,2,1,0:T(8,128)} %rates.3) | copy-start | bytes 786436
  1.0 15.4 %copy-start = (f32[1,2,4,64,128]{4,3,2,1,0:T(8,128)S(1)}, f32[1,2,4,64,128]{4,3,2,1,0:T(8,128)}, u32[]{:S(2)}) copy-start(f32[1,2,4,64,128]{4,3,2,1,0:T(8,128)} %param.10) | copy-start | bytes 786436
  1.1 15.3 %collective-permute-start = (f32[2,2,4,16,128]{4,3,2,1,0:T(8,128)S(1)}, f32[2,2,4,16,128]{4,3,2,1,0:T(8,128)S(1)}, u32[]{:S(2)}, u32[]{:S(2)}) collective-permute-start(f32[2,2,4,16,128]{4,3,2,1,0:T(8,128)S(1)} %pad_maximum_fusion), channel_id=1, source_target_pairs={{8,16},{16,8},{24,32},{32,24},{40,48},{48,40},{56,64},{64,56},{72,... | collective-permute-start | bytes 393224 | tf_op jit(solution)/shard_map/ppermute | solution.py:462
  4.7 11.7 %collective-permute-start.1 = (f32[2,2,4,16,128]{4,3,2,1,0:T(8,128)S(1)}, f32[2,2,4,16,128]{4,3,2,1,0:T(8,128)S(1)}, u32[]{:S(2)}, u32[]{:S(2)}) collective-permute-start(f32[2,2,4,16,128]{4,3,2,1,0:T(8,128)S(1)} %pad_maximum_fusion.1), channel_id=1, source_target_pairs={{0,8},{8,0},{16,24},{24,16},{32,40},{40,32},{48,56},{56,48},{64,72... | collective-permute-start | bytes 393224 | tf_op jit(solution)/shard_map/ppermute | solution.py:462
  17.4 7.9 %collective-permute-start.2 = (f32[2,96,128]{2,1,0:T(8,128)S(1)}, f32[2,96,128]{2,1,0:T(8,128)S(1)}, u32[]{:S(2)}, u32[]{:S(2)}) collective-permute-start(f32[2,96,128]{2,1,0:T(8,128)S(1)} %get-tuple-element.45), channel_id=1, source_target_pairs={{1,2},{2,1},{3,4},{4,3},{5,6},{6,5},{7,0},{0,7},{9,10},{10,9},{11,... | collective-permute-start | bytes 294920 | tf_op jit(solution)/shard_map/ppermute | solution.py:462
  19.3 6.9 %collective-permute-start.3 = (f32[2,96,128]{2,1,0:T(8,128)S(1)}, f32[2,96,128]{2,1,0:T(8,128)S(1)}, u32[]{:S(2)}, u32[]{:S(2)}) collective-permute-start(f32[2,96,128]{2,1,0:T(8,128)S(1)} %get-tuple-element.46), channel_id=1, source_target_pairs={{0,1},{1,0},{2,3},{3,2},{4,5},{5,4},{6,7},{7,6},{8,9},{9,8},{10,11... | collective-permute-start | bytes 294920 | tf_op jit(solution)/shard_map/ppermute | solution.py:462
  31.3 32.1 %collective-permute-start.4 = (f32[2,2,80,128]{3,2,1,0:T(8,128)S(1)}, f32[2,2,80,128]{3,2,1,0:T(8,128)S(1)}, u32[]{:S(2)}, u32[]{:S(2)}) collective-permute-start(f32[2,2,80,128]{3,2,1,0:T(8,128)S(1)} %get-tuple-element.54), channel_id=1, source_target_pairs={{0,896},{128,768},{256,640},{384,512},{1,897},{129,769},{257,641},... | collective-permute-start | bytes 491528 | tf_op jit(solution)/shard_map/ppermute | solution.py:509
  33.2 33.5 %collective-permute-start.5 = (f32[3,72,128]{2,1,0:T(8,128)S(1)}, f32[3,72,128]{2,1,0:T(8,128)S(1)}, u32[]{:S(2)}, u32[]{:S(2)}) collective-permute-start(f32[3,72,128]{2,1,0:T(8,128)S(1)} %get-tuple-element.55), channel_id=1, source_target_pairs={{0,896},{128,768},{256,640},{384,512},{1,897},{129,769},{257,641},... | collective-permute-start | bytes 331784 | tf_op jit(solution)/shard_map/ppermute | solution.py:509

commit v10 on v9

--- a/solution.py
+++ b/solution.py
@@ -14,6 +14,8 @@
 WIN = ROWS + 2 * 12
 LATE_WIN = ROWS + 2 * 8
 SENT_TWO = ROWS + 2 * 4
+COLUMNS_ONE = SUB + 2 * 7
+COLUMNS_TWO = SUB + 2 * 4
 LANES = 128
 EXT = ROWS + 2 * HALO
 TILES = EXT // 8
@@ -347,33 +349,47 @@
     lax.fori_loop(first, GROUP, turn, 0)
 
 
-def pack_two(sent, window):
+def between(lane, begin, end):
+    return (lane >= begin) & (lane < end)
+
+
+def strip_start(b, k, width):
+    start = width * b - LANES * k
+    return start if -width < start < LANES else None
+
+
+def pack_columns(sent, window, width):
     lane = lane_index()
-    begin = (window.shape[2] - SENT_TWO) // 2
-    for r in range(0, SENT_TWO, 8):
-        for k in range(3):
+    begin = (window.shape[2] - sent.shape[1]) // 2
+    for r in range(0, sent.shape[1], 8):
+        for k in range(sent.shape[0]):
             block = jnp.zeros((8, LANES), jnp.float32)
-            for i in range(3):
-                b = 3 * k + i
-                if b < 8:
+            for b in range(8):
+                start = strip_start(b, k, width)
+                if start is not None:
                     c, p, half = b // 4, b // 2 % 2, b % 2
                     rows = window[c, p, begin + r : begin + r + 8, :]
-                    here = (lane >= 40 * i) & (lane < 40 * i + 40)
-                    block = jnp.where(here, roll(rows, 40 * i - 12 - 64 * half, 1), block)
+                    own = 64 * half + (64 - width) // 2
+                    block = jnp.where(between(lane, start, start + width), roll(rows, start - own, 1), block)
             sent[k, r : r + 8, :] = block
 
 
-def unpack_two(sent, window):
+def unpack_columns(sent, window, width):
     lane = lane_index()
-    begin = (window.shape[2] - SENT_TWO) // 2
-    for r in range(0, SENT_TWO, 8):
+    begin = (window.shape[2] - sent.shape[1]) // 2
+    for r in range(0, sent.shape[1], 8):
         for c in range(2):
             for p in range(2):
                 halves = []
                 for half in range(2):
-                    b = 4 * c + 2 * p + half
-                    rows = sent[b // 3, r : r + 8, :]
-                    halves.append(roll(rows, 12 + 64 * half - 40 * (b % 3), 1))
+                    own = 64 * half + (64 - width) // 2
+                    value = None
+                    for k in range(sent.shape[0]):
+                        start = strip_start(4 * c + 2 * p + half, k, width)
+                        if start is not None:
+                            part = roll(sent[k, r : r + 8, :], own - start, 1)
+                            value = part if value is None else jnp.where(lane < own - start, value, part)
+                    halves.append(value)
                 window[c, p, begin + r : begin + r + 8, :] = jnp.where(lane < 64, halves[0], halves[1])
 
 
@@ -384,10 +400,7 @@
         save_state(starts.at[1], load_window(windows.at[0]))
         sweep(1, windows, coefs, starts, coarse_ends)
         save_window(window, load_state(starts.at[GROUP]))
-        begin = (WIN - LATE_WIN) // 2
-        for c in range(2):
-            for p in range(2):
-                sent[c, p] = window[c, p, begin : begin + LATE_WIN, :]
+        pack_columns(sent, window, COLUMNS_ONE)
 
 
 def early_second_kernel(me, starts, coarse_ends, rates, ends, sent, coefs, terms, current, rows, window):
@@ -401,14 +414,15 @@
         save_state(current, state)
         second_sweep(2, coefs, current, terms, rows, ends)
         save_window(window, load_state(current))
-        pack_two(sent, window)
-
-
-def late_first_kernel(me, windows, rates, received, terms, coefs, starts, coarse_ends):
+        pack_columns(sent, window, COLUMNS_TWO)
+
+
+def late_first_kernel(me, windows, rates, received, terms, coefs, starts, coarse_ends, window):
     @pl.when(me[0] >= GROUP)
     def _():
         save_coefs(coefs, rates, (0, 1))
-        save_state(starts.at[0], load_window(received))
+        unpack_columns(received, window, COLUMNS_ONE)
+        save_state(starts.at[0], load_window(window))
         sweep(0, windows, coefs, starts, coarse_ends)
         second_terms(0, coefs, starts, coarse_ends, terms)
 
@@ -416,7 +430,7 @@
 def late_second_kernel(terms, rates, received, ends, coefs, current, rows, window):
     save_coefs(coefs, rates, (1,))
     window[...] = jnp.zeros_like(window)
-    unpack_two(received, window)
+    unpack_columns(received, window, COLUMNS_TWO)
     save_state(current, load_window(window))
     second_sweep(0, coefs, current, terms, rows, ends)
 
@@ -524,7 +538,7 @@
     windows = lax.cond(early, exchange, leave, early_windows)
     starts, coarse_ends, sent = call(
         early_first_kernel,
-        [starts_shape, slices_shape, (2, 2, LATE_WIN, LANES)],
+        [starts_shape, slices_shape, (3, LATE_WIN, LANES)],
         scratch=[coefs, window],
         scalars=1,
     )(me, windows, rates_here)
@@ -545,7 +559,7 @@
     (terms,) = call(
         late_first_kernel,
         [slices_shape],
-        scratch=[coefs, pltpu.VMEM(starts_shape, jnp.float32), pltpu.VMEM(slices_shape, jnp.float32)],
+        scratch=[coefs, pltpu.VMEM(starts_shape, jnp.float32), pltpu.VMEM(slices_shape, jnp.float32), window],
         scalars=1,
     )(me, windows, rates_here, received_one)
 

time: 82.3 us -> 81.2 us (0.987)
  the two profiles are of different devices: /device:TPU:638 before, /device:TPU:14 now
where the time goes in v10:
time: 81.2 us; the launch traced here: 80.7 us
  blocking collectives  40.4 us (50%)
  starting transfers between devices  20.8 us (26%)
  Pallas kernels  12.3 us (15%)
  waiting for transfers between devices  5.76 us (7%)
  local copies, waits for them, and re-layouts  1.09 us (1%)
    all_to_all x2, blocking collectives, exchange(): return lax.all_to_all(block, 'tl', 0, 0)  40.4 us
    ppermute x4, starting transfers between devices, swap(): return lax.ppermute(block, axis, route)  18.2 us
    pallas_call x6, Pallas kernels, run(): pl.pallas_call(kernel, out_shape=[jax.ShapeDtypeStruct(s, jnp.float32) fo...  12.3 us
    ppermute x4, waiting for transfers between devices, swap(): return lax.ppermute(block, axis, route)  5.76 us
    ppermute x2, starting transfers between devices, hand_over(): return lax.ppermute(block, ('th', 'tl'), route)  2.59 us
  transfers between devices with their start and end apart: 6, of which 3 were waited for; matrix products, arithmetic and copies ran while one was open for 0% of the time, Pallas kernels for 5%

profile of v10, /device:TPU:14, one launch (start us, length us, event | category | flops | bytes accessed | tf_op | source)
XLA Modules:
  0.0 80.7 jit_solution(9807519281203285207)
XLA Ops:
  0.0 0.0 copy-start.1
  0.0 0.9 %constant_dynamic-slice_fusion = (f32[1,2,4,16,128]{4,3,2,1,0:T(8,128)S(1)}, f32[1,2,4,16,128]{4,3,2,1,0:T(8,128)S(1)}) fusion(f32[1,2,4,64,128]{4,3,2,1,0:T(8,128)} %param.10, s32[]{:T(128)S(6)} %select_n.17, s32[]{:T(128)S(6)} %select_n.16), kind=kLoop, calls=%fused_computation.4 | loop fusion | bytes 262152 | tf_op jit(solution)/shard_map/dynamic_slice | solution.py:480
  0.9 0.1 copy-done.1
  1.0 0.0 copy-start
  1.1 8.9 %collective-permute-start = (f32[2,2,4,16,128]{4,3,2,1,0:T(8,128)S(1)}, f32[2,2,4,16,128]{4,3,2,1,0:T(8,128)S(1)}, u32[]{:S(2)}, u32[]{:S(2)}) collective-permute-start(f32[2,2,4,16,128]{4,3,2,1,0:T(8,128)S(1)} %pad_maximum_fusion), channel_id=1, source_target_pairs={{8,16},{16,8},{24,32},{32,24},{40,48},{48,40},{56,64},{64,56},{72,... | collective-permute-start | bytes 393224 | tf_op jit(solution)/shard_map/ppermute | solution.py:476
  10.0 1.9 %collective-permute-start.1 = (f32[2,2,4,16,128]{4,3,2,1,0:T(8,128)S(1)}, f32[2,2,4,16,128]{4,3,2,1,0:T(8,128)S(1)}, u32[]{:S(2)}, u32[]{:S(2)}) collective-permute-start(f32[2,2,4,16,128]{4,3,2,1,0:T(8,128)S(1)} %pad_maximum_fusion.1), channel_id=1, source_target_pairs={{0,8},{8,0},{16,24},{24,16},{32,40},{40,32},{48,56},{56,48},{64,72... | collective-permute-start | bytes 393224 | tf_op jit(solution)/shard_map/ppermute | solution.py:476
  11.9 0.1 pad_add_fusion.me
  12.0 3.9 %collective-permute-done.y_two = f32[2,2,4,16,128]{4,3,2,1,0:T(8,128)S(1)} collective-permute-done((f32[2,2,4,16,128]{4,3,2,1,0:T(8,128)S(1)}, f32[2,2,4,16,128]{4,3,2,1,0:T(8,128)S(1)}, u32[]{:S(2)}, u32[]{:S(2)}) %collective-permute-start) | collective-permute-done | bytes 131104 | tf_op jit(solution)/shard_map/ppermute | solution.py:476
  15.9 0.9 %collective-permute-done.1.y_one = f32[2,2,4,16,128]{4,3,2,1,0:T(8,128)S(1)} collective-permute-done((f32[2,2,4,16,128]{4,3,2,1,0:T(8,128)S(1)}, f32[2,2,4,16,128]{4,3,2,1,0:T(8,128)S(1)}, u32[]{:S(2)}, u32[]{:S(2)}) %collective-permute-start.1) | collective-permute-done | bytes 131104 | tf_op jit(solution)/shard_map/ppermute | solution.py:476
  16.8 0.0 copy-done
  16.8 1.0 %shard_map.28 = (f32[2,96,128]{2,1,0:T(8,128)S(1)}, f32[2,96,128]{2,1,0:T(8,128)S(1)}) custom-call(s32[3]{0:T(128)S(1)} %pad_add_fusion.me, f32[2,4,64,128]{3,2,1,0:T(8,128)S(1)} %bitcast.9, f32[2,4,64,128]{3,2,1,0:T(8,128)S(1)} %copy-done.1, f32[2,2,4,16,128]{4,3,2,1,0:T(8,128)S(1)} %collective-permute-done.y_two, ...), custom_call_target="tpu_custom_call" | custom-call | tf_op jit(solution)/shard_map/pallas_call | solution.py:458
  17.8 1.9 %collective-permute-start.2 = (f32[2,96,128]{2,1,0:T(8,128)S(1)}, f32[2,96,128]{2,1,0:T(8,128)S(1)}, u32[]{:S(2)}, u32[]{:S(2)}) collective-permute-start(f32[2,96,128]{2,1,0:T(8,128)S(1)} %get-tuple-element.45), channel_id=1, source_target_pairs={{1,2},{2,1},{3,4},{4,3},{5,6},{6,5},{7,0},{0,7},{9,10},{10,9},{11,... | collective-permute-start | bytes 294920 | tf_op jit(solution)/shard_map/ppermute | solution.py:476
  19.7 5.4 %collective-permute-start.3 = (f32[2,96,128]{2,1,0:T(8,128)S(1)}, f32[2,96,128]{2,1,0:T(8,128)S(1)}, u32[]{:S(2)}, u32[]{:S(2)}) collective-permute-start(f32[2,96,128]{2,1,0:T(8,128)S(1)} %get-tuple-element.46), channel_id=1, source_target_pairs={{0,1},{1,0},{2,3},{3,2},{4,5},{5,4},{6,7},{7,6},{8,9},{9,8},{10,11... | collective-permute-start | bytes 294920 | tf_op jit(solution)/shard_map/ppermute | solution.py:476
  25.2 0.0 collective-permute-done.2.z_two
  25.2 0.9 %collective-permute-done.3.z_one = f32[2,96,128]{2,1,0:T(8,128)S(1)} collective-permute-done((f32[2,96,128]{2,1,0:T(8,128)S(1)}, f32[2,96,128]{2,1,0:T(8,128)S(1)}, u32[]{:S(2)}, u32[]{:S(2)}) %collective-permute-start.3) | collective-permute-done | bytes 98336 | tf_op jit(solution)/shard_map/ppermute | solution.py:476
  26.1 4.6 %shard_map.29 = (f32[4,2,2,88,128]{4,3,2,1,0:T(8,128)S(1)}, f32[4,2,2,80,128]{4,3,2,1,0:T(8,128)S(1)}, f32[2,2,88,128]{3,2,1,0:T(8,128)S(1)}) custom-call(s32[3]{0:T(128)S(1)} %pad_add_fusion.me, f32[2,4,64,128]{3,2,1,0:T(8,128)S(1)} %bitcast.10, f32[2,4,64,128]{3,2,1,0:T(8,128)S(1)} %copy-done.1, f32[2,2,4,16,128]{4,3,2,1,0:T(8,128)S(1)} %collective-permute-done.y_two, ...), custom_call_target="tpu_custom_call" | custom-call | tf_op jit(solution)/shard_map/pallas_call | solution.py:458
  30.7 29.2 %conditional.4 = (f32[4,2,2,88,128]{4,3,2,1,0:T(8,128)S(1)}) conditional(s32[]{:T(128)} %convert_element_type.2, f32[4,2,2,88,128]{4,3,2,1,0:T(8,128)S(1)} %get-tuple-element.47, f32[4,2,2,88,128]{4,3,2,1,0:T(8,128)S(1)} %get-tuple-element.47), branch_computations={%region_0.1_spmd, %region_1.2_spmd} | conditional | bytes 2883592 | solution.py:538
  30.8 29.1 %all_to_all.16 = f32[4,2,2,88,128]{4,3,2,1,0:T(8,128)S(1)} all-to-all(f32[4,2,2,88,128]{4,3,2,1,0:T(8,128)S(1)} %copy.11), channel_id=1, replica_groups=mesh['th'=2,'tl'=4,'gy'=16,'gz'=8] {'tl'}, dimensions={0} | all-to-all | bytes 1441792 | tf_op jit(solution)/shard_map/cond/branch_1_fun/all_to_all | solution.py:513
  59.9 1.4 %shard_map.30 = (f32[5,2,2,11,8,128]{5,4,3,2,1,0:T(8,128)S(1)}, f32[4,2,2,11,8,128]{5,4,3,2,1,0:T(8,128)S(1)}, f32[3,80,128]{2,1,0:T(8,128)S(1)}) custom-call(s32[3]{0:T(128)S(1)} %pad_add_fusion.me, f32[4,2,2,88,128]{4,3,2,1,0:T(8,128)S(1)} %get-tuple-element.61.windows, f32[2,2,88,128]{3,2,1,0:T(8,128)S(1)} %get-tuple-element.48.rates), custom_call_target="tpu_custom_call" | custom-call | tf_op jit(solution)/shard_map/pallas_call | solution.py:458
  61.3 1.3 %collective-permute-start.4 = (f32[3,80,128]{2,1,0:T(8,128)S(1)}, f32[3,80,128]{2,1,0:T(8,128)S(1)}, u32[]{:S(2)}, u32[]{:S(2)}) collective-permute-start(f32[3,80,128]{2,1,0:T(8,128)S(1)} %get-tuple-element.54), channel_id=1, source_target_pairs={{0,896},{128,768},{256,640},{384,512},{1,897},{129,769},{257,641},... | collective-permute-start | bytes 368648 | tf_op jit(solution)/shard_map/ppermute | solution.py:523
  62.6 3.3 %shard_map.31 = (f32[4,2,64,128]{3,2,1,0:T(8,128)S(1)}, f32[3,72,128]{2,1,0:T(8,128)S(1)}) custom-call(s32[3]{0:T(128)S(1)} %pad_add_fusion.me, f32[5,2,2,11,8,128]{5,4,3,2,1,0:T(8,128)S(1)} %get-tuple-element.49.starts, f32[4,2,2,11,8,128]{5,4,3,2,1,0:T(8,128)S(1)} %get-tuple-element.50.coarse_ends, f32[2,2,88,128]{3,2,1,0:T(8,128)S(1)} %get-tuple-element.48.rates), custom_call_target="tpu_custom_call" | custom-call | tf_op jit(solution)/shard_map/pallas_call | solution.py:458
  65.9 1.3 %collective-permute-start.5 = (f32[3,72,128]{2,1,0:T(8,128)S(1)}, f32[3,72,128]{2,1,0:T(8,128)S(1)}, u32[]{:S(2)}, u32[]{:S(2)}) collective-permute-start(f32[3,72,128]{2,1,0:T(8,128)S(1)} %get-tuple-element.55), channel_id=1, source_target_pairs={{0,896},{128,768},{256,640},{384,512},{1,897},{129,769},{257,641},... | collective-permute-start | bytes 331784 | tf_op jit(solution)/shard_map/ppermute | solution.py:523
  67.2 11.4 %conditional.6 = (f32[4,2,64,128]{3,2,1,0:T(8,128)S(1)}) conditional(s32[]{:T(128)} %convert_element_type.2, f32[4,2,64,128]{3,2,1,0:T(8,128)S(1)} %get-tuple-element.56, f32[4,2,64,128]{3,2,1,0:T(8,128)S(1)} %get-tuple-element.56), branch_computations={%region_4.5_spmd, %region_5.6_spmd} | conditional | bytes 1048584 | solution.py:555
  67.3 11.3 %all_to_all.18 = f32[4,2,64,128]{3,2,1,0:T(8,128)S(1)} all-to-all(f32[4,2,64,128]{3,2,1,0:T(8,128)S(1)} %copy.13), channel_id=1, replica_groups=mesh['th'=2,'tl'=4,'gy'=16,'gz'=8] {'tl'}, dimensions={0} | all-to-all | bytes 524288 | tf_op jit(solution)/shard_map/cond/branch_1_fun/all_to_all | solution.py:513
  78.6 0.0 collective-permute-done.4.received
  78.6 0.5 shard_map.32
  79.2 0.0 collective-permute-done.5
  79.2 1.5 %shard_map.33 = f32[2,4,64,128]{3,2,1,0:T(8,128)} custom-call(s32[3]{0:T(128)S(1)} %pad_add_fusion.me, f32[4,2,64,128]{3,2,1,0:T(8,128)S(1)} %get-tuple-element.64.parts), custom_call_target="tpu_custom_call" | custom-call | tf_op jit(solution)/shard_map/pallas_call | solution.py:458
  (7 shorter events, 0.1 us)
Async XLA Ops:
  0.0 1.0 %copy-start.1 = (f32[2,4,64,128]{3,2,1,0:T(8,128)S(1)}, f32[2,4,64,128]{3,2,1,0:T(8,128)}, u32[]{:S(2)}) copy-start(f32[2,4,64,128]{3,2,1,0:T(8,128)} %rates.3) | copy-start | bytes 786436
  1.0 15.8 %copy-start = (f32[1,2,4,64,128]{4,3,2,1,0:T(8,128)S(1)}, f32[1,2,4,64,128]{4,3,2,1,0:T(8,128)}, u32[]{:S(2)}) copy-start(f32[1,2,4,64,128]{4,3,2,1,0:T(8,128)} %param.10) | copy-start | bytes 786436
  1.1 14.8 %collective-permute-start = (f32[2,2,4,16,128]{4,3,2,1,0:T(8,128)S(1)}, f32[2,2,4,16,128]{4,3,2,1,0:T(8,128)S(1)}, u32[]{:S(2)}, u32[]{:S(2)}) collective-permute-start(f32[2,2,4,16,128]{4,3,2,1,0:T(8,128)S(1)} %pad_maximum_fusion), channel_id=1, source_target_pairs={{8,16},{16,8},{24,32},{32,24},{40,48},{48,40},{56,64},{64,56},{72,... | collective-permute-start | bytes 393224 | tf_op jit(solution)/shard_map/ppermute | solution.py:476
  10.0 6.9 %collective-permute-start.1 = (f32[2,2,4,16,128]{4,3,2,1,0:T(8,128)S(1)}, f32[2,2,4,16,128]{4,3,2,1,0:T(8,128)S(1)}, u32[]{:S(2)}, u32[]{:S(2)}) collective-permute-start(f32[2,2,4,16,128]{4,3,2,1,0:T(8,128)S(1)} %pad_maximum_fusion.1), channel_id=1, source_target_pairs={{0,8},{8,0},{16,24},{24,16},{32,40},{40,32},{48,56},{56,48},{64,72... | collective-permute-start | bytes 393224 | tf_op jit(solution)/shard_map/ppermute | solution.py:476
  17.8 7.4 %collective-permute-start.2 = (f32[2,96,128]{2,1,0:T(8,128)S(1)}, f32[2,96,128]{2,1,0:T(8,128)S(1)}, u32[]{:S(2)}, u32[]{:S(2)}) collective-permute-start(f32[2,96,128]{2,1,0:T(8,128)S(1)} %get-tuple-element.45), channel_id=1, source_target_pairs={{1,2},{2,1},{3,4},{4,3},{5,6},{6,5},{7,0},{0,7},{9,10},{10,9},{11,... | collective-permute-start | bytes 294920 | tf_op jit(solution)/shard_map/ppermute | solution.py:476
  19.7 6.4 %collective-permute-start.3 = (f32[2,96,128]{2,1,0:T(8,128)S(1)}, f32[2,96,128]{2,1,0:T(8,128)S(1)}, u32[]{:S(2)}, u32[]{:S(2)}) collective-permute-start(f32[2,96,128]{2,1,0:T(8,128)S(1)} %get-tuple-element.46), channel_id=1, source_target_pairs={{0,1},{1,0},{2,3},{3,2},{4,5},{5,4},{6,7},{7,6},{8,9},{9,8},{10,11... | collective-permute-start | bytes 294920 | tf_op jit(solution)/shard_map/ppermute | solution.py:476
  61.3 17.3 %collective-permute-start.4 = (f32[3,80,128]{2,1,0:T(8,128)S(1)}, f32[3,80,128]{2,1,0:T(8,128)S(1)}, u32[]{:S(2)}, u32[]{:S(2)}) collective-permute-start(f32[3,80,128]{2,1,0:T(8,128)S(1)} %get-tuple-element.54), channel_id=1, source_target_pairs={{0,896},{128,768},{256,640},{384,512},{1,897},{129,769},{257,641},... | collective-permute-start | bytes 368648 | tf_op jit(solution)/shard_map/ppermute | solution.py:523
  65.9 13.3 %collective-permute-start.5 = (f32[3,72,128]{2,1,0:T(8,128)S(1)}, f32[3,72,128]{2,1,0:T(8,128)S(1)}, u32[]{:S(2)}, u32[]{:S(2)}) collective-permute-start(f32[3,72,128]{2,1,0:T(8,128)S(1)} %get-tuple-element.55), channel_id=1, source_target_pairs={{0,896},{128,768},{256,640},{384,512},{1,897},{129,769},{257,641},... | collective-permute-start | bytes 331784 | tf_op jit(solution)/shard_map/ppermute | solution.py:523

commit v11 on v10

--- a/solution.py
+++ b/solution.py
@@ -121,8 +121,8 @@
     rates,
     y_two,
     y_one,
+    z_one,
     z_two,
-    z_one,
     early_windows,
     late_windows,
     rates_here,
@@ -507,7 +507,7 @@
             tile_state,
         ],
         scalars=1,
-    )(me, state, rates, y_two, y_one, z_two, z_one)
+    )(me, state, rates, y_two, y_one, z_one, z_two)
 
     def exchange(block):
         return lax.all_to_all(block, "tl", 0, 0)

time: 81.2 us -> 81.7 us (level)
  starting transfers between devices: 20.8 us -> 17.9 us
  waiting for transfers between devices: 5.76 us -> 8.22 us
  blocking collectives: 40.4 us -> 41.4 us
    ppermute x4, starting transfers between devices: 18.2 us -> 15.3 us  [swap(): return lax.ppermute(block, axis, route)]
    ppermute x4, waiting for transfers between devices: 5.76 us -> 8.22 us  [swap(): return lax.ppermute(block, axis, route)]
    all_to_all x2, blocking collectives: 40.4 us -> 41.4 us  [exchange(): return lax.all_to_all(block, 'tl', 0, 0)]
where the time goes in v11:
time: 81.7 us; the launch traced here: 81.3 us
  blocking collectives  41.4 us (51%)
  starting transfers between devices  17.9 us (22%)
  Pallas kernels  12.3 us (15%)
  waiting for transfers between devices  8.22 us (10%)
  local copies, waits for them, and re-layouts  1.09 us (1%)
    all_to_all x2, blocking collectives, exchange(): return lax.all_to_all(block, 'tl', 0, 0)  41.4 us
    ppermute x4, starting transfers between devices, swap(): return lax.ppermute(block, axis, route)  15.3 us
    pallas_call x6, Pallas kernels, run(): pl.pallas_call(kernel, out_shape=[jax.ShapeDtypeStruct(s, jnp.float32) fo...  12.3 us
    ppermute x4, waiting for transfers between devices, swap(): return lax.ppermute(block, axis, route)  8.22 us
    ppermute x2, starting transfers between devices, hand_over(): return lax.ppermute(block, ('th', 'tl'), route)  2.59 us
  transfers between devices with their start and end apart: 6, of which 3 were waited for; matrix products, arithmetic and copies ran while one was open for 0% of the time, Pallas kernels for 5%

profile of v11, /device:TPU:14, one launch (start us, length us, event | category | flops | bytes accessed | tf_op | source)
XLA Modules:
  0.0 81.3 jit_solution(6777810064830887611)
XLA Ops:
  0.0 0.0 copy-start.1
  0.0 0.9 %constant_dynamic-slice_fusion = (f32[1,2,4,16,128]{4,3,2,1,0:T(8,128)S(1)}, f32[1,2,4,16,128]{4,3,2,1,0:T(8,128)S(1)}) fusion(f32[1,2,4,64,128]{4,3,2,1,0:T(8,128)} %param.10, s32[]{:T(128)S(6)} %select_n.17, s32[]{:T(128)S(6)} %select_n.16), kind=kLoop, calls=%fused_computation.4 | loop fusion | bytes 262152 | tf_op jit(solution)/shard_map/dynamic_slice | solution.py:480
  0.9 0.1 copy-done.1
  1.0 0.0 copy-start
  1.1 8.9 %collective-permute-start = (f32[2,2,4,16,128]{4,3,2,1,0:T(8,128)S(1)}, f32[2,2,4,16,128]{4,3,2,1,0:T(8,128)S(1)}, u32[]{:S(2)}, u32[]{:S(2)}) collective-permute-start(f32[2,2,4,16,128]{4,3,2,1,0:T(8,128)S(1)} %pad_maximum_fusion), channel_id=1, source_target_pairs={{8,16},{16,8},{24,32},{32,24},{40,48},{48,40},{56,64},{64,56},{72,... | collective-permute-start | bytes 393224 | tf_op jit(solution)/shard_map/ppermute | solution.py:476
  10.0 1.9 %collective-permute-start.1 = (f32[2,2,4,16,128]{4,3,2,1,0:T(8,128)S(1)}, f32[2,2,4,16,128]{4,3,2,1,0:T(8,128)S(1)}, u32[]{:S(2)}, u32[]{:S(2)}) collective-permute-start(f32[2,2,4,16,128]{4,3,2,1,0:T(8,128)S(1)} %pad_maximum_fusion.1), channel_id=1, source_target_pairs={{0,8},{8,0},{16,24},{24,16},{32,40},{40,32},{48,56},{56,48},{64,72... | collective-permute-start | bytes 393224 | tf_op jit(solution)/shard_map/ppermute | solution.py:476
  11.9 0.1 pad_add_fusion.me
  12.0 3.9 %collective-permute-done.y_two = f32[2,2,4,16,128]{4,3,2,1,0:T(8,128)S(1)} collective-permute-done((f32[2,2,4,16,128]{4,3,2,1,0:T(8,128)S(1)}, f32[2,2,4,16,128]{4,3,2,1,0:T(8,128)S(1)}, u32[]{:S(2)}, u32[]{:S(2)}) %collective-permute-start) | collective-permute-done | bytes 131104 | tf_op jit(solution)/shard_map/ppermute | solution.py:476
  15.9 0.9 %collective-permute-done.1.y_one = f32[2,2,4,16,128]{4,3,2,1,0:T(8,128)S(1)} collective-permute-done((f32[2,2,4,16,128]{4,3,2,1,0:T(8,128)S(1)}, f32[2,2,4,16,128]{4,3,2,1,0:T(8,128)S(1)}, u32[]{:S(2)}, u32[]{:S(2)}) %collective-permute-start.1) | collective-permute-done | bytes 131104 | tf_op jit(solution)/shard_map/ppermute | solution.py:476
  16.8 0.0 copy-done
  16.8 1.0 %shard_map.28 = (f32[2,96,128]{2,1,0:T(8,128)S(1)}, f32[2,96,128]{2,1,0:T(8,128)S(1)}) custom-call(s32[3]{0:T(128)S(1)} %pad_add_fusion.me, f32[2,4,64,128]{3,2,1,0:T(8,128)S(1)} %bitcast.9, f32[2,4,64,128]{3,2,1,0:T(8,128)S(1)} %copy-done.1, f32[2,2,4,16,128]{4,3,2,1,0:T(8,128)S(1)} %collective-permute-done.y_two, ...), custom_call_target="tpu_custom_call" | custom-call | tf_op jit(solution)/shard_map/pallas_call | solution.py:458
  17.8 1.9 %collective-permute-start.2 = (f32[2,96,128]{2,1,0:T(8,128)S(1)}, f32[2,96,128]{2,1,0:T(8,128)S(1)}, u32[]{:S(2)}, u32[]{:S(2)}) collective-permute-start(f32[2,96,128]{2,1,0:T(8,128)S(1)} %get-tuple-element.45), channel_id=1, source_target_pairs={{0,1},{1,0},{2,3},{3,2},{4,5},{5,4},{6,7},{7,6},{8,9},{9,8},{10,11... | collective-permute-start | bytes 294920 | tf_op jit(solution)/shard_map/ppermute | solution.py:476
  19.7 2.5 %collective-permute-start.3 = (f32[2,96,128]{2,1,0:T(8,128)S(1)}, f32[2,96,128]{2,1,0:T(8,128)S(1)}, u32[]{:S(2)}, u32[]{:S(2)}) collective-permute-start(f32[2,96,128]{2,1,0:T(8,128)S(1)} %get-tuple-element.46), channel_id=1, source_target_pairs={{1,2},{2,1},{3,4},{4,3},{5,6},{6,5},{7,0},{0,7},{9,10},{10,9},{11,... | collective-permute-start | bytes 294920 | tf_op jit(solution)/shard_map/ppermute | solution.py:476
  22.3 0.0 collective-permute-done.2.z_one
  22.3 3.4 %collective-permute-done.3.z_two = f32[2,96,128]{2,1,0:T(8,128)S(1)} collective-permute-done((f32[2,96,128]{2,1,0:T(8,128)S(1)}, f32[2,96,128]{2,1,0:T(8,128)S(1)}, u32[]{:S(2)}, u32[]{:S(2)}) %collective-permute-start.3) | collective-permute-done | bytes 98336 | tf_op jit(solution)/shard_map/ppermute | solution.py:476
  25.7 4.6 %shard_map.29 = (f32[4,2,2,88,128]{4,3,2,1,0:T(8,128)S(1)}, f32[4,2,2,80,128]{4,3,2,1,0:T(8,128)S(1)}, f32[2,2,88,128]{3,2,1,0:T(8,128)S(1)}) custom-call(s32[3]{0:T(128)S(1)} %pad_add_fusion.me, f32[2,4,64,128]{3,2,1,0:T(8,128)S(1)} %bitcast.10, f32[2,4,64,128]{3,2,1,0:T(8,128)S(1)} %copy-done.1, f32[2,2,4,16,128]{4,3,2,1,0:T(8,128)S(1)} %collective-permute-done.y_two, ...), custom_call_target="tpu_custom_call" | custom-call | tf_op jit(solution)/shard_map/pallas_call | solution.py:458
  30.3 28.7 %conditional.4 = (f32[4,2,2,88,128]{4,3,2,1,0:T(8,128)S(1)}) conditional(s32[]{:T(128)} %convert_element_type.2, f32[4,2,2,88,128]{4,3,2,1,0:T(8,128)S(1)} %get-tuple-element.47, f32[4,2,2,88,128]{4,3,2,1,0:T(8,128)S(1)} %get-tuple-element.47), branch_computations={%region_0.1_spmd, %region_1.2_spmd} | conditional | bytes 2883592 | solution.py:538
  30.4 28.6 %all_to_all.16 = f32[4,2,2,88,128]{4,3,2,1,0:T(8,128)S(1)} all-to-all(f32[4,2,2,88,128]{4,3,2,1,0:T(8,128)S(1)} %copy.11), channel_id=1, replica_groups=mesh['th'=2,'tl'=4,'gy'=16,'gz'=8] {'tl'}, dimensions={0} | all-to-all | bytes 1441792 | tf_op jit(solution)/shard_map/cond/branch_1_fun/all_to_all | solution.py:513
  59.0 1.4 %shard_map.30 = (f32[5,2,2,11,8,128]{5,4,3,2,1,0:T(8,128)S(1)}, f32[4,2,2,11,8,128]{5,4,3,2,1,0:T(8,128)S(1)}, f32[3,80,128]{2,1,0:T(8,128)S(1)}) custom-call(s32[3]{0:T(128)S(1)} %pad_add_fusion.me, f32[4,2,2,88,128]{4,3,2,1,0:T(8,128)S(1)} %get-tuple-element.61.windows, f32[2,2,88,128]{3,2,1,0:T(8,128)S(1)} %get-tuple-element.48.rates), custom_call_target="tpu_custom_call" | custom-call | tf_op jit(solution)/shard_map/pallas_call | solution.py:458
  60.3 1.3 %collective-permute-start.4 = (f32[3,80,128]{2,1,0:T(8,128)S(1)}, f32[3,80,128]{2,1,0:T(8,128)S(1)}, u32[]{:S(2)}, u32[]{:S(2)}) collective-permute-start(f32[3,80,128]{2,1,0:T(8,128)S(1)} %get-tuple-element.54), channel_id=1, source_target_pairs={{0,896},{128,768},{256,640},{384,512},{1,897},{129,769},{257,641},... | collective-permute-start | bytes 368648 | tf_op jit(solution)/shard_map/ppermute | solution.py:523
  61.6 3.3 %shard_map.31 = (f32[4,2,64,128]{3,2,1,0:T(8,128)S(1)}, f32[3,72,128]{2,1,0:T(8,128)S(1)}) custom-call(s32[3]{0:T(128)S(1)} %pad_add_fusion.me, f32[5,2,2,11,8,128]{5,4,3,2,1,0:T(8,128)S(1)} %get-tuple-element.49.starts, f32[4,2,2,11,8,128]{5,4,3,2,1,0:T(8,128)S(1)} %get-tuple-element.50.coarse_ends, f32[2,2,88,128]{3,2,1,0:T(8,128)S(1)} %get-tuple-element.48.rates), custom_call_target="tpu_custom_call" | custom-call | tf_op jit(solution)/shard_map/pallas_call | solution.py:458
  65.0 1.3 %collective-permute-start.5 = (f32[3,72,128]{2,1,0:T(8,128)S(1)}, f32[3,72,128]{2,1,0:T(8,128)S(1)}, u32[]{:S(2)}, u32[]{:S(2)}) collective-permute-start(f32[3,72,128]{2,1,0:T(8,128)S(1)} %get-tuple-element.55), channel_id=1, source_target_pairs={{0,896},{128,768},{256,640},{384,512},{1,897},{129,769},{257,641},... | collective-permute-start | bytes 331784 | tf_op jit(solution)/shard_map/ppermute | solution.py:523
  66.3 12.9 %conditional.6 = (f32[4,2,64,128]{3,2,1,0:T(8,128)S(1)}) conditional(s32[]{:T(128)} %convert_element_type.2, f32[4,2,64,128]{3,2,1,0:T(8,128)S(1)} %get-tuple-element.56, f32[4,2,64,128]{3,2,1,0:T(8,128)S(1)} %get-tuple-element.56), branch_computations={%region_4.5_spmd, %region_5.6_spmd} | conditional | bytes 1048584 | solution.py:555
  66.3 12.8 %all_to_all.18 = f32[4,2,64,128]{3,2,1,0:T(8,128)S(1)} all-to-all(f32[4,2,64,128]{3,2,1,0:T(8,128)S(1)} %copy.13), channel_id=1, replica_groups=mesh['th'=2,'tl'=4,'gy'=16,'gz'=8] {'tl'}, dimensions={0} | all-to-all | bytes 524288 | tf_op jit(solution)/shard_map/cond/branch_1_fun/all_to_all | solution.py:513
  79.2 0.0 collective-permute-done.4.received
  79.2 0.5 shard_map.32
  79.7 0.0 collective-permute-done.5
  79.8 1.5 %shard_map.33 = f32[2,4,64,128]{3,2,1,0:T(8,128)} custom-call(s32[3]{0:T(128)S(1)} %pad_add_fusion.me, f32[4,2,64,128]{3,2,1,0:T(8,128)S(1)} %get-tuple-element.64.parts), custom_call_target="tpu_custom_call" | custom-call | tf_op jit(solution)/shard_map/pallas_call | solution.py:458
  (7 shorter events, 0.1 us)
Async XLA Ops:
  0.0 1.0 %copy-start.1 = (f32[2,4,64,128]{3,2,1,0:T(8,128)S(1)}, f32[2,4,64,128]{3,2,1,0:T(8,128)}, u32[]{:S(2)}) copy-start(f32[2,4,64,128]{3,2,1,0:T(8,128)} %rates.3) | copy-start | bytes 786436
  1.0 15.8 %copy-start = (f32[1,2,4,64,128]{4,3,2,1,0:T(8,128)S(1)}, f32[1,2,4,64,128]{4,3,2,1,0:T(8,128)}, u32[]{:S(2)}) copy-start(f32[1,2,4,64,128]{4,3,2,1,0:T(8,128)} %param.10) | copy-start | bytes 786436
  1.1 14.8 %collective-permute-start = (f32[2,2,4,16,128]{4,3,2,1,0:T(8,128)S(1)}, f32[2,2,4,16,128]{4,3,2,1,0:T(8,128)S(1)}, u32[]{:S(2)}, u32[]{:S(2)}) collective-permute-start(f32[2,2,4,16,128]{4,3,2,1,0:T(8,128)S(1)} %pad_maximum_fusion), channel_id=1, source_target_pairs={{8,16},{16,8},{24,32},{32,24},{40,48},{48,40},{56,64},{64,56},{72,... | collective-permute-start | bytes 393224 | tf_op jit(solution)/shard_map/ppermute | solution.py:476
  10.0 6.9 %collective-permute-start.1 = (f32[2,2,4,16,128]{4,3,2,1,0:T(8,128)S(1)}, f32[2,2,4,16,128]{4,3,2,1,0:T(8,128)S(1)}, u32[]{:S(2)}, u32[]{:S(2)}) collective-permute-start(f32[2,2,4,16,128]{4,3,2,1,0:T(8,128)S(1)} %pad_maximum_fusion.1), channel_id=1, source_target_pairs={{0,8},{8,0},{16,24},{24,16},{32,40},{40,32},{48,56},{56,48},{64,72... | collective-permute-start | bytes 393224 | tf_op jit(solution)/shard_map/ppermute | solution.py:476
  17.8 4.5 %collective-permute-start.2 = (f32[2,96,128]{2,1,0:T(8,128)S(1)}, f32[2,96,128]{2,1,0:T(8,128)S(1)}, u32[]{:S(2)}, u32[]{:S(2)}) collective-permute-start(f32[2,96,128]{2,1,0:T(8,128)S(1)} %get-tuple-element.45), channel_id=1, source_target_pairs={{0,1},{1,0},{2,3},{3,2},{4,5},{5,4},{6,7},{7,6},{8,9},{9,8},{10,11... | collective-permute-start | bytes 294920 | tf_op jit(solution)/shard_map/ppermute | solution.py:476
  19.7 5.9 %collective-permute-start.3 = (f32[2,96,128]{2,1,0:T(8,128)S(1)}, f32[2,96,128]{2,1,0:T(8,128)S(1)}, u32[]{:S(2)}, u32[]{:S(2)}) collective-permute-start(f32[2,96,128]{2,1,0:T(8,128)S(1)} %get-tuple-element.46), channel_id=1, source_target_pairs={{1,2},{2,1},{3,4},{4,3},{5,6},{6,5},{7,0},{0,7},{9,10},{10,9},{11,... | collective-permute-start | bytes 294920 | tf_op jit(solution)/shard_map/ppermute | solution.py:476
  60.3 18.8 %collective-permute-start.4 = (f32[3,80,128]{2,1,0:T(8,128)S(1)}, f32[3,80,128]{2,1,0:T(8,128)S(1)}, u32[]{:S(2)}, u32[]{:S(2)}) collective-permute-start(f32[3,80,128]{2,1,0:T(8,128)S(1)} %get-tuple-element.54), channel_id=1, source_target_pairs={{0,896},{128,768},{256,640},{384,512},{1,897},{129,769},{257,641},... | collective-permute-start | bytes 368648 | tf_op jit(solution)/shard_map/ppermute | solution.py:523
  65.0 14.8 %collective-permute-start.5 = (f32[3,72,128]{2,1,0:T(8,128)S(1)}, f32[3,72,128]{2,1,0:T(8,128)S(1)}, u32[]{:S(2)}, u32[]{:S(2)}) collective-permute-start(f32[3,72,128]{2,1,0:T(8,128)S(1)} %get-tuple-element.55), channel_id=1, source_target_pairs={{0,896},{128,768},{256,640},{384,512},{1,897},{129,769},{257,641},... | collective-permute-start | bytes 331784 | tf_op jit(solution)/shard_map/ppermute | solution.py:523

commit v12 on v10

--- a/solution.py
+++ b/solution.py
@@ -51,20 +51,40 @@
     return pick(even, one[rows, :], two[rows, :])
 
 
-def strips_kernel(me, state, rates, y_two, y_one, two, one):
+def pack_edges(blocks, lane):
+    first = jnp.zeros((8, LANES), jnp.float32)
+    last = jnp.zeros((8, LANES), jnp.float32)
+    for k, rows in enumerate(blocks):
+        here = (lane >= 16 * k) & (lane < 16 * k + 16)
+        first = jnp.where(here, roll(rows, 16 * k, 1), first)
+        last = jnp.where(here, roll(rows, 16 * k + 16, 1), last)
+    return first, last
+
+
+def own_strips_kernel(me, state, rates, two, one):
+    lane = lane_index()
+    even_z = me[2] % 2 == 0
+    for which, source in enumerate((state, rates)):
+        for at in range(0, ROWS, 8):
+            rows = slice(at, at + 8)
+            first, last = pack_edges([source[k // 4, k % 4, rows, :] for k in range(8)], lane)
+            one[which, rows, :] = pick(even_z, last, first)
+            two[which, rows, :] = pick(even_z, first, last)
+
+
+def strips_kernel(me, own_two, own_one, y_two, y_one, two, one):
     lane = lane_index()
     even_y = me[1] % 2 == 0
     even_z = me[2] % 2 == 0
-    for which, source in enumerate((state, rates)):
-        for tile in range(TILES):
-            first = jnp.zeros((8, LANES), jnp.float32)
-            last = jnp.zeros((8, LANES), jnp.float32)
-            for k in range(8):
-                c, x = k // 4, k % 4
-                rows = ext_tile(y_one.at[which, c, x], y_two.at[which, c, x], source.at[c, x], even_y, tile)
-                here = (lane >= 16 * k) & (lane < 16 * k + 16)
-                first = jnp.where(here, roll(rows, 16 * k, 1), first)
-                last = jnp.where(here, roll(rows, 16 * k + 16, 1), last)
+    one[:, HALO : HALO + ROWS, :] = own_one[...]
+    two[:, HALO : HALO + ROWS, :] = own_two[...]
+    for which in range(2):
+        for tile in (0, 1, TILES - 2, TILES - 1):
+            blocks = [
+                ext_tile(y_one.at[which, k // 4, k % 4], y_two.at[which, k // 4, k % 4], None, even_y, tile)
+                for k in range(8)
+            ]
+            first, last = pack_edges(blocks, lane)
             one[which, 8 * tile : 8 * tile + 8, :] = pick(even_z, last, first)
             two[which, 8 * tile : 8 * tile + 8, :] = pick(even_z, first, last)
 
@@ -491,7 +511,9 @@
     y_two = swap(two, "gy", 1)
     y_one = swap(one, "gy", 0)
     strip = (2, EXT, LANES)
-    two, one = call(strips_kernel, [strip, strip], scalars=1)(me, state, rates, y_two, y_one)
+    own = (2, ROWS, LANES)
+    own_two, own_one = call(own_strips_kernel, [own, own], scalars=1)(me, state, rates)
+    two, one = call(strips_kernel, [strip, strip], scalars=1)(me, own_two, own_one, y_two, y_one)
     z_two = swap(two, "gz", 1)
     z_one = swap(one, "gz", 0)
     tile_state = pltpu.VMEM((2, 4, TILES, 8, LANES), jnp.float32)

time: 81.2 us -> 80.9 us (level)
  waiting for transfers between devices: 5.76 us -> 4.91 us
    ppermute x4, waiting for transfers between devices: 5.76 us -> 4.91 us  [swap(): return lax.ppermute(block, axis, route)]
    pallas_call x6 -> x7, Pallas kernels: 12.3 us -> 12.9 us  [run(): pl.pallas_call(kernel, out_shape=[jax.ShapeDtypeStruct(s, jnp.float32) fo...]
  transfers between devices with their start and end apart: 6 -> 6, of which waited for: 3 -> 3; matrix products, arithmetic and copies ran while one was open for 0% -> 0% of each run, Pallas kernels for 5% -> 6%
where the time goes in v12:
time: 80.9 us; the launch traced here: 80.5 us
  blocking collectives  40.4 us (50%)
  starting transfers between devices  20.8 us (26%)
  Pallas kernels  12.9 us (16%)
  waiting for transfers between devices  4.91 us (6%)
  local copies, waits for them, and re-layouts  1.09 us (1%)
    all_to_all x2, blocking collectives, exchange(): return lax.all_to_all(block, 'tl', 0, 0)  40.4 us
    ppermute x4, starting transfers between devices, swap(): return lax.ppermute(block, axis, route)  18.2 us
    pallas_call x7, Pallas kernels, run(): pl.pallas_call(kernel, out_shape=[jax.ShapeDtypeStruct(s, jnp.float32) fo...  12.9 us
    ppermute x4, waiting for transfers between devices, swap(): return lax.ppermute(block, axis, route)  4.91 us
    ppermute x2, starting transfers between devices, hand_over(): return lax.ppermute(block, ('th', 'tl'), route)  2.59 us
  transfers between devices with their start and end apart: 6, of which 3 were waited for; matrix products, arithmetic and copies ran while one was open for 0% of the time, Pallas kernels for 6%

profile of v12, /device:TPU:14, one launch (start us, length us, event | category | flops | bytes accessed | tf_op | source)
XLA Modules:
  0.0 80.5 jit_solution(2304266958496440889)
XLA Ops:
  0.0 0.0 copy-start.1
  0.0 0.9 %constant_dynamic-slice_fusion = (f32[1,2,4,16,128]{4,3,2,1,0:T(8,128)S(1)}, f32[1,2,4,16,128]{4,3,2,1,0:T(8,128)S(1)}) fusion(f32[1,2,4,64,128]{4,3,2,1,0:T(8,128)} %param.10, s32[]{:T(128)S(6)} %select_n.17, s32[]{:T(128)S(6)} %select_n.16), kind=kLoop, calls=%fused_computation.4 | loop fusion | bytes 262152 | tf_op jit(solution)/shard_map/dynamic_slice | solution.py:500
  0.9 0.1 copy-done.1
  1.0 0.0 copy-start
  1.1 8.9 %collective-permute-start = (f32[2,2,4,16,128]{4,3,2,1,0:T(8,128)S(1)}, f32[2,2,4,16,128]{4,3,2,1,0:T(8,128)S(1)}, u32[]{:S(2)}, u32[]{:S(2)}) collective-permute-start(f32[2,2,4,16,128]{4,3,2,1,0:T(8,128)S(1)} %pad_maximum_fusion), channel_id=1, source_target_pairs={{8,16},{16,8},{24,32},{32,24},{40,48},{48,40},{56,64},{64,56},{72,... | collective-permute-start | bytes 393224 | tf_op jit(solution)/shard_map/ppermute | solution.py:496
  10.0 1.9 %collective-permute-start.1 = (f32[2,2,4,16,128]{4,3,2,1,0:T(8,128)S(1)}, f32[2,2,4,16,128]{4,3,2,1,0:T(8,128)S(1)}, u32[]{:S(2)}, u32[]{:S(2)}) collective-permute-start(f32[2,2,4,16,128]{4,3,2,1,0:T(8,128)S(1)} %pad_maximum_fusion.1), channel_id=1, source_target_pairs={{0,8},{8,0},{16,24},{24,16},{32,40},{40,32},{48,56},{56,48},{64,72... | collective-permute-start | bytes 393224 | tf_op jit(solution)/shard_map/ppermute | solution.py:496
  11.9 0.1 pad_add_fusion.me
  12.0 0.0 copy-done
  12.0 0.8 %shard_map.28 = (f32[2,64,128]{2,1,0:T(8,128)S(1)}, f32[2,64,128]{2,1,0:T(8,128)S(1)}) custom-call(s32[3]{0:T(128)S(1)} %pad_add_fusion.me, f32[2,4,64,128]{3,2,1,0:T(8,128)S(1)} %bitcast.9, f32[2,4,64,128]{3,2,1,0:T(8,128)S(1)} %copy-done.1), custom_call_target="tpu_custom_call" | custom-call | tf_op jit(solution)/shard_map/pallas_call | solution.py:478
  12.8 3.1 %collective-permute-done.y_two = f32[2,2,4,16,128]{4,3,2,1,0:T(8,128)S(1)} collective-permute-done((f32[2,2,4,16,128]{4,3,2,1,0:T(8,128)S(1)}, f32[2,2,4,16,128]{4,3,2,1,0:T(8,128)S(1)}, u32[]{:S(2)}, u32[]{:S(2)}) %collective-permute-start) | collective-permute-done | bytes 131104 | tf_op jit(solution)/shard_map/ppermute | solution.py:496
  15.9 0.9 %collective-permute-done.1.y_one = f32[2,2,4,16,128]{4,3,2,1,0:T(8,128)S(1)} collective-permute-done((f32[2,2,4,16,128]{4,3,2,1,0:T(8,128)S(1)}, f32[2,2,4,16,128]{4,3,2,1,0:T(8,128)S(1)}, u32[]{:S(2)}, u32[]{:S(2)}) %collective-permute-start.1) | collective-permute-done | bytes 131104 | tf_op jit(solution)/shard_map/ppermute | solution.py:496
  16.8 0.7 shard_map.29
  17.6 1.9 %collective-permute-start.2 = (f32[2,96,128]{2,1,0:T(8,128)S(1)}, f32[2,96,128]{2,1,0:T(8,128)S(1)}, u32[]{:S(2)}, u32[]{:S(2)}) collective-permute-start(f32[2,96,128]{2,1,0:T(8,128)S(1)} %get-tuple-element.49), channel_id=1, source_target_pairs={{1,2},{2,1},{3,4},{4,3},{5,6},{6,5},{7,0},{0,7},{9,10},{10,9},{11,... | collective-permute-start | bytes 294920 | tf_op jit(solution)/shard_map/ppermute | solution.py:496
  19.5 5.4 %collective-permute-start.3 = (f32[2,96,128]{2,1,0:T(8,128)S(1)}, f32[2,96,128]{2,1,0:T(8,128)S(1)}, u32[]{:S(2)}, u32[]{:S(2)}) collective-permute-start(f32[2,96,128]{2,1,0:T(8,128)S(1)} %get-tuple-element.50), channel_id=1, source_target_pairs={{0,1},{1,0},{2,3},{3,2},{4,5},{5,4},{6,7},{7,6},{8,9},{9,8},{10,11... | collective-permute-start | bytes 294920 | tf_op jit(solution)/shard_map/ppermute | solution.py:496
  25.0 0.0 collective-permute-done.2.z_two
  25.0 0.9 %collective-permute-done.3.z_one = f32[2,96,128]{2,1,0:T(8,128)S(1)} collective-permute-done((f32[2,96,128]{2,1,0:T(8,128)S(1)}, f32[2,96,128]{2,1,0:T(8,128)S(1)}, u32[]{:S(2)}, u32[]{:S(2)}) %collective-permute-start.3) | collective-permute-done | bytes 98336 | tf_op jit(solution)/shard_map/ppermute | solution.py:496
  25.9 4.6 %shard_map.30 = (f32[4,2,2,88,128]{4,3,2,1,0:T(8,128)S(1)}, f32[4,2,2,80,128]{4,3,2,1,0:T(8,128)S(1)}, f32[2,2,88,128]{3,2,1,0:T(8,128)S(1)}) custom-call(s32[3]{0:T(128)S(1)} %pad_add_fusion.me, f32[2,4,64,128]{3,2,1,0:T(8,128)S(1)} %bitcast.10, f32[2,4,64,128]{3,2,1,0:T(8,128)S(1)} %copy-done.1, f32[2,2,4,16,128]{4,3,2,1,0:T(8,128)S(1)} %collective-permute-done.y_two, ...), custom_call_target="tpu_custom_call" | custom-call | tf_op jit(solution)/shard_map/pallas_call | solution.py:478
  30.5 29.2 %conditional.4 = (f32[4,2,2,88,128]{4,3,2,1,0:T(8,128)S(1)}) conditional(s32[]{:T(128)} %convert_element_type.2, f32[4,2,2,88,128]{4,3,2,1,0:T(8,128)S(1)} %get-tuple-element.51, f32[4,2,2,88,128]{4,3,2,1,0:T(8,128)S(1)} %get-tuple-element.51), branch_computations={%region_0.1_spmd, %region_1.2_spmd} | conditional | bytes 2883592 | solution.py:560
  30.6 29.1 %all_to_all.16 = f32[4,2,2,88,128]{4,3,2,1,0:T(8,128)S(1)} all-to-all(f32[4,2,2,88,128]{4,3,2,1,0:T(8,128)S(1)} %copy.11), channel_id=1, replica_groups=mesh['th'=2,'tl'=4,'gy'=16,'gz'=8] {'tl'}, dimensions={0} | all-to-all | bytes 1441792 | tf_op jit(solution)/shard_map/cond/branch_1_fun/all_to_all | solution.py:535
  59.7 1.4 %shard_map.31 = (f32[5,2,2,11,8,128]{5,4,3,2,1,0:T(8,128)S(1)}, f32[4,2,2,11,8,128]{5,4,3,2,1,0:T(8,128)S(1)}, f32[3,80,128]{2,1,0:T(8,128)S(1)}) custom-call(s32[3]{0:T(128)S(1)} %pad_add_fusion.me, f32[4,2,2,88,128]{4,3,2,1,0:T(8,128)S(1)} %get-tuple-element.65.windows, f32[2,2,88,128]{3,2,1,0:T(8,128)S(1)} %get-tuple-element.52.rates), custom_call_target="tpu_custom_call" | custom-call | tf_op jit(solution)/shard_map/pallas_call | solution.py:478
  61.0 1.3 %collective-permute-start.4 = (f32[3,80,128]{2,1,0:T(8,128)S(1)}, f32[3,80,128]{2,1,0:T(8,128)S(1)}, u32[]{:S(2)}, u32[]{:S(2)}) collective-permute-start(f32[3,80,128]{2,1,0:T(8,128)S(1)} %get-tuple-element.58), channel_id=1, source_target_pairs={{0,896},{128,768},{256,640},{384,512},{1,897},{129,769},{257,641},... | collective-permute-start | bytes 368648 | tf_op jit(solution)/shard_map/ppermute | solution.py:545
  62.3 3.3 %shard_map.32 = (f32[4,2,64,128]{3,2,1,0:T(8,128)S(1)}, f32[3,72,128]{2,1,0:T(8,128)S(1)}) custom-call(s32[3]{0:T(128)S(1)} %pad_add_fusion.me, f32[5,2,2,11,8,128]{5,4,3,2,1,0:T(8,128)S(1)} %get-tuple-element.53.starts, f32[4,2,2,11,8,128]{5,4,3,2,1,0:T(8,128)S(1)} %get-tuple-element.54.coarse_ends, f32[2,2,88,128]{3,2,1,0:T(8,128)S(1)} %get-tuple-element.52.rates), custom_call_target="tpu_custom_call" | custom-call | tf_op jit(solution)/shard_map/pallas_call | solution.py:478
  65.7 1.3 %collective-permute-start.5 = (f32[3,72,128]{2,1,0:T(8,128)S(1)}, f32[3,72,128]{2,1,0:T(8,128)S(1)}, u32[]{:S(2)}, u32[]{:S(2)}) collective-permute-start(f32[3,72,128]{2,1,0:T(8,128)S(1)} %get-tuple-element.59), channel_id=1, source_target_pairs={{0,896},{128,768},{256,640},{384,512},{1,897},{129,769},{257,641},... | collective-permute-start | bytes 331784 | tf_op jit(solution)/shard_map/ppermute | solution.py:545
  67.0 11.4 %conditional.6 = (f32[4,2,64,128]{3,2,1,0:T(8,128)S(1)}) conditional(s32[]{:T(128)} %convert_element_type.2, f32[4,2,64,128]{3,2,1,0:T(8,128)S(1)} %get-tuple-element.60, f32[4,2,64,128]{3,2,1,0:T(8,128)S(1)} %get-tuple-element.60), branch_computations={%region_4.5_spmd, %region_5.6_spmd} | conditional | bytes 1048584 | solution.py:577
  67.0 11.3 %all_to_all.18 = f32[4,2,64,128]{3,2,1,0:T(8,128)S(1)} all-to-all(f32[4,2,64,128]{3,2,1,0:T(8,128)S(1)} %copy.13), channel_id=1, replica_groups=mesh['th'=2,'tl'=4,'gy'=16,'gz'=8] {'tl'}, dimensions={0} | all-to-all | bytes 524288 | tf_op jit(solution)/shard_map/cond/branch_1_fun/all_to_all | solution.py:535
  78.4 0.0 collective-permute-done.4.received
  78.4 0.5 shard_map.33
  78.9 0.0 collective-permute-done.5
  79.0 1.5 %shard_map.34 = f32[2,4,64,128]{3,2,1,0:T(8,128)} custom-call(s32[3]{0:T(128)S(1)} %pad_add_fusion.me, f32[4,2,64,128]{3,2,1,0:T(8,128)S(1)} %get-tuple-element.68.parts), custom_call_target="tpu_custom_call" | custom-call | tf_op jit(solution)/shard_map/pallas_call | solution.py:478
  (7 shorter events, 0.1 us)
Async XLA Ops:
  0.0 1.0 %copy-start.1 = (f32[2,4,64,128]{3,2,1,0:T(8,128)S(1)}, f32[2,4,64,128]{3,2,1,0:T(8,128)}, u32[]{:S(2)}) copy-start(f32[2,4,64,128]{3,2,1,0:T(8,128)} %rates.3) | copy-start | bytes 786436
  1.0 11.0 %copy-start = (f32[1,2,4,64,128]{4,3,2,1,0:T(8,128)S(1)}, f32[1,2,4,64,128]{4,3,2,1,0:T(8,128)}, u32[]{:S(2)}) copy-start(f32[1,2,4,64,128]{4,3,2,1,0:T(8,128)} %param.10) | copy-start | bytes 786436
  1.1 14.8 %collective-permute-start = (f32[2,2,4,16,128]{4,3,2,1,0:T(8,128)S(1)}, f32[2,2,4,16,128]{4,3,2,1,0:T(8,128)S(1)}, u32[]{:S(2)}, u32[]{:S(2)}) collective-permute-start(f32[2,2,4,16,128]{4,3,2,1,0:T(8,128)S(1)} %pad_maximum_fusion), channel_id=1, source_target_pairs={{8,16},{16,8},{24,32},{32,24},{40,48},{48,40},{56,64},{64,56},{72,... | collective-permute-start | bytes 393224 | tf_op jit(solution)/shard_map/ppermute | solution.py:496
  10.0 6.9 %collective-permute-start.1 = (f32[2,2,4,16,128]{4,3,2,1,0:T(8,128)S(1)}, f32[2,2,4,16,128]{4,3,2,1,0:T(8,128)S(1)}, u32[]{:S(2)}, u32[]{:S(2)}) collective-permute-start(f32[2,2,4,16,128]{4,3,2,1,0:T(8,128)S(1)} %pad_maximum_fusion.1), channel_id=1, source_target_pairs={{0,8},{8,0},{16,24},{24,16},{32,40},{40,32},{48,56},{56,48},{64,72... | collective-permute-start | bytes 393224 | tf_op jit(solution)/shard_map/ppermute | solution.py:496
  17.6 7.4 %collective-permute-start.2 = (f32[2,96,128]{2,1,0:T(8,128)S(1)}, f32[2,96,128]{2,1,0:T(8,128)S(1)}, u32[]{:S(2)}, u32[]{:S(2)}) collective-permute-start(f32[2,96,128]{2,1,0:T(8,128)S(1)} %get-tuple-element.49), channel_id=1, source_target_pairs={{1,2},{2,1},{3,4},{4,3},{5,6},{6,5},{7,0},{0,7},{9,10},{10,9},{11,... | collective-permute-start | bytes 294920 | tf_op jit(solution)/shard_map/ppermute | solution.py:496
  19.5 6.4 %collective-permute-start.3 = (f32[2,96,128]{2,1,0:T(8,128)S(1)}, f32[2,96,128]{2,1,0:T(8,128)S(1)}, u32[]{:S(2)}, u32[]{:S(2)}) collective-permute-start(f32[2,96,128]{2,1,0:T(8,128)S(1)} %get-tuple-element.50), channel_id=1, source_target_pairs={{0,1},{1,0},{2,3},{3,2},{4,5},{5,4},{6,7},{7,6},{8,9},{9,8},{10,11... | collective-permute-start | bytes 294920 | tf_op jit(solution)/shard_map/ppermute | solution.py:496
  61.0 17.3 %collective-permute-start.4 = (f32[3,80,128]{2,1,0:T(8,128)S(1)}, f32[3,80,128]{2,1,0:T(8,128)S(1)}, u32[]{:S(2)}, u32[]{:S(2)}) collective-permute-start(f32[3,80,128]{2,1,0:T(8,128)S(1)} %get-tuple-element.58), channel_id=1, source_target_pairs={{0,896},{128,768},{256,640},{384,512},{1,897},{129,769},{257,641},... | collective-permute-start | bytes 368648 | tf_op jit(solution)/shard_map/ppermute | solution.py:545
  65.7 13.3 %collective-permute-start.5 = (f32[3,72,128]{2,1,0:T(8,128)S(1)}, f32[3,72,128]{2,1,0:T(8,128)S(1)}, u32[]{:S(2)}, u32[]{:S(2)}) collective-permute-start(f32[3,72,128]{2,1,0:T(8,128)S(1)} %get-tuple-element.59), channel_id=1, source_target_pairs={{0,896},{128,768},{256,640},{384,512},{1,897},{129,769},{257,641},... | collective-permute-start | bytes 331784 | tf_op jit(solution)/shard_map/ppermute | solution.py:545
